TPU v7x, 256 devices: a whole 4x4x8 slice. The times are simulated.
256 devices in a mesh: tile: 64 (over y, z, core), mem: 4 (over x).
Axes of the slice: x: 4, y: 4, z: 8, core: 2. Of those that a mesh axis runs over, the one named last changes fastest.
Arguments:
- ensemble: float32 [64, 4, 24, 128, 256], P('mem', None, None, 'tile'), may hold values from -6 to 6
- courant: float32 [2, 24, 128, 256], P(None, None, 'tile'), may hold values from -0.5 to 0.5
- diffusion: float32 [4, 24], replicated, may hold values from 0.02 to 0.2
- observation_row: int32 [256], replicated, may hold values from 0 to 127
- observation_column: int32 [256], replicated, may hold values from 0 to 255
- observation_field: int32 [256], replicated, may hold values from 0 to 3
- observation_level: int32 [256], replicated, may hold values from 0 to 23
- obs_value: float32 [256], replicated, may hold values from -6 to 6
- obs_error: float32 [256], replicated, may hold values from 0.2 to 2
- localize: float32 [64, 256], replicated, may hold values from 0 to 1
Outputs:
- analysis: float32 [64, 4, 24, 128, 256], P('mem', None, None, 'tile')
All inputs are finite; a program needn't handle non-finite values.
Results may differ from a plain program's by a relative error of at most 0.00013.
Values sent between devices are 32-bit elements; how exact they have to be, the bound alone decides.
No kernel may reach another device: no remote copies, remote signals or barrier semaphores. Data moves between devices by JAX's collectives and lax.ppermute only.
A program may use at most 128 MiB of HBM per device.

v0:
```python
import jax
import jax.numpy as jnp
from jax import lax
from jax.sharding import PartitionSpec as P

STEPS = 2


def padded(cells, sides, width):
    for axis, dim in sides:
        count = lax.axis_size(axis)
        head = lax.slice_in_dim(cells, 0, width, axis=dim)
        tail = lax.slice_in_dim(cells, cells.shape[dim] - width, cells.shape[dim], axis=dim)
        cells = jnp.concatenate(
            [
                lax.ppermute(tail, axis, [(i, (i + 1) % count) for i in range(count)]),
                cells,
                lax.ppermute(head, axis, [((i + 1) % count, i) for i in range(count)]),
            ],
            axis=dim,
        )
    return cells


def advance(extended, courant, diffusion):
    centre = extended[..., 2:-2, :]
    up_one = extended[..., 3:-1, :]
    down_one = extended[..., 1:-3, :]
    up_two = extended[..., 4:, :]
    down_two = extended[..., :-4, :]
    right_one = jnp.roll(centre, -1, axis=-1)
    left_one = jnp.roll(centre, 1, axis=-1)
    right_two = jnp.roll(centre, -2, axis=-1)
    left_two = jnp.roll(centre, 2, axis=-1)
    slope_rows = (8.0 * (up_one - down_one) - (up_two - down_two)) / 12.0
    slope_cols = (8.0 * (right_one - left_one) - (right_two - left_two)) / 12.0
    spread = up_one + down_one + right_one + left_one - 4.0 * centre
    return (
        centre
        - courant[0] * slope_rows
        - courant[1] * slope_cols
        + diffusion[:, :, None, None] * spread
    )


def assimilate(prior, values, errors, row_weights, tile_weights):
    members = prior.shape[1]
    start = jnp.broadcast_to(
        jnp.eye(members, dtype=jnp.float32), (tile_weights.shape[0], members, members)
    )

    def one_obs(position, state_pair):
        priors, transform = state_pair
        sample = lax.dynamic_index_in_dim(priors, position, 0, keepdims=False)
        centre = jnp.mean(sample)
        anomaly = sample - centre
        variance = jnp.sum(anomaly * anomaly) / (members - 1.0)
        obs_err = lax.dynamic_index_in_dim(errors, position, 0, keepdims=False)
        target = lax.dynamic_index_in_dim(values, position, 0, keepdims=False)
        spread_sum = variance + obs_err
        shrink = 1.0 / (1.0 + jnp.sqrt(obs_err / spread_sum))
        increment = (target - centre - shrink * anomaly) / spread_sum
        scaled = anomaly / (members - 1.0)
        projected = jnp.dot(priors, scaled, precision=lax.Precision.HIGHEST)
        weight_rows = lax.dynamic_index_in_dim(row_weights, position, 1, keepdims=False)
        priors = priors + (weight_rows * projected)[:, None] * increment[None, :]
        pushed = jnp.einsum("tab,b->ta", transform, scaled, precision=lax.Precision.HIGHEST)
        weight_tiles = lax.dynamic_index_in_dim(tile_weights, position, 1, keepdims=False)
        transform = (
            transform + weight_tiles[:, None, None] * pushed[:, :, None] * increment[None, None, :]
        )
        return (priors, transform)

    return lax.fori_loop(0, prior.shape[0], one_obs, (prior, start), unroll=8)[1]


def on_device(
    ensemble,
    courant,
    diffusion,
    observation_row,
    observation_column,
    observation_field,
    observation_level,
    obs_value,
    obs_error,
    localize,
):
    members_here = ensemble.shape[0]
    rows_here = ensemble.shape[3]
    state = ensemble
    for step_count in range(STEPS):
        extended = padded(state, (("tile", 3),), 2)
        state = advance(extended, courant, diffusion)
    tile_pos = lax.axis_index("tile")
    member_start = lax.axis_index("mem") * members_here
    ens_size = members_here * lax.axis_size("mem")
    obs_count = observation_row.shape[0]
    half = obs_count // 2
    local_row = observation_row - tile_pos * rows_here
    owned = (local_row >= 0) & (local_row < rows_here)
    clipped = jnp.clip(local_row, 0, rows_here - 1)
    sampled = state[:, observation_field, observation_level, clipped, observation_column].T
    mine = jnp.where(owned[:, None], sampled, 0.0)
    placed = lax.dynamic_update_slice(
        jnp.zeros((obs_count, ens_size), jnp.float32), mine, (jnp.int32(0), member_start)
    )
    owner = observation_row // rows_here
    tiles = localize.shape[0]
    owner_hot = (owner[:, None] == jnp.arange(tiles, dtype=jnp.int32)[None, :]).astype(jnp.float32)
    row_weights = jnp.dot(owner_hot, localize, precision=lax.Precision.HIGHEST)
    own_weights = lax.dynamic_slice_in_dim(localize, tile_pos, 1, 0)
    prior_first = lax.psum(placed[:half], ("tile", "mem"))
    leading_part = assimilate(
        prior_first,
        obs_value[:half],
        obs_error[:half],
        row_weights[:half, :half],
        own_weights[:, :half],
    )[0]
    member_block = lax.dynamic_slice(
        leading_part, (member_start, jnp.int32(0)), (members_here, ens_size)
    )
    share = jnp.dot(mine[half:], member_block, precision=lax.Precision.HIGHEST)
    second_prior = lax.psum(share, ("tile", "mem"))
    trailing_part = assimilate(
        second_prior,
        obs_value[half:],
        obs_error[half:],
        row_weights[half:, half:],
        own_weights[:, half:],
    )[0]
    joined_result = jnp.dot(leading_part, trailing_part, precision=lax.Precision.HIGHEST)
    flat_state = state.reshape(members_here, -1)
    my_columns = lax.dynamic_slice(
        joined_result, (jnp.int32(0), member_start), (ens_size, members_here)
    )
    result = jnp.dot(
        my_columns.T,
        lax.all_gather(flat_state, "mem", axis=0, tiled=True),
        precision=lax.Precision.HIGHEST,
    )
    return result.reshape(state.shape)


def solution(mesh):
    placed = (
        P("mem", None, None, "tile", None),
        P(None, None, "tile", None),
        P(),
        P(),
        P(),
        P(),
        P(),
        P(),
        P(),
        P(),
    )
    return jax.shard_map(
        on_device,
        mesh=mesh,
        in_specs=placed,
        out_specs=P("mem", None, None, "tile", None),
        check_vma=False,
    )
```

profile of v0, /device:TPU:2, one launch (start us, length us, event | category | flops | bytes accessed | tf_op | source)
XLA Modules:
  0.0 2125.7 jit_solution(3052971806988817165)
XLA Ops:
  6.5 2.2 copy.154
  8.8 7.8 collective-permute-start
  16.7 2.2 fusion.298
  18.9 2.2 fusion.299
  22.2 3.8 fusion.300
  26.0 25.3 %collective-permute-done = f32[16,4,24,2,256]{4,2,3,1,0:T(8,128)S(1)} collective-permute-done((f32[16,4,24,2,256]{4,2,3,1,0:T(8,128)S(1)}, f32[16,4,24,2,256]{4,2,3,1,0:T(8,128)S(1)}, u32[]{:S(2)}, u32[]{:S(2)}) %collective-permute-start) | collective-permute-done | bytes 3145760 | tf_op jit(solution)/shard_map/ppermute | solution.py:18
  51.4 5.2 collective-permute-done.1
  58.4 9.6 fusion.259
  71.0 2.2 fusion.294
  73.1 2.2 fusion.295
  76.5 2.8 fusion.296
  79.4 24.4 %collective-permute-done.2 = f32[16,4,24,2,256]{4,2,3,1,0:T(8,128)} collective-permute-done((f32[16,4,24,2,256]{4,2,3,1,0:T(8,128)S(1)}, f32[16,4,24,2,256]{4,2,3,1,0:T(8,128)}, u32[]{:S(2)}, u32[]{:S(2)}) %collective-permute-start.2) | collective-permute-done | bytes 3145760 | tf_op jit(solution)/shard_map/ppermute | solution.py:18
  103.8 5.3 collective-permute-done.3
  109.1 9.9 fusion.263
  119.0 14.3 copy.165
  133.4 3.4 copy.169
  136.8 3.5 gather_fusion
  141.4 72.0 %psum.14 = f32[128,64]{1,0:T(8,128)S(1)} all-reduce(f32[128,64]{1,0:T(8,128)S(1)} %slice.162), channel_id=1, replica_groups=mesh['tile'=64,'mem'=4] {'tile','mem'}, use_global_device_ids=true, to_apply=%region_0.1 | all-reduce | flops 8192 | bytes 65536 | tf_op jit(solution)/shard_map/psum | solution.py:113
  213.3 955.9 %while.42 = (s32[]{:T(128)}, f32[128,64]{1,0:T(8,128)S(1)}, f32[1,64,64]{2,1,0:T(8,128)S(1)}, f32[128,128]{0,1:T(8,128)}, f32[128]{0:T(128)S(1)}, /*index=5*/f32...) while((s32[]{:T(128)}, f32[128,64]{1,0:T(8,128)S(1)}, ...), condition=%wide.region_18.19_spmd.clone.clone, body=%wide.region_1.18_spmd.clone.clone.clone.sunk | while | flops 1972298 | bytes 1055781 | solution.py:74
  255.5 2.1 fusion.492
  265.0 2.1 fusion.493
  315.2 2.1 fusion.492
  324.8 2.1 fusion.493
  375.0 2.1 fusion.492
  384.6 2.1 fusion.493
  434.7 2.1 fusion.492
  444.3 2.1 fusion.493
  494.5 2.1 fusion.492
  504.1 2.1 fusion.493
  554.3 2.1 fusion.492
  563.9 2.1 fusion.493
  614.0 2.1 fusion.492
  623.6 2.1 fusion.493
  673.7 2.1 fusion.492
  683.3 2.1 fusion.493
  743.1 2.1 fusion.493
  802.9 2.1 fusion.493
  862.6 2.1 fusion.493
  922.3 2.1 fusion.493
  982.0 2.1 fusion.493
  1041.7 2.1 fusion.493
  1101.5 2.1 fusion.493
  1161.3 2.1 fusion.493
  1169.6 74.9 %psum.15 = f32[128,64]{0,1:T(8,128)S(1)} all-reduce(f32[128,64]{0,1:T(8,128)S(1)} %fusion.265), channel_id=1, replica_groups=mesh['tile'=64,'mem'=4] {'tile','mem'}, use_global_device_ids=true, to_apply=%region_19.20 | all-reduce | flops 8192 | bytes 65536 | tf_op jit(solution)/shard_map/psum | solution.py:125
  1244.6 3.7 reshape.1678
  1249.0 857.1 %while.43 = (s32[]{:T(128)}, f32[128,64]{1,0:T(8,128)S(1)}, f32[1,64,64]{2,1,0:T(8,128)S(1)}, f32[128,128]{0,1:T(8,128)}, f32[128]{0:T(128)S(1)}, /*index=5*/f32...) while((s32[]{:T(128)}, f32[128,64]{1,0:T(8,128)S(1)}, ...), condition=%wide.region_37.38_spmd.clone.clone, body=%wide.region_20.37_spmd.clone.clone.clone.sunk | while | flops 1972298 | bytes 1049469 | solution.py:74
  2106.4 8.6 fusion.273
  2115.0 3.9 reshape.1679
  (1891 shorter events, 931.2 us)
Async XLA Ops:
  6.5 2099.9 %all-gather.2.cloned.1.call-start = ((), (), s32[]{:S(2)}) async-start(), calls=%async_computation | async-start | bytes 15728640 | tf_op jit(solution)/shard_map/all_gather | solution.py:140
  8.8 42.6 %collective-permute-start = (f32[16,4,24,2,256]{4,2,3,1,0:T(8,128)S(1)}, f32[16,4,24,2,256]{4,2,3,1,0:T(8,128)S(1)}, u32[]{:S(2)}, u32[]{:S(2)}) collective-permute-start(f32[16,4,24,2,256]{4,2,3,1,0:T(8,128)S(1)} %copy.154), channel_id=1, source_target_pairs={{4,0},{8,4},{12,8},{16,12},{20,16},{24,20},{28,24},{32,28},{36,32}... | collective-permute-start | bytes 9437192 | tf_op jit(solution)/shard_map/ppermute | solution.py:18
  16.6 40.0 %collective-permute-start.1 = (f32[16,4,24,2,256]{4,2,3,1,0:T(8,128)S(1)}, f32[16,4,24,2,256]{4,2,3,1,0:T(8,128)S(1)}, u32[]{:S(2)}, u32[]{:S(2)}) collective-permute-start(f32[16,4,24,2,256]{4,2,3,1,0:T(8,128)S(1)} %copy.154), channel_id=1, source_target_pairs={{0,4},{4,8},{8,12},{12,16},{16,20},{20,24},{24,28},{28,32},{32,36}... | collective-permute-start | bytes 9437192 | tf_op jit(solution)/shard_map/ppermute | solution.py:16
  22.2 36.1 %copy-start.15 = (f32[4,24]{1,0:T(4,128)S(1)}, f32[4,24]{1,0:T(4,128)}, u32[]{:S(2)}) copy-start(f32[4,24]{1,0:T(4,128)} %param.16) | copy-start | bytes 1156
  58.3 10.7 copy-start.16
  58.3 10.7 copy-start.17
  58.3 10.7 copy-start.18
  58.3 10.7 copy-start.19
  58.3 10.7 copy-start.10
  58.4 12.6 copy-start.20
  58.4 12.6 copy-start.21
  68.0 35.8 %collective-permute-start.2 = (f32[16,4,24,2,256]{4,2,3,1,0:T(8,128)S(1)}, f32[16,4,24,2,256]{4,2,3,1,0:T(8,128)}, u32[]{:S(2)}, u32[]{:S(2)}) collective-permute-start(f32[16,4,24,2,256]{4,2,3,1,0:T(8,128)S(1)} %fusion.259), channel_id=1, source_target_pairs={{4,0},{8,4},{12,8},{16,12},{20,16},{24,20},{28,24},{32,28},{36,32}... | collective-permute-start | bytes 9437192 | tf_op jit(solution)/shard_map/ppermute | solution.py:18
  69.0 40.1 %collective-permute-start.3 = (f32[16,4,24,2,256]{4,2,3,1,0:T(8,128)S(1)}, f32[16,4,24,2,256]{4,2,3,1,0:T(8,128)}, u32[]{:S(2)}, u32[]{:S(2)}) collective-permute-start(f32[16,4,24,2,256]{4,2,3,1,0:T(8,128)S(1)} %fusion.259), channel_id=1, source_target_pairs={{0,4},{4,8},{8,12},{12,16},{16,20},{20,24},{24,28},{28,32},{32,36}... | collective-permute-start | bytes 9437192 | tf_op jit(solution)/shard_map/ppermute | solution.py:16
  119.0 14.3 copy-start
  133.3 80.0 %copy-start.4 = (f32[1,64,64]{2,1,0:T(8,128)S(1)}, f32[1,64,64]{2,1,0:T(8,128)}, u32[]{:S(2)}) copy-start(f32[1,64,64]{2,1,0:T(8,128)} %copy-done.2) | copy-start | bytes 49156
  213.3 1031.2 %copy-start.1 = (f32[16,4,24,2,256]{4,3,2,1,0:T(2,128)S(1)}, f32[16,4,24,2,256]{4,3,2,1,0:T(2,128)}, u32[]{:S(2)}) copy-start(f32[16,4,24,2,256]{4,3,2,1,0:T(2,128)} %copy.169) | copy-start | bytes 9437188
  223.7 15.4 copy-start.11
  230.1 12.1 copy-start.12
  283.4 15.5 copy-start.11
  289.8 12.1 copy-start.12
  343.2 15.5 copy-start.11
  349.6 12.1 copy-start.12
  403.0 15.5 copy-start.11
  409.4 12.1 copy-start.12
  462.7 15.5 copy-start.11
  469.1 12.1 copy-start.12
  522.5 15.5 copy-start.11
  528.9 12.1 copy-start.12
  582.2 15.5 copy-start.11
  588.7 12.1 copy-start.12
  642.0 15.4 copy-start.11
  648.4 12.1 copy-start.12
  701.7 15.5 copy-start.11
  708.1 12.1 copy-start.12
  761.5 15.5 copy-start.11
  767.9 12.1 copy-start.12
  821.2 15.4 copy-start.11
  827.7 12.1 copy-start.12
  880.9 15.5 copy-start.11
  887.4 12.1 copy-start.12
  940.7 15.5 copy-start.11
  947.1 12.1 copy-start.12
  1000.4 15.5 copy-start.11
  1006.8 12.1 copy-start.12
  1060.1 15.5 copy-start.11
  1066.5 12.1 copy-start.12
  1119.9 15.5 copy-start.11
  1126.3 12.1 copy-start.12
  (69 other events, 312.2 us)
Sparse Core Ops, SparseCore 0:
  1248.4 116.5 all-gather.1
where the time goes:
time: 2150 us; the launch traced here: 2130 us
  loops' own time  841 us (39%)
  matrix products  504 us (23%)
  other arithmetic  452 us (21%)
  blocking collectives  147 us (7%)
  local copies, waits for them, and re-layouts  99.8 us (5%)
  waiting for transfers between devices  60.4 us (3%)
    another operation x2, loops' own time, assimilate(): lax.fori_loop(0, prior.shape[0], one_obs, (prior, start), unroll=8)[1]  841 us
    dot_general x256, matrix products, one_obs(): jnp.einsum('tab,b->ta', transform, scaled, precision=lax.Precision.HIGHEST)  262 us
    dot_general x256, matrix products, one_obs(): projected = jnp.dot(priors, scaled, precision=lax.Precision.HIGHEST)  233 us
    reduce_sum x256, other arithmetic, one_obs(): variance = jnp.sum(anomaly * anomaly) / (members - 1.0)  166 us
    reduce_sum x256, other arithmetic, one_obs(): centre = jnp.mean(sample)  164 us
    psum x1, blocking collectives, on_device(): second_prior = lax.psum(share, ('tile', 'mem'))  74.9 us
    psum x1, blocking collectives, on_device(): prior_first = lax.psum(placed[:half], ('tile', 'mem'))  72 us
    add x256, other arithmetic, one_obs(): priors = priors + (weight_rows * projected)[:, None] * increment[None, :]  62.6 us
  transfers between devices with their start and end apart: 5, of which 4 were waited for; matrix products, arithmetic and copies ran while one was open for 21% of the time, Pallas kernels for 0%

commit v1 on v0

v1 whole, which is shorter than its diff:
```python
import functools

import jax
import jax.numpy as jnp
from jax import lax
from jax.experimental import pallas as pl
from jax.experimental.pallas import tpu as pltpu
from jax.sharding import PartitionSpec as P

STEPS = 2


def padded(cells, sides, width):
    for axis, dim in sides:
        count = lax.axis_size(axis)
        head = lax.slice_in_dim(cells, 0, width, axis=dim)
        tail = lax.slice_in_dim(cells, cells.shape[dim] - width, cells.shape[dim], axis=dim)
        cells = jnp.concatenate(
            [
                lax.ppermute(tail, axis, [(i, (i + 1) % count) for i in range(count)]),
                cells,
                lax.ppermute(head, axis, [((i + 1) % count, i) for i in range(count)]),
            ],
            axis=dim,
        )
    return cells


def advance(extended, courant, diffusion):
    centre = extended[..., 2:-2, :]
    up_one = extended[..., 3:-1, :]
    down_one = extended[..., 1:-3, :]
    up_two = extended[..., 4:, :]
    down_two = extended[..., :-4, :]
    right_one = jnp.roll(centre, -1, axis=-1)
    left_one = jnp.roll(centre, 1, axis=-1)
    right_two = jnp.roll(centre, -2, axis=-1)
    left_two = jnp.roll(centre, 2, axis=-1)
    slope_rows = (8.0 * (up_one - down_one) - (up_two - down_two)) / 12.0
    slope_cols = (8.0 * (right_one - left_one) - (right_two - left_two)) / 12.0
    spread = up_one + down_one + right_one + left_one - 4.0 * centre
    return (
        centre
        - courant[0] * slope_rows
        - courant[1] * slope_cols
        + diffusion[:, :, None, None] * spread
    )


HI = lax.Precision.HIGHEST
BLK = 8


def filter_kernel(obs_ref, err_ref, root_ref, raw_ref, wide_ref, out_ref, gram, shift, slope, inc, mean_ref, *, members, group):
    count = raw_ref.shape[0]
    lanes = gram.shape[1]
    freedom = members - 1.0
    raw = raw_ref[...]
    centre = jnp.sum(raw, axis=1, keepdims=True) / members
    anomaly = raw - centre
    mean_ref[...] = jnp.transpose(jnp.broadcast_to(centre, (count, 8 * 16)))[:8, :]
    gram[:, :count] = lax.dot_general(
        anomaly, anomaly * (1.0 / freedom), (((1,), (1,)), ((), ())), precision=HI,
        preferred_element_type=jnp.float32)
    gram[:, count:] = jnp.concatenate([anomaly * (1.0 / freedom), anomaly], axis=1)

    def lift(array, row, column):
        return jnp.broadcast_to(jnp.broadcast_to(array[:, column:column + 1], (BLK, 128))[row:row + 1, :], (BLK, 128))

    def block(position, first, last):
        base = pl.multiple_of(position * BLK, BLK)
        tile = pl.multiple_of((base // 128) * 128, 128)
        back = lax.rem(128 - lax.rem(base, 128), 128)
        panel = gram[pl.ds(base, BLK), :]
        weight = wide_ref[pl.ds(base, BLK), :]
        corner = pltpu.roll(gram[pl.ds(base, BLK), pl.ds(tile, 128)], back, 1)
        corner_w = pltpu.roll(wide_ref[pl.ds(base, BLK), pl.ds(tile, 128)], back, 1)
        corner_m = pltpu.roll(mean_ref[:, pl.ds(tile, 128)], back, 1)
        cell = {(k, l): lift(corner, l, k) for l in range(BLK) for k in range(l, BLK)}
        means = [jnp.broadcast_to(corner_m[:, k:k + 1], (BLK, 128)) for k in range(BLK)]
        rows = [[jnp.broadcast_to(panel[k:k + 1, c:c + 128], (BLK, 128)) for c in range(0, lanes, 128)] for k in range(BLK)]
        line = lax.broadcasted_iota(jnp.int32, (BLK, 128), 0)
        tiles = range(lanes // 128)
        keep_x = [jnp.zeros((BLK, 128), jnp.float32) for _ in tiles]
        keep_z = [jnp.zeros((BLK, 128), jnp.float32) for _ in tiles]
        keep_g = jnp.zeros((BLK, 128), jnp.float32)
        mean_row = [mean_ref[:, c:c + 128] for c in range(0, count, 128)]
        for i in range(BLK):
            err = err_ref[base + i]
            root = root_ref[base + i]
            v = cell[i, i]
            s = v + err
            t = lax.rsqrt(s)
            e = 1.0 / (s + root * (s * t))
            h = 0.5 * (e * v)
            d = (obs_ref[base + i] - means[i]) * (t * t)
            xs, zs = {}, {}
            for k in range(i + 1, BLK):
                q = cell[k, i]
                xs[k] = lift(corner_w, i, k) * q
                zs[k] = e * (q - h * xs[k])
                means[k] = means[k] + d * xs[k]
            for l in range(i + 1, BLK):
                for k in range(l, BLK):
                    cell[k, l] = cell[k, l] - xs[k] * zs[l] - zs[k] * xs[l]
            for c in range(lanes // 128):
                q = rows[i][c]
                x = jnp.broadcast_to(weight[i:i + 1, 128 * c:128 * c + 128], (BLK, 128)) * q
                z = e * (q - h * x)
                for k in range(i + 1, BLK):
                    rows[k][c] = rows[k][c] - xs[k] * z - zs[k] * x
                keep_x[c] = jnp.where(line == i, x, keep_x[c])
                keep_z[c] = jnp.where(line == i, z, keep_z[c])
                if c < count // 128:
                    mean_row[c] = mean_row[c] + d * x
                if c == lanes // 128 - 1:
                    keep_g = jnp.where(line == i, d - e * q, keep_g)
        for c in range(count // 128):
            mean_ref[:, 128 * c:128 * c + 128] = mean_row[c]
        x = jnp.concatenate(keep_x, axis=1)
        z = jnp.concatenate(keep_z, axis=1)
        shift[pl.ds(base, BLK), :] = x
        slope[pl.ds(base, BLK), :] = z
        inc[pl.ds(base, BLK), :] = keep_g
        left = jnp.concatenate([x[:, first:last], z[:, first:last]], axis=0)
        right = jnp.concatenate([z, x], axis=0)
        gram[first:last, :] = gram[first:last, :] - lax.dot_general(
            left, right, (((0,), (0,)), ((), ())), precision=HI, preferred_element_type=jnp.float32)

    for first in range(0, count, group):
        last = first + group

        def body(position, carry):
            block(position, first, last)
            return carry

        lax.fori_loop(first // BLK, last // BLK, body, 0)
        if last < count:
            x = shift[first:last, :]
            z = slope[first:last, :]
            left = jnp.concatenate([x[:, last:count], z[:, last:count]], axis=0)
            right = jnp.concatenate([z, x], axis=0)
            gram[last:count, :] = gram[last:count, :] - lax.dot_general(
                left, right, (((0,), (0,)), ((), ())), precision=HI, preferred_element_type=jnp.float32)
    whole = lax.dot_general(
        inc[...], shift[:, count:], (((0,), (0,)), ((), ())), precision=HI, preferred_element_type=jnp.float32)
    eye = (lax.broadcasted_iota(jnp.int32, (members, members), 0) == lax.broadcasted_iota(jnp.int32, (members, members), 1))
    out_ref[...] = whole[members:2 * members, :members] + eye.astype(jnp.float32)


def run_filter(raw, obs_value, obs_error, wide, group=64):
    count, members = raw.shape
    lanes = count + 2 * members
    smem = pl.BlockSpec(memory_space=pltpu.SMEM)
    vmem = pl.BlockSpec(memory_space=pltpu.VMEM)
    return pl.pallas_call(
        functools.partial(filter_kernel, members=members, group=group),
        out_shape=jax.ShapeDtypeStruct((members, members), jnp.float32),
        in_specs=[smem, smem, smem, vmem, vmem],
        out_specs=vmem,
        scratch_shapes=[
            pltpu.VMEM((count, lanes), jnp.float32),
            pltpu.VMEM((count, lanes), jnp.float32),
            pltpu.VMEM((count, lanes), jnp.float32),
            pltpu.VMEM((count, 128), jnp.float32),
            pltpu.VMEM((8, count), jnp.float32),
        ],
        compiler_params=pltpu.CompilerParams(vmem_limit_bytes=32 * 2**20),
    )(obs_value, obs_error, jnp.sqrt(obs_error), raw, wide)


def wide_weights(observation_row, localize, own, rows_here, members):
    owner = observation_row // rows_here
    tiles = localize.shape[0]
    hot = (owner[None, :] == jnp.arange(tiles, dtype=jnp.int32)[:, None]).astype(jnp.float32)
    across = lax.dot_general(localize, hot, (((0,), (0,)), ((), ())), precision=HI)
    count = owner.shape[0]
    return jnp.concatenate(
        [across, jnp.broadcast_to(own[:, None], (count, members)), jnp.zeros((count, members), jnp.float32)], axis=1)


def on_device(
    ensemble,
    courant,
    diffusion,
    observation_row,
    observation_column,
    observation_field,
    observation_level,
    obs_value,
    obs_error,
    localize,
):
    members_here = ensemble.shape[0]
    rows_here = ensemble.shape[3]
    state = ensemble
    for step_count in range(STEPS):
        extended = padded(state, (("tile", 3),), 2)
        state = advance(extended, courant, diffusion)
    tile_pos = lax.axis_index("tile")
    member_start = lax.axis_index("mem") * members_here
    ens_size = members_here * lax.axis_size("mem")
    obs_count = observation_row.shape[0]
    local_row = observation_row - tile_pos * rows_here
    owned = (local_row >= 0) & (local_row < rows_here)
    clipped = jnp.clip(local_row, 0, rows_here - 1)
    sampled = state[:, observation_field, observation_level, clipped, observation_column].T
    mine = jnp.where(owned[:, None], sampled, 0.0)
    placed = lax.dynamic_update_slice(
        jnp.zeros((obs_count, ens_size), jnp.float32), mine, (jnp.int32(0), member_start)
    )
    raw = lax.psum(placed, ("tile", "mem"))
    own = lax.dynamic_slice_in_dim(localize, tile_pos, 1, 0)[0]
    wide = wide_weights(observation_row, localize, own, rows_here, ens_size)
    turned = run_filter(raw, obs_value, obs_error, wide)
    flat_state = state.reshape(members_here, -1)
    my_rows = lax.dynamic_slice(turned, (member_start, jnp.int32(0)), (members_here, ens_size))
    result = jnp.dot(
        my_rows,
        lax.all_gather(flat_state, "mem", axis=0, tiled=True),
        precision=lax.Precision.HIGHEST,
    )
    return result.reshape(state.shape)


def solution(mesh):
    placed = (
        P("mem", None, None, "tile", None),
        P(None, None, "tile", None),
        P(),
        P(),
        P(),
        P(),
        P(),
        P(),
        P(),
        P(),
    )
    return jax.shard_map(
        on_device,
        mesh=mesh,
        in_specs=placed,
        out_specs=P("mem", None, None, "tile", None),
        check_vma=False,
    )
```

time: 2150 us -> 504 us (0.23); the launches traced: 2130 us -> 504 us
  loops' own time: 841 us -> 0 us
  matrix products: 504 us -> 10.2 us
  other arithmetic: 452 us -> 19.6 us
  waiting for transfers between devices: 60.4 us -> 367 us
  blocking collectives: 147 us -> 0 us
  local copies, waits for them, and re-layouts: 99.8 us -> 56.8 us
  Pallas kernels: 0 us -> 26.2 us
    another operation x2 -> x0, loops' own time: 841 us -> none  [assimilate(): lax.fori_loop(0, prior.shape[0], one_obs, (prior, start), unroll=8)[1]]
    dot_general x516 -> x2, matrix products: 504 us -> 10.2 us  [the longest x1 9.88 us: on_device(): jnp.dot(my_rows, lax.all_gather(flat_state, 'mem', axis=0, tiled=True), p...]
    reduce_sum x512 -> x0, other arithmetic: 330 us -> none  [the longest x256 166 us: one_obs(): variance = jnp.sum(anomaly * anomaly) / (members - 1.0)]
    psum x0 -> x1, waiting for transfers between devices: none -> 305 us  [on_device(): raw = lax.psum(placed, ('tile', 'mem'))]
    psum x2 -> x0, blocking collectives: 147 us -> none  [the longest x1 74.9 us: on_device(): second_prior = lax.psum(share, ('tile', 'mem'))]
    add x320 -> x0, other arithmetic: 80.8 us -> none  [the longest x256 62.6 us: one_obs(): priors = priors + (weight_rows * projected)[:, None] * increment[None, :]]
    dynamic_slice x64 -> x1, local copies, waits for them, and re-layouts: 45.6 us -> 0.01 us  [on_device(): own = lax.dynamic_slice_in_dim(localize, tile_pos, 1, 0)[0]]
    pallas_call x0 -> x1, Pallas kernels: none -> 26.2 us  [run_filter(): pl.pallas_call(functools.partial(filter_kernel, members=members, group=gr...]
  transfers between devices with their start and end apart: 5 -> 6, of which waited for: 4 -> 5; matrix products, arithmetic and copies ran while one was open for 21% -> 5% of each run, Pallas kernels for 0% -> 5%
where the time goes in v1:
time: 504 us
  waiting for transfers between devices  367 us (73%)
  local copies, waits for them, and re-layouts  56.8 us (11%)
  Pallas kernels  26.2 us (5%)
  other arithmetic  19.6 us (4%)
  between operations  15.1 us (3%)
  matrix products  10.2 us (2%)
  starting transfers between devices  9.12 us (2%)
    psum x1, waiting for transfers between devices, on_device(): raw = lax.psum(placed, ('tile', 'mem'))  305 us
    ppermute x2, waiting for transfers between devices, padded(): lax.ppermute(head, axis, [((i + 1) % count, i) for i in range(count)])  51.6 us
    pallas_call x1, Pallas kernels, run_filter(): pl.pallas_call(functools.partial(filter_kernel, members=members, group=gr...  26.2 us
    add x2, other arithmetic, advance(): centre - courant[0] * slope_rows - courant[1] * slope_cols  19.3 us
    add x2, local copies, waits for them, and re-layouts, advance(): centre - courant[0] * slope_rows - courant[1] * slope_cols  17.9 us
    ppermute x2, waiting for transfers between devices, padded(): lax.ppermute(tail, axis, [(i, (i + 1) % count) for i in range(count)])  10.6 us
  transfers between devices with their start and end apart: 6, of which 5 were waited for; matrix products, arithmetic and copies ran while one was open for 5% of the time, Pallas kernels for 5%

profile of v1, /device:TPU:2, one launch (start us, length us, event | category | flops | bytes accessed | tf_op | source)
XLA Modules:
  0.0 503.8 jit_solution(12790385635510715619)
XLA Ops:
  7.4 0.0 copy-start
  7.4 0.0 all-reduce.2.cloned.1.call-start
  7.4 2.2 copy.144
  9.6 7.8 %collective-permute-start = (f32[16,4,24,2,256]{4,2,3,1,0:T(8,128)S(1)}, f32[16,4,24,2,256]{4,2,3,1,0:T(8,128)S(1)}, u32[]{:S(2)}, u32[]{:S(2)}) collective-permute-start(f32[16,4,24,2,256]{4,2,3,1,0:T(8,128)S(1)} %copy.144), channel_id=1, source_target_pairs={{4,0},{8,4},{12,8},{16,12},{20,16},{24,20},{28,24},{32,28},{36,32}... | collective-permute-start | bytes 9437192 | tf_op jit(solution)/shard_map/ppermute | solution.py:22
  17.4 0.0 collective-permute-start.1
  17.5 0.0 copy-done.8
  17.5 0.1 multiply_bitcast_fusion.1
  17.5 2.2 fusion.28
  19.7 2.2 fusion.29
  21.9 1.1 fusion.27
  23.1 0.0 copy-start.9
  23.1 3.8 fusion.30
  26.9 25.3 %collective-permute-done = f32[16,4,24,2,256]{4,2,3,1,0:T(8,128)S(1)} collective-permute-done((f32[16,4,24,2,256]{4,2,3,1,0:T(8,128)S(1)}, f32[16,4,24,2,256]{4,2,3,1,0:T(8,128)S(1)}, u32[]{:S(2)}, u32[]{:S(2)}) %collective-permute-start) | collective-permute-done | bytes 3145760 | tf_op jit(solution)/shard_map/ppermute | solution.py:22
  52.2 5.2 %collective-permute-done.1 = f32[16,4,24,2,256]{4,2,3,1,0:T(8,128)S(1)} collective-permute-done((f32[16,4,24,2,256]{4,2,3,1,0:T(8,128)S(1)}, f32[16,4,24,2,256]{4,2,3,1,0:T(8,128)S(1)}, u32[]{:S(2)}, u32[]{:S(2)}) %collective-permute-start.1) | collective-permute-done | bytes 3145760 | tf_op jit(solution)/shard_map/ppermute | solution.py:20
  57.5 0.0 copy-done.5
  57.5 1.7 copy-done.6
  59.2 0.0 copy-start.13
  59.2 9.5 %fusion.3 = f32[16,4,24,2,256]{4,2,3,1,0:T(8,128)S(1)} fusion(f32[16,4,24,2,2]{4,2,3,1,0:T(8,128)} %get-tuple-element.18, f32[16,4,24,2,254]{4,2,3,1,0:T(8,128)} %get-tuple-element.20, f32[16,4,24,2,254]{4,2,3,1,0:T(8,128)} %get-tuple-element.19, f32[16,4,24,2,2]{4,2,3,1,0:T(8,128)} %get-tuple-element.17, f32[16,4,24,2,256]{4,2,3,1,0:T(8,128)S(1)} %copy.144, ...), kind=kLoop, calls=%fused_computation.11 | loop fusion | flops 19660800 | bytes 25264512 | tf_op jit(solution)/shard_map/add | solution.py:43
  68.7 1.0 collective-permute-start.2
  69.8 0.0 collective-permute-start.3
  69.8 2.2 fusion.25
  72.1 2.2 fusion.24
  74.3 1.1 fusion.26
  75.4 2.8 fusion.23
  78.3 26.3 %collective-permute-done.2 = f32[16,4,24,2,256]{4,2,3,1,0:T(8,128)} collective-permute-done((f32[16,4,24,2,256]{4,2,3,1,0:T(8,128)S(1)}, f32[16,4,24,2,256]{4,2,3,1,0:T(8,128)}, u32[]{:S(2)}, u32[]{:S(2)}) %collective-permute-start.2) | collective-permute-done | bytes 3145760 | tf_op jit(solution)/shard_map/ppermute | solution.py:22
  104.5 5.3 %collective-permute-done.3 = f32[16,4,24,2,256]{4,2,3,1,0:T(8,128)} collective-permute-done((f32[16,4,24,2,256]{4,2,3,1,0:T(8,128)S(1)}, f32[16,4,24,2,256]{4,2,3,1,0:T(8,128)}, u32[]{:S(2)}, u32[]{:S(2)}) %collective-permute-start.3) | collective-permute-done | bytes 3145760 | tf_op jit(solution)/shard_map/ppermute | solution.py:20
  109.9 9.8 %fusion.7 = f32[16,4,24,2,256]{4,2,3,1,0:T(8,128)} fusion(f32[16,4,24,2,2]{4,2,3,1,0:T(8,128)} %get-tuple-element.10, f32[16,4,24,2,254]{4,2,3,1,0:T(8,128)S(1)} %get-tuple-element.12, f32[16,4,24,2,254]{4,2,3,1,0:T(8,128)S(1)} %get-tuple-element.11, f32[16,4,24,2,2]{4,2,3,1,0:T(8,128)} %get-tuple-element.9, f32[16,4,24,2,256]{4,2,3,1,0:T(8,128)S(1)} %fusion.3, ...), kind=kLoop, calls=%fused_computation.18 | loop fusion | flops 19660800 | bytes 25264512 | tf_op jit(solution)/shard_map/add | solution.py:43
  119.7 14.5 %copy.155 = f32[16,4,24,2,256]{0,4,3,2,1:T(8,128)} copy(f32[16,4,24,2,256]{4,2,3,1,0:T(8,128)} %fusion.7) | data formatting | bytes 6291456 | tf_op jit(solution)/shard_map/add | solution.py:43
  134.1 3.6 gather_fusion
  137.7 0.1 broadcast_select_fusion
  137.8 0.9 dynamic_update_slice.3
  138.7 0.6 copy-done.7
  139.4 0.0 all-reduce.2.cloned.1.call-update
  139.4 0.3 all-gather.2.cloned.1.call-start
  139.7 3.4 copy.157
  143.1 5.1 %reshape.16 = f32[16,49152]{1,0:T(8,128)} reshape(f32[16,4,24,2,256]{4,3,2,1,0:T(2,128)} %copy.157) | data formatting | bytes 6291456 | tf_op jit(solution)/shard_map/reshape | solution.py:216
  148.3 0.0 all-gather.2.cloned.1.call-update
  148.3 0.7 copy-done.2
  148.9 0.3 convolution_bitcast_fusion
  149.3 0.1 broadcast_in_dim.41
  149.4 0.1 pad_maximum_fusion.8.wide_ref
  149.5 304.6 %all-reduce.2.cloned.1.call-done.raw_ref = f32[256,64]{1,0:T(8,128)} async-done(((f32[256,64]{1,0:T(8,128)}), f32[256,64]{1,0:T(8,128)}) %all-reduce.2.cloned.1.call-update) | async-done | bytes 65552 | tf_op jit(solution)/shard_map/psum | solution.py:212
  454.1 0.0 copy-done.3
  454.1 0.9 copy-done.1
  455.0 26.2 %shard_map.100 = f32[64,64]{1,0:T(8,128)S(1)} custom-call(f32[256]{0:T(256)S(1)} %copy-done.3, f32[256]{0:T(256)S(1)} %copy-done.2, f32[256]{0:T(256)S(1)} %sqrt.3.root_ref, f32[256,64]{1,0:T(8,128)S(1)} %copy-done.1, f32[256,384]{1,0:T(8,128)S(1)} %pad_maximum_fusion.8.wide_ref), custom_call_target="tpu_custom_call" | custom-call | tf_op jit(solution)/shard_map/pallas_call | solution.py:156
  481.2 0.0 all-gather.2.cloned.1.call-done
  481.3 9.9 %fusion.9 = f32[16,49152]{1,0:T(8,128)} fusion(f32[64,49152]{1,0:T(8,128)} %all-gather.2.cloned.1.call-done, f32[64,64]{1,0:T(8,128)S(1)} %shard_map.100, s32[]{:T(128)S(6)} %select_n.37), kind=kOutput, calls=%fused_computation.26 | convolution fusion | flops 603979776 | bytes 15736836 | tf_op jit(solution)/shard_map/dot_general | solution.py:218
  491.2 5.2 %reshape.17 = f32[16,4,24,2,256]{4,3,2,1,0:T(2,128)} reshape(f32[16,49152]{1,0:T(8,128)} %fusion.9) | data formatting | bytes 6291456 | tf_op jit(solution)/shard_map/reshape | solution.py:223
  (26 shorter events, 0.1 us)
Async XLA Ops:
  7.4 141.6 %copy-start = (f32[64,256]{1,0:T(8,128)S(1)}, f32[64,256]{1,0:T(8,128)}, u32[]{:S(2)}) copy-start(f32[64,256]{1,0:T(8,128)} %param.19) | copy-start | bytes 196612
  7.4 10.1 %copy-start.8 = (f32[2,24,2,256]{3,2,1,0:T(2,128)S(1)}, f32[2,24,2,256]{3,2,1,0:T(2,128)}, u32[]{:S(2)}) copy-start(f32[2,24,2,256]{3,2,1,0:T(2,128)} %param.11) | copy-start | bytes 294916
  7.4 446.7 %all-reduce.2.cloned.1.call-start = ((), (), s32[]{:S(2)}) async-start(), calls=%async_computation | async-start | bytes 262144 | tf_op jit(solution)/shard_map/psum | solution.py:212
  9.6 42.6 %collective-permute-start = (f32[16,4,24,2,256]{4,2,3,1,0:T(8,128)S(1)}, f32[16,4,24,2,256]{4,2,3,1,0:T(8,128)S(1)}, u32[]{:S(2)}, u32[]{:S(2)}) collective-permute-start(f32[16,4,24,2,256]{4,2,3,1,0:T(8,128)S(1)} %copy.144), channel_id=1, source_target_pairs={{4,0},{8,4},{12,8},{16,12},{20,16},{24,20},{28,24},{32,28},{36,32}... | collective-permute-start | bytes 9437192 | tf_op jit(solution)/shard_map/ppermute | solution.py:22
  17.4 40.0 %collective-permute-start.1 = (f32[16,4,24,2,256]{4,2,3,1,0:T(8,128)S(1)}, f32[16,4,24,2,256]{4,2,3,1,0:T(8,128)S(1)}, u32[]{:S(2)}, u32[]{:S(2)}) collective-permute-start(f32[16,4,24,2,256]{4,2,3,1,0:T(8,128)S(1)} %copy.144), channel_id=1, source_target_pairs={{0,4},{4,8},{8,12},{12,16},{16,20},{20,24},{24,28},{28,32},{32,36}... | collective-permute-start | bytes 9437192 | tf_op jit(solution)/shard_map/ppermute | solution.py:20
  23.1 36.1 %copy-start.9 = (f32[4,24]{1,0:T(4,128)S(1)}, f32[4,24]{1,0:T(4,128)}, u32[]{:S(2)}) copy-start(f32[4,24]{1,0:T(4,128)} %param.12) | copy-start | bytes 1156
  52.2 5.2 %copy-start.5 = (f32[16,4,24,2,256]{4,2,3,1,0:T(8,128)}, f32[16,4,24,2,256]{4,2,3,1,0:T(8,128)S(1)}, u32[]{:S(2)}) copy-start(f32[16,4,24,2,256]{4,2,3,1,0:T(8,128)S(1)} %collective-permute-done) | copy-start | bytes 9437188
  57.5 1.7 copy-start.6
  59.2 10.6 %copy-start.10 = (s32[256]{0:T(256)S(1)}, s32[256]{0:T(256)}, u32[]{:S(2)}) copy-start(s32[256]{0:T(256)} %param.13) | copy-start | bytes 3076
  59.2 10.6 %copy-start.11 = (s32[256]{0:T(256)S(1)}, s32[256]{0:T(256)}, u32[]{:S(2)}) copy-start(s32[256]{0:T(256)} %param.14) | copy-start | bytes 3076
  59.2 10.6 %copy-start.12 = (s32[256]{0:T(256)S(1)}, s32[256]{0:T(256)}, u32[]{:S(2)}) copy-start(s32[256]{0:T(256)} %param.16) | copy-start | bytes 3076
  59.2 10.6 %copy-start.13 = (s32[256]{0:T(256)S(1)}, s32[256]{0:T(256)}, u32[]{:S(2)}) copy-start(s32[256]{0:T(256)} %param.15) | copy-start | bytes 3076
  68.7 35.8 %collective-permute-start.2 = (f32[16,4,24,2,256]{4,2,3,1,0:T(8,128)S(1)}, f32[16,4,24,2,256]{4,2,3,1,0:T(8,128)}, u32[]{:S(2)}, u32[]{:S(2)}) collective-permute-start(f32[16,4,24,2,256]{4,2,3,1,0:T(8,128)S(1)} %fusion.3), channel_id=1, source_target_pairs={{4,0},{8,4},{12,8},{16,12},{20,16},{24,20},{28,24},{32,28},{36,32}... | collective-permute-start | bytes 9437192 | tf_op jit(solution)/shard_map/ppermute | solution.py:22
  69.8 40.1 %collective-permute-start.3 = (f32[16,4,24,2,256]{4,2,3,1,0:T(8,128)S(1)}, f32[16,4,24,2,256]{4,2,3,1,0:T(8,128)}, u32[]{:S(2)}, u32[]{:S(2)}) collective-permute-start(f32[16,4,24,2,256]{4,2,3,1,0:T(8,128)S(1)} %fusion.3), channel_id=1, source_target_pairs={{0,4},{4,8},{8,12},{12,16},{16,20},{20,24},{24,28},{28,32},{32,36}... | collective-permute-start | bytes 9437192 | tf_op jit(solution)/shard_map/ppermute | solution.py:20
  119.7 20.0 %copy-start.4 = (f32[16,4,24,2,256]{4,2,3,1,0:T(8,128)S(1)}, f32[16,4,24,2,256]{4,2,3,1,0:T(8,128)}, u32[]{:S(2)}) copy-start(f32[16,4,24,2,256]{4,2,3,1,0:T(8,128)} %fusion.7) | copy-start | bytes 9437188
  138.7 0.7 copy-start.7
  139.4 341.9 %all-gather.2.cloned.1.call-start = ((), (), s32[]{:S(2)}) async-start(), calls=%async_computation.1 | async-start | bytes 15728640 | tf_op jit(solution)/shard_map/all_gather | solution.py:220
  148.2 0.7 copy-start.2
  148.3 305.8 %copy-start.3 = (f32[256]{0:T(256)S(1)}, f32[256]{0:T(256)}, u32[]{:S(2)}) copy-start(f32[256]{0:T(256)} %obs_ref.1) | copy-start | bytes 3076
  454.1 0.9 copy-start.1
Sparse Core Ops, SparseCore 0:
  139.5 314.5 all-reduce.1
Sparse Core Ops, SparseCore 1:
  148.4 114.8 all-gather.1

commit v2 on v1

--- a/solution.py
+++ b/solution.py
@@ -8,54 +8,113 @@
 from jax.sharding import PartitionSpec as P
 
 STEPS = 2
-
-
-def padded(cells, sides, width):
-    for axis, dim in sides:
-        count = lax.axis_size(axis)
-        head = lax.slice_in_dim(cells, 0, width, axis=dim)
-        tail = lax.slice_in_dim(cells, cells.shape[dim] - width, cells.shape[dim], axis=dim)
-        cells = jnp.concatenate(
-            [
-                lax.ppermute(tail, axis, [(i, (i + 1) % count) for i in range(count)]),
-                cells,
-                lax.ppermute(head, axis, [((i + 1) % count, i) for i in range(count)]),
-            ],
-            axis=dim,
-        )
-    return cells
-
-
-def advance(extended, courant, diffusion):
-    centre = extended[..., 2:-2, :]
-    up_one = extended[..., 3:-1, :]
-    down_one = extended[..., 1:-3, :]
-    up_two = extended[..., 4:, :]
-    down_two = extended[..., :-4, :]
-    right_one = jnp.roll(centre, -1, axis=-1)
-    left_one = jnp.roll(centre, 1, axis=-1)
-    right_two = jnp.roll(centre, -2, axis=-1)
-    left_two = jnp.roll(centre, 2, axis=-1)
-    slope_rows = (8.0 * (up_one - down_one) - (up_two - down_two)) / 12.0
-    slope_cols = (8.0 * (right_one - left_one) - (right_two - left_two)) / 12.0
-    spread = up_one + down_one + right_one + left_one - 4.0 * centre
-    return (
-        centre
-        - courant[0] * slope_rows
-        - courant[1] * slope_cols
-        + diffusion[:, :, None, None] * spread
-    )
-
-
 HI = lax.Precision.HIGHEST
 BLK = 8
-
-
-def filter_kernel(obs_ref, err_ref, root_ref, raw_ref, wide_ref, out_ref, gram, shift, slope, inc, mean_ref, *, members, group):
-    count = raw_ref.shape[0]
+SUB = 8
+GROUPS = ((0, 1), (2, 3))
+
+
+def iota(shape, dim):
+    return lax.broadcasted_iota(jnp.int32, shape, dim)
+
+
+def step_kernel(cells_ref, below_ref, above_ref, courant_ref, spread_ref, *refs):
+    out_ref = refs[-1]
+    width = cells_ref.shape[-1]
+    spread = spread_ref[0]
+    for r in range(2):
+        along, across = courant_ref[0, r], courant_ref[1, r]
+        middle = 1.0 - 4.0 * spread
+        up, down, two = spread - along * (2.0 / 3.0), spread + along * (2.0 / 3.0), along * (1.0 / 12.0)
+        right, left, far = spread - across * (2.0 / 3.0), spread + across * (2.0 / 3.0), across * (1.0 / 12.0)
+        for member in range(cells_ref.shape[0]):
+            rows = [ref[member, 0, i] for ref in (below_ref, cells_ref, above_ref) for i in range(2)]
+            centre = rows[2 + r]
+            out_ref[member, 0, r] = (
+                (middle * centre + two * (rows[4 + r] - rows[r]))
+                + (up * rows[3 + r] + down * rows[1 + r])
+                + (right * pltpu.roll(centre, width - 1, 1) + left * pltpu.roll(centre, 1, 1))
+                + far * (pltpu.roll(centre, width - 2, 1) - pltpu.roll(centre, 2, 1))
+            )
+
+
+def forecast_step(cells, below, above, courant, spread, field, into=None):
+    count, _, rows, levels, width = below.shape
+    part = 8
+    block = pl.BlockSpec((part, 1, rows, levels, width), lambda m: (m, 0, 0, 0, 0))
+    fields, place, sofar = into or (1, 0, None)
+    more = [] if sofar is None else [sofar]
+    return pl.pallas_call(
+        step_kernel,
+        grid=(count // part,),
+        out_shape=jax.ShapeDtypeStruct((count, fields, rows, levels, width), jnp.float32),
+        in_specs=[
+            block,
+            block,
+            block,
+            pl.BlockSpec((2, rows, levels, width), lambda m: (0, 0, 0, 0)),
+            pl.BlockSpec((1, levels, width), lambda m: (field, 0, 0)),
+        ] + [pl.BlockSpec(memory_space=pl.ANY) for _ in more],
+        out_specs=pl.BlockSpec((part, 1, rows, levels, width), lambda m: (m, place, 0, 0, 0)),
+        input_output_aliases={5: 0} if more else {},
+        cost_estimate=pl.CostEstimate(flops=26 * below.size, bytes_accessed=16 * below.size, transcendentals=0),
+    )(cells, below, above, courant, spread, *more)
+
+
+def sample_kernel(tile_ref, row_ref, column_ref, field_ref, level_ref, *refs):
+    out_ref = refs[-1]
+    fields = refs[:-1]
+    members, count = out_ref.shape
+    rows_here = fields[0].shape[2]
+    first = tile_ref[0] * rows_here
+    out_ref[...] = jnp.zeros(out_ref.shape, jnp.float32)
+    line = iota((members, SUB, 128), 1)
+    place = iota((members, 128), 1)
+
+    def one(k, carry):
+        row = row_ref[k] - first
+
+        @pl.when((row >= 0) & (row < rows_here))
+        def _():
+            level = level_ref[k]
+            column = column_ref[k]
+            level_base = pl.multiple_of((level // SUB) * SUB, SUB)
+            column_base = pl.multiple_of((column // 128) * 128, 128)
+            target = pl.multiple_of((k // 128) * 128, 128)
+            for f, (ref, inner) in enumerate((ref, g) for ref in fields for g in range(ref.shape[1])):
+
+                @pl.when(field_ref[k] == f)
+                def _(ref=ref, inner=inner):
+                    seen = ref[:, inner, row, pl.ds(level_base, SUB), pl.ds(column_base, 128)]
+                    value = jnp.sum(jnp.where(line == level - level_base, seen, 0.0), axis=1)
+                    shift = lax.rem(k - column + 512, 128)
+                    value = pltpu.roll(value, shift, 1)
+                    kept = out_ref[:, pl.ds(target, 128)]
+                    out_ref[:, pl.ds(target, 128)] = jnp.where(place == k - target, value, kept)
+
+        return carry
+
+    lax.fori_loop(0, count, one, 0)
+
+
+def sample(state, tile_pos, row, column, field, level):
+    smem = pl.BlockSpec(memory_space=pltpu.SMEM)
+    vmem = pl.BlockSpec(memory_space=pltpu.VMEM)
+    return pl.pallas_call(
+        sample_kernel,
+        out_shape=jax.ShapeDtypeStruct((state[0].shape[0], row.shape[0]), jnp.float32),
+        in_specs=[smem] * 5 + [vmem] * len(state),
+        out_specs=vmem,
+        compiler_params=pltpu.CompilerParams(vmem_limit_bytes=32 * 2**20),
+    )(tile_pos.reshape(1), row, column, field, level, *state)
+
+
+def filter_kernel(obs_ref, err_ref, root_ref, raw_0, raw_1, raw_2, raw_3, wide_ref, high_ref, low_ref, gram, shift, slope, inc, mean_ref, *, members, group):
+    count = raw_0.shape[1]
     lanes = gram.shape[1]
     freedom = members - 1.0
-    raw = raw_ref[...]
+    here = raw_0.shape[0]
+    raw = jnp.transpose(jnp.concatenate([raw_0[...], raw_1[...], raw_2[...], raw_3[...]], axis=0))
     centre = jnp.sum(raw, axis=1, keepdims=True) / members
     anomaly = raw - centre
     mean_ref[...] = jnp.transpose(jnp.broadcast_to(centre, (count, 8 * 16)))[:8, :]
@@ -144,20 +203,30 @@
                 left, right, (((0,), (0,)), ((), ())), precision=HI, preferred_element_type=jnp.float32)
     whole = lax.dot_general(
         inc[...], shift[:, count:], (((0,), (0,)), ((), ())), precision=HI, preferred_element_type=jnp.float32)
-    eye = (lax.broadcasted_iota(jnp.int32, (members, members), 0) == lax.broadcasted_iota(jnp.int32, (members, members), 1))
-    out_ref[...] = whole[members:2 * members, :members] + eye.astype(jnp.float32)
-
-
-def run_filter(raw, obs_value, obs_error, wide, group=64):
-    count, members = raw.shape
+    mine = whole[members:members + here, :members]
+    mine = mine + (iota(mine.shape, 0) == iota(mine.shape, 1)).astype(jnp.float32)
+    tall, broad = high_ref.shape
+    down = (iota((tall, here), 0) // SUB == iota((tall, here), 1)).astype(jnp.float32)
+    over = (iota((members, broad), 1) // SUB == iota((members, broad), 0)).astype(jnp.float32)
+    spread = jnp.dot(jnp.dot(down, mine, precision=HI), over, precision=HI)
+    spread = jnp.where(iota((tall, broad), 0) % SUB == iota((tall, broad), 1) % SUB, spread, 0.0)
+    high = spread.astype(jnp.bfloat16)
+    high_ref[...] = high
+    low_ref[...] = (spread - high.astype(jnp.float32)).astype(jnp.bfloat16)
+
+
+def run_filter(pieces, obs_value, obs_error, wide, group=64):
+    here, count = pieces[0].shape
+    members = here * len(pieces)
     lanes = count + 2 * members
     smem = pl.BlockSpec(memory_space=pltpu.SMEM)
     vmem = pl.BlockSpec(memory_space=pltpu.VMEM)
+    spread = jax.ShapeDtypeStruct((here * SUB, members * SUB), jnp.bfloat16)
     return pl.pallas_call(
         functools.partial(filter_kernel, members=members, group=group),
-        out_shape=jax.ShapeDtypeStruct((members, members), jnp.float32),
-        in_specs=[smem, smem, smem, vmem, vmem],
-        out_specs=vmem,
+        out_shape=(spread, spread),
+        in_specs=[smem] * 3 + [vmem] * 5,
+        out_specs=(vmem, vmem),
         scratch_shapes=[
             pltpu.VMEM((count, lanes), jnp.float32),
             pltpu.VMEM((count, lanes), jnp.float32),
@@ -166,7 +235,7 @@
             pltpu.VMEM((8, count), jnp.float32),
         ],
         compiler_params=pltpu.CompilerParams(vmem_limit_bytes=32 * 2**20),
-    )(obs_value, obs_error, jnp.sqrt(obs_error), raw, wide)
+    )(obs_value, obs_error, jnp.sqrt(obs_error), *pieces, wide)
 
 
 def wide_weights(observation_row, localize, own, rows_here, members):
@@ -177,6 +246,49 @@
     count = owner.shape[0]
     return jnp.concatenate(
         [across, jnp.broadcast_to(own[:, None], (count, members)), jnp.zeros((count, members), jnp.float32)], axis=1)
+
+
+def update_kernel(order_ref, high_ref, low_ref, *refs):
+    out_ref = refs[-1]
+    high = high_ref[...]
+    low = low_ref[...]
+    both = jnp.concatenate([high, low], axis=0)
+    tall = high.shape[0]
+    here = out_ref.shape[0]
+    groups = refs[0].shape[0] // here
+    for f, (ref, inner) in enumerate((ref, g) for ref in refs[:-1] for g in range(ref.shape[1])):
+        for r in range(out_ref.shape[2]):
+            cells = jnp.concatenate(
+                [ref[pl.ds(order_ref[j] * here, here), inner, r].reshape(-1, ref.shape[-1]) for j in range(groups)], axis=0
+            )
+            top = cells.astype(jnp.bfloat16)
+            rest = (cells - top.astype(jnp.float32)).astype(jnp.bfloat16)
+            first = jnp.dot(both, top, preferred_element_type=jnp.float32)
+            second = jnp.dot(high, rest, preferred_element_type=jnp.float32)
+            total = first[:tall] + (first[tall:] + second)
+            out_ref[:, f, r] = total.reshape(out_ref.shape[0], SUB, -1)
+
+
+def update(order, high, low, gathered):
+    flat = gathered
+    _, _, rows, levels, width = flat[0].shape
+    here = high.shape[0] // SUB
+    fields = sum(p.shape[1] for p in flat)
+    full = pl.BlockSpec(high.shape, lambda i: (0, 0))
+    return pl.pallas_call(
+        update_kernel,
+        grid=(levels // SUB,),
+        out_shape=jax.ShapeDtypeStruct((here, fields, rows, levels, width), jnp.float32),
+        in_specs=[pl.BlockSpec(memory_space=pltpu.SMEM), full, full] + [pl.BlockSpec(p.shape[:2] + (rows, SUB, width), lambda i: (0, 0, 0, i, 0)) for p in flat],
+        out_specs=pl.BlockSpec((here, fields, rows, SUB, width), lambda i: (0, 0, 0, i, 0)),
+        compiler_params=pltpu.CompilerParams(vmem_limit_bytes=40 * 2**20),
+    )(order, high, low, *flat)
+
+
+def exchange(total, swaps):
+    for pairs in swaps:
+        total = total + lax.ppermute(total, "tile", pairs)
+    return total
 
 
 def on_device(
@@ -191,36 +303,42 @@
     obs_error,
     localize,
 ):
-    members_here = ensemble.shape[0]
-    rows_here = ensemble.shape[3]
-    state = ensemble
-    for step_count in range(STEPS):
-        extended = padded(state, (("tile", 3),), 2)
-        state = advance(extended, courant, diffusion)
+    members_here, fields, levels, rows_here, width = ensemble.shape
+    tiles = lax.axis_size("tile")
+    groups = lax.axis_size("mem")
+    ens_size = members_here * groups
     tile_pos = lax.axis_index("tile")
-    member_start = lax.axis_index("mem") * members_here
-    ens_size = members_here * lax.axis_size("mem")
-    obs_count = observation_row.shape[0]
-    local_row = observation_row - tile_pos * rows_here
-    owned = (local_row >= 0) & (local_row < rows_here)
-    clipped = jnp.clip(local_row, 0, rows_here - 1)
-    sampled = state[:, observation_field, observation_level, clipped, observation_column].T
-    mine = jnp.where(owned[:, None], sampled, 0.0)
-    placed = lax.dynamic_update_slice(
-        jnp.zeros((obs_count, ens_size), jnp.float32), mine, (jnp.int32(0), member_start)
-    )
-    raw = lax.psum(placed, ("tile", "mem"))
+    onward = [(i, (i + 1) % tiles) for i in range(tiles)]
+    backward = [((i + 1) % tiles, i) for i in range(tiles)]
+    start = jnp.transpose(ensemble, (0, 1, 3, 2, 4))
+    flow = jnp.transpose(courant, (0, 2, 1, 3))
+    spread = jnp.broadcast_to(diffusion[:, :, None], (fields, levels, width))
     own = lax.dynamic_slice_in_dim(localize, tile_pos, 1, 0)[0]
     wide = wide_weights(observation_row, localize, own, rows_here, ens_size)
-    turned = run_filter(raw, obs_value, obs_error, wide)
-    flat_state = state.reshape(members_here, -1)
-    my_rows = lax.dynamic_slice(turned, (member_start, jnp.int32(0)), (members_here, ens_size))
-    result = jnp.dot(
-        my_rows,
-        lax.all_gather(flat_state, "mem", axis=0, tiled=True),
-        precision=lax.Precision.HIGHEST,
-    )
-    return result.reshape(state.shape)
+
+    state = []
+    for group in GROUPS:
+        whole = None
+        middle = []
+        for f in group:
+            cells = start[:, f:f + 1]
+            below = lax.ppermute(cells, "tile", onward)
+            above = lax.ppermute(cells, "tile", backward)
+            middle.append(forecast_step(cells, below, above, flow, spread, f))
+        for place, f in enumerate(group):
+            below = lax.ppermute(middle[place], "tile", onward)
+            above = lax.ppermute(middle[place], "tile", backward)
+            whole = forecast_step(middle[place], below, above, flow, spread, f, (len(group), place, whole))
+        state.append(whole)
+    gathered = [lax.all_gather(cells, "mem", axis=0, tiled=True) for cells in state]
+    seen = sample(state, tile_pos, observation_row, observation_column, observation_field, observation_level)
+    swaps = [[(i, i ^ bit) for i in range(tiles)] for bit in (1, 2, 4, 8, 16, 32)]
+    seen = exchange(seen, swaps)
+    pieces = [seen] + [lax.ppermute(seen, "mem", [(i, (i + d) % groups) for i in range(groups)]) for d in range(1, groups)]
+    high, low = run_filter(pieces, obs_value, obs_error, wide)
+    order = lax.rem(lax.axis_index("mem") - jnp.arange(groups, dtype=jnp.int32) + groups, groups)
+    result = update(order, high, low, gathered)
+    return jnp.transpose(result, (0, 1, 3, 2, 4))
 
 
 def solution(mesh):

time: 504 us -> 217 us (0.43)
  waiting for transfers between devices: 367 us -> 95.1 us
  local copies, waits for them, and re-layouts: 56.8 us -> 14.8 us
  Pallas kernels: 26.2 us -> 62.8 us
  other arithmetic: 19.6 us -> 0.08 us
  starting transfers between devices: 9.12 us -> 28.5 us
  matrix products: 10.2 us -> 0.32 us
    psum x1 -> x0, waiting for transfers between devices: 305 us -> none  [on_device(): raw = lax.psum(placed, ('tile', 'mem'))]
    pallas_call x0 -> x10, Pallas kernels: none -> 35.9 us  [the longest x8 25.3 us: forecast_step(): pl.pallas_call(step_kernel, grid=(count // part,), out_shape=jax.ShapeDty...]
    ppermute x4 -> x25, starting transfers between devices: 8.85 us -> 28.5 us  [the longest x4 18.8 us: on_device(): above = lax.ppermute(cells, 'tile', backward)]
    add x2 -> x6, other arithmetic: 19.3 us -> 0.03 us  [exchange(): total = total + lax.ppermute(total, 'tile', pairs)]
    add x2 -> x0, local copies, waits for them, and re-layouts: 17.9 us -> none  [advance(): centre - courant[0] * slope_rows - courant[1] * slope_cols]
    all_gather x1 -> x2, waiting for transfers between devices: 0.03 us -> 17.8 us  [on_device(): lax.all_gather(cells, 'mem', axis=0, tiled=True)]
    slice x8 -> x1, local copies, waits for them, and re-layouts: 17.8 us -> 0.27 us  [on_device(): cells = start[:, f:f + 1]]
    ppermute x4 -> x25, waiting for transfers between devices: 62.1 us -> 77.3 us  [the longest x6 25.5 us: exchange(): total = total + lax.ppermute(total, 'tile', pairs)]
  transfers between devices with their start and end apart: 6 -> 27, of which waited for: 5 -> 21; matrix products, arithmetic and copies ran while one was open for 5% -> 1% of each run, Pallas kernels for 5% -> 25%
where the time goes in v2:
time: 217 us; the launch traced here: 215 us
  waiting for transfers between devices  95.1 us (44%)
  Pallas kernels  62.8 us (29%)
  starting transfers between devices  28.5 us (13%)
  local copies, waits for them, and re-layouts  14.8 us (7%)
  between operations  13.7 us (6%)
    pallas_call x1, Pallas kernels, run_filter(): pl.pallas_call(functools.partial(filter_kernel, members=members, group=gr...  26.9 us
    ppermute x6, waiting for transfers between devices, exchange(): total = total + lax.ppermute(total, 'tile', pairs)  25.5 us
    pallas_call x8, Pallas kernels, forecast_step(): pl.pallas_call(step_kernel, grid=(count // part,), out_shape=jax.ShapeDty...  25.3 us
    ppermute x4, waiting for transfers between devices, on_device(): below = lax.ppermute(middle[place], 'tile', onward)  20.6 us
    ppermute x4, starting transfers between devices, on_device(): above = lax.ppermute(cells, 'tile', backward)  18.8 us
    all_gather x2, waiting for transfers between devices, on_device(): lax.all_gather(cells, 'mem', axis=0, tiled=True)  17.8 us
    ppermute x4, waiting for transfers between devices, on_device(): below = lax.ppermute(cells, 'tile', onward)  17.5 us
    unnamed x54, local copies, waits for them, and re-layouts  10.1 us
  transfers between devices with their start and end apart: 27, of which 21 were waited for; matrix products, arithmetic and copies ran while one was open for 1% of the time, Pallas kernels for 25%

profile of v2, /device:TPU:2, one launch (start us, length us, event | category | flops | bytes accessed | tf_op | source)
XLA Modules:
  0.0 215.3 jit_solution(16589698646552218941)
XLA Ops:
  6.5 2.2 %copy.24 = f32[16,4,24,2,256]{4,2,3,1,0:T(8,128)S(1)} copy(f32[16,4,24,2,256]{4,3,2,1,0:T(2,128)} %param.10) | data formatting | bytes 6291456 | tf_op args[0]
  9.1 7.8 %collective-permute-start.13 = (f32[16,1,2,24,256]{4,3,2,1,0:T(8,128)S(1)}, f32[16,1,2,24,256]{4,3,2,1,0:T(8,128)S(1)}, u32[]{:S(2)}, u32[]{:S(2)}) collective-permute-start(f32[16,1,2,24,256]{4,3,2,1,0:T(8,128)S(1)} %get-tuple-element.9.cells_ref), channel_id=1, source_target_pairs={{4,0},{8,4},{12,8},{16,12},{20,16},{24,20},{28,24},{32,28},{36,32}... | collective-permute-start | bytes 2359304 | tf_op jit(solution)/shard_map/ppermute | solution.py:326
  16.9 5.1 %collective-permute-start.9 = (f32[16,1,2,24,256]{4,3,2,1,0:T(8,128)S(1)}, f32[16,1,2,24,256]{4,3,2,1,0:T(8,128)}, u32[]{:S(2)}, u32[]{:S(2)}) collective-permute-start(f32[16,1,2,24,256]{4,3,2,1,0:T(8,128)S(1)} %get-tuple-element.10.cells_ref), channel_id=1, source_target_pairs={{4,0},{8,4},{12,8},{16,12},{20,16},{24,20},{28,24},{32,28},{36,32}... | collective-permute-start | bytes 2359304 | tf_op jit(solution)/shard_map/ppermute | solution.py:326
  22.7 3.8 %collective-permute-done.13.above_ref = f32[16,1,2,24,256]{4,3,2,1,0:T(8,128)S(1)} collective-permute-done((f32[16,1,2,24,256]{4,3,2,1,0:T(8,128)S(1)}, f32[16,1,2,24,256]{4,3,2,1,0:T(8,128)S(1)}, u32[]{:S(2)}, u32[]{:S(2)}) %collective-permute-start.13) | collective-permute-done | bytes 786464 | tf_op jit(solution)/shard_map/ppermute | solution.py:326
  26.5 5.2 %collective-permute-done.12.below_ref = f32[16,1,2,24,256]{4,3,2,1,0:T(8,128)S(1)} collective-permute-done((f32[16,1,2,24,256]{4,3,2,1,0:T(8,128)S(1)}, f32[16,1,2,24,256]{4,3,2,1,0:T(8,128)S(1)}, u32[]{:S(2)}, u32[]{:S(2)}) %collective-permute-start.12) | collective-permute-done | bytes 786464 | tf_op jit(solution)/shard_map/ppermute | solution.py:325
  31.7 0.8 broadcast_in_dim.8.spread_ref
  32.6 3.2 %shard_map.105.cells_ref = f32[16,1,2,24,256]{4,3,2,1,0:T(8,128)} custom-call(f32[16,1,2,24,256]{4,3,2,1,0:T(8,128)} %copy-done.13, f32[16,1,2,24,256]{4,3,2,1,0:T(8,128)} %copy-done.18, f32[16,1,2,24,256]{4,3,2,1,0:T(8,128)} %copy-done.16, f32[2,2,24,256]{3,2,1,0:T(8,128)} %bitcast.14, f32[4,24,256]{2,1,0:T(8,128)} %broadcast_in_dim.8.spread_ref), custom_call_target="tpu_custom_call" | custom-call | flops 5111808 | bytes 3145728 | tf_op jit(solution)/shard_map/pallas_call | solution.py:47
  35.8 0.9 collective-permute-start.15
  36.7 3.5 %collective-permute-done.8.below_ref = f32[16,1,2,24,256]{4,3,2,1,0:T(8,128)} collective-permute-done((f32[16,1,2,24,256]{4,3,2,1,0:T(8,128)S(1)}, f32[16,1,2,24,256]{4,3,2,1,0:T(8,128)}, u32[]{:S(2)}, u32[]{:S(2)}) %collective-permute-start.8) | collective-permute-done | bytes 786464 | tf_op jit(solution)/shard_map/ppermute | solution.py:325
  40.2 3.2 %shard_map.104.cells_ref = f32[16,1,2,24,256]{4,3,2,1,0:T(8,128)} custom-call(f32[16,1,2,24,256]{4,3,2,1,0:T(8,128)} %copy-done.12, f32[16,1,2,24,256]{4,3,2,1,0:T(8,128)} %collective-permute-done.8.below_ref, f32[16,1,2,24,256]{4,3,2,1,0:T(8,128)} %collective-permute-done.9.above_ref, f32[2,2,24,256]{3,2,1,0:T(8,128)} %bitcast.15, ...), custom_call_target="tpu_custom_call" | custom-call | flops 5111808 | bytes 3145728 | tf_op jit(solution)/shard_map/pallas_call | solution.py:47
  43.4 1.6 collective-permute-start.11
  44.9 1.6 collective-permute-done.15.above_ref
  46.5 5.2 %collective-permute-done.14.below_ref = f32[16,1,2,24,256]{4,3,2,1,0:T(8,128)} collective-permute-done((f32[16,1,2,24,256]{4,3,2,1,0:T(8,128)}, f32[16,1,2,24,256]{4,3,2,1,0:T(8,128)}, u32[]{:S(2)}, u32[]{:S(2)}) %collective-permute-start.14) | collective-permute-done | bytes 786464 | tf_op jit(solution)/shard_map/ppermute | solution.py:329
  51.7 3.2 %shard_map.106.refs_0_ = f32[16,2,2,24,256]{4,3,2,1,0:T(8,128)} custom-call(f32[16,1,2,24,256]{4,3,2,1,0:T(8,128)} %shard_map.105.cells_ref, f32[16,1,2,24,256]{4,3,2,1,0:T(8,128)} %collective-permute-done.14.below_ref, f32[16,1,2,24,256]{4,3,2,1,0:T(8,128)} %copy-done.19, f32[2,2,24,256]{3,2,1,0:T(8,128)} %bitcast.16, f32[4,24,256]{2,1,0:T(8,128)} %broadcast_in_dim.8.spread_ref), custom_call_target="tpu_custom_call" | custom-call | flops 5111808 | bytes 3145728 | tf_op jit(solution)/shard_map/pallas_call | solution.py:47
  54.9 5.2 %collective-permute-done.10.below_ref = f32[16,1,2,24,256]{4,3,2,1,0:T(8,128)} collective-permute-done((f32[16,1,2,24,256]{4,3,2,1,0:T(8,128)}, f32[16,1,2,24,256]{4,3,2,1,0:T(8,128)}, u32[]{:S(2)}, u32[]{:S(2)}) %collective-permute-start.10) | collective-permute-done | bytes 786464 | tf_op jit(solution)/shard_map/ppermute | solution.py:329
  60.2 3.1 %shard_map.107.refs_1_ = f32[16,2,2,24,256]{4,3,2,1,0:T(8,128)} custom-call(f32[16,1,2,24,256]{4,3,2,1,0:T(8,128)} %shard_map.104.cells_ref, f32[16,1,2,24,256]{4,3,2,1,0:T(8,128)} %collective-permute-done.10.below_ref, f32[16,1,2,24,256]{4,3,2,1,0:T(8,128)} %copy-done.22, f32[2,2,24,256]{3,2,1,0:T(8,128)} %bitcast.17, ...), custom_call_target="tpu_custom_call", output_to_operand_aliasing={{}: (5, {})} | custom-call | flops 5111808 | bytes 3145728 | tf_op jit(solution)/shard_map/pallas_call | solution.py:47
  63.4 0.8 collective-permute-start.5
  64.2 5.1 %collective-permute-start.1 = (f32[16,1,2,24,256]{4,3,2,1,0:T(8,128)S(1)}, f32[16,1,2,24,256]{4,3,2,1,0:T(8,128)S(1)}, u32[]{:S(2)}, u32[]{:S(2)}) collective-permute-start(f32[16,1,2,24,256]{4,3,2,1,0:T(8,128)S(1)} %get-tuple-element.12.cells_ref), channel_id=1, source_target_pairs={{4,0},{8,4},{12,8},{16,12},{20,16},{24,20},{28,24},{32,28},{36,32}... | collective-permute-start | bytes 2359304 | tf_op jit(solution)/shard_map/ppermute | solution.py:326
  69.3 4.4 %collective-permute-done.5.above_ref = f32[16,1,2,24,256]{4,3,2,1,0:T(8,128)S(1)} collective-permute-done((f32[16,1,2,24,256]{4,3,2,1,0:T(8,128)S(1)}, f32[16,1,2,24,256]{4,3,2,1,0:T(8,128)S(1)}, u32[]{:S(2)}, u32[]{:S(2)}) %collective-permute-start.5) | collective-permute-done | bytes 786464 | tf_op jit(solution)/shard_map/ppermute | solution.py:326
  73.7 0.9 copy-done.17
  74.6 4.4 %collective-permute-done.4.below_ref = f32[16,1,2,24,256]{4,3,2,1,0:T(8,128)} collective-permute-done((f32[16,1,2,24,256]{4,3,2,1,0:T(8,128)S(1)}, f32[16,1,2,24,256]{4,3,2,1,0:T(8,128)}, u32[]{:S(2)}, u32[]{:S(2)}) %collective-permute-start.4) | collective-permute-done | bytes 786464 | tf_op jit(solution)/shard_map/ppermute | solution.py:325
  79.1 3.2 %shard_map.101.cells_ref = f32[16,1,2,24,256]{4,3,2,1,0:T(8,128)} custom-call(f32[16,1,2,24,256]{4,3,2,1,0:T(8,128)} %copy-done.11, f32[16,1,2,24,256]{4,3,2,1,0:T(8,128)} %collective-permute-done.4.below_ref, f32[16,1,2,24,256]{4,3,2,1,0:T(8,128)} %copy-done.17, f32[2,2,24,256]{3,2,1,0:T(8,128)} %bitcast.18, f32[4,24,256]{2,1,0:T(8,128)} %broadcast_in_dim.8.spread_ref), custom_call_target="tpu_custom_call" | custom-call | flops 5111808 | bytes 3145728 | tf_op jit(solution)/shard_map/pallas_call | solution.py:47
  83.1 4.3 %collective-permute-done.below_ref = f32[16,1,2,24,256]{4,3,2,1,0:T(8,128)S(1)} collective-permute-done((f32[16,1,2,24,256]{4,3,2,1,0:T(8,128)S(1)}, f32[16,1,2,24,256]{4,3,2,1,0:T(8,128)S(1)}, u32[]{:S(2)}, u32[]{:S(2)}) %collective-permute-start) | collective-permute-done | bytes 786464 | tf_op jit(solution)/shard_map/ppermute | solution.py:325
  87.4 0.9 copy-done.15
  88.3 3.2 %shard_map.100.cells_ref = f32[16,1,2,24,256]{4,3,2,1,0:T(8,128)} custom-call(f32[16,1,2,24,256]{4,3,2,1,0:T(8,128)} %copy-done.10, f32[16,1,2,24,256]{4,3,2,1,0:T(8,128)} %copy-done.15, f32[16,1,2,24,256]{4,3,2,1,0:T(8,128)} %copy-done.14, f32[2,2,24,256]{3,2,1,0:T(8,128)} %bitcast.19, f32[4,24,256]{2,1,0:T(8,128)} %broadcast_in_dim.8.spread_ref), custom_call_target="tpu_custom_call" | custom-call | flops 5111808 | bytes 3145728 | tf_op jit(solution)/shard_map/pallas_call | solution.py:47
  91.4 1.6 collective-permute-start.3
  93.1 5.0 %collective-permute-done.6.below_ref = f32[16,1,2,24,256]{4,3,2,1,0:T(8,128)} collective-permute-done((f32[16,1,2,24,256]{4,3,2,1,0:T(8,128)}, f32[16,1,2,24,256]{4,3,2,1,0:T(8,128)}, u32[]{:S(2)}, u32[]{:S(2)}) %collective-permute-start.6) | collective-permute-done | bytes 786464 | tf_op jit(solution)/shard_map/ppermute | solution.py:329
  98.1 3.1 %shard_map.102.refs_0_ = f32[16,2,2,24,256]{4,3,2,1,0:T(8,128)} custom-call(f32[16,1,2,24,256]{4,3,2,1,0:T(8,128)} %shard_map.101.cells_ref, f32[16,1,2,24,256]{4,3,2,1,0:T(8,128)} %collective-permute-done.6.below_ref, f32[16,1,2,24,256]{4,3,2,1,0:T(8,128)} %copy-done.20, f32[2,2,24,256]{3,2,1,0:T(8,128)} %bitcast.20, f32[4,24,256]{2,1,0:T(8,128)} %broadcast_in_dim.8.spread_ref), custom_call_target="tpu_custom_call" | custom-call | flops 5111808 | bytes 3145728 | tf_op jit(solution)/shard_map/pallas_call | solution.py:47
  101.3 1.6 collective-permute-done.3.above_ref
  102.9 5.1 %collective-permute-done.2.below_ref = f32[16,1,2,24,256]{4,3,2,1,0:T(8,128)S(1)} collective-permute-done((f32[16,1,2,24,256]{4,3,2,1,0:T(8,128)}, f32[16,1,2,24,256]{4,3,2,1,0:T(8,128)S(1)}, u32[]{:S(2)}, u32[]{:S(2)}) %collective-permute-start.2) | collective-permute-done | bytes 786464 | tf_op jit(solution)/shard_map/ppermute | solution.py:329
  108.0 1.0 copy-done.23
  109.0 3.2 %shard_map.103.refs_0_ = f32[16,2,2,24,256]{4,3,2,1,0:T(8,128)} custom-call(f32[16,1,2,24,256]{4,3,2,1,0:T(8,128)} %shard_map.100.cells_ref, f32[16,1,2,24,256]{4,3,2,1,0:T(8,128)} %copy-done.23, f32[16,1,2,24,256]{4,3,2,1,0:T(8,128)} %copy-done.21, f32[2,2,24,256]{3,2,1,0:T(8,128)} %bitcast.21, ...), custom_call_target="tpu_custom_call", output_to_operand_aliasing={{}: (5, {})} | custom-call | flops 5111808 | bytes 3145728 | tf_op jit(solution)/shard_map/pallas_call | solution.py:47
  112.3 1.4 copy-done.1
  113.7 4.8 %shard_map.108 = f32[16,256]{1,0:T(8,128)S(1)} custom-call(s32[1]{0:T(128)} %bitcast.tile_ref, s32[256]{0:T(256)S(1)} %copy-done.4, s32[256]{0:T(256)S(1)} %copy-done.6, s32[256]{0:T(256)S(1)} %copy-done.7, s32[256]{0:T(256)S(1)} %copy-done.8, f32[16,2,2,24,256]{4,3,2,1,0:T(8,128)S(1)} %copy-done.1, f32[16,2,2,24,256]{4,3,2,1,0:T(8,128)S(1)} %copy-done.2), custom_call_target="tpu_custom_call" | custom-call | tf_op jit(solution)/shard_map/pallas_call | solution.py:103
  118.5 1.2 collective-permute-done.16
  119.7 3.7 %collective-permute-done.17 = f32[16,256]{1,0:T(8,128)S(1)} collective-permute-done((f32[16,256]{1,0:T(8,128)S(1)}, f32[16,256]{1,0:T(8,128)S(1)}, u32[]{:S(2)}, u32[]{:S(2)}) %collective-permute-start.17) | collective-permute-done | bytes 16416 | tf_op jit(solution)/shard_map/ppermute | solution.py:290
  123.5 4.6 %collective-permute-done.18 = f32[16,256]{1,0:T(8,128)S(1)} collective-permute-done((f32[16,256]{1,0:T(8,128)S(1)}, f32[16,256]{1,0:T(8,128)S(1)}, u32[]{:S(2)}, u32[]{:S(2)}) %collective-permute-start.18) | collective-permute-done | bytes 16416 | tf_op jit(solution)/shard_map/ppermute | solution.py:290
  128.5 7.3 %collective-permute-done.19 = f32[16,256]{1,0:T(8,128)S(1)} collective-permute-done((f32[16,256]{1,0:T(8,128)S(1)}, f32[16,256]{1,0:T(8,128)S(1)}, u32[]{:S(2)}, u32[]{:S(2)}) %collective-permute-start.19) | collective-permute-done | bytes 16416 | tf_op jit(solution)/shard_map/ppermute | solution.py:290
  135.9 3.6 %collective-permute-done.20 = f32[16,256]{1,0:T(8,128)S(1)} collective-permute-done((f32[16,256]{1,0:T(8,128)S(1)}, f32[16,256]{1,0:T(8,128)S(1)}, u32[]{:S(2)}, u32[]{:S(2)}) %collective-permute-start.20) | collective-permute-done | bytes 16416 | tf_op jit(solution)/shard_map/ppermute | solution.py:290
  139.7 5.1 %collective-permute-done.21 = f32[16,256]{1,0:T(8,128)S(1)} collective-permute-done((f32[16,256]{1,0:T(8,128)S(1)}, f32[16,256]{1,0:T(8,128)S(1)}, u32[]{:S(2)}, u32[]{:S(2)}) %collective-permute-start.21) | collective-permute-done | bytes 16416 | tf_op jit(solution)/shard_map/ppermute | solution.py:290
  145.4 2.3 %collective-permute-start.23 = (f32[16,256]{1,0:T(8,128)S(1)}, f32[16,256]{1,0:T(8,128)S(1)}, u32[]{:S(2)}, u32[]{:S(2)}) collective-permute-start(f32[16,256]{1,0:T(8,128)S(1)} %add.31.raw_0), channel_id=1, source_target_pairs={{0,2},{1,3},{2,0},{3,1},{4,6},{5,7},{6,4},{7,5},{8,10},{9,11},{10,... | collective-permute-start | bytes 49160 | tf_op jit(solution)/shard_map/ppermute | solution.py:337
  147.7 1.8 collective-permute-start.22
  149.5 1.5 collective-permute-done.23.raw_2
  151.7 26.9 %shard_map.109 = (bf16[128,512]{1,0:T(8,128)(2,1)S(1)}, bf16[128,512]{1,0:T(8,128)(2,1)S(1)}) custom-call(f32[256]{0:T(256)S(1)} %copy-done.9, f32[256]{0:T(256)S(1)} %copy-done.5, f32[256]{0:T(256)S(1)} %sqrt.3.root_ref, f32[16,256]{1,0:T(8,128)S(1)} %add.31.raw_0, f32[16,256]{1,0:T(8,128)S(1)} %collective-permute-done.22.raw_1, ...), custom_call_target="tpu_custom_call" | custom-call | tf_op jit(solution)/shard_map/pallas_call | solution.py:225
  178.6 17.8 %all-gather.3.cloned.1.call-done.refs_0_ = f32[64,2,2,24,256]{4,3,2,1,0:T(8,128)} async-done(((f32[16,2,2,24,256]{4,3,2,1,0:T(8,128)}), f32[64,2,2,24,256]{4,3,2,1,0:T(8,128)}) %all-gather.3.cloned.1.call-update) | async-done | bytes 6291472 | tf_op jit(solution)/shard_map/all_gather | solution.py:333
  196.4 2.8 %copy-done.3 = f32[64,2,2,24,256]{4,3,2,1,0:T(8,128)S(1)} copy-done((f32[64,2,2,24,256]{4,3,2,1,0:T(8,128)S(1)}, f32[64,2,2,24,256]{4,3,2,1,0:T(8,128)}, u32[]{:S(2)}) %copy-start.3) | copy-done | bytes 6291480
  199.2 5.8 %shard_map.110 = f32[16,4,2,24,256]{4,3,2,1,0:T(8,128)S(1)} custom-call(s32[4]{0:T(128)S(1)} %compare_select_fusion.order_ref, bf16[128,512]{1,0:T(8,128)(2,1)S(1)} %get-tuple-element.7.high_ref, bf16[128,512]{1,0:T(8,128)(2,1)S(1)} %get-tuple-element.8.low_ref, f32[64,2,2,24,256]{4,3,2,1,0:T(8,128)S(1)} %copy-done.3, ...), custom_call_target="tpu_custom_call" | custom-call | tf_op jit(solution)/shard_map/pallas_call | solution.py:278
  205.0 3.5 %copy.20 = f32[16,4,24,2,256]{4,3,2,1,0:T(2,128)} copy(f32[16,4,24,2,256]{4,2,3,1,0:T(8,128)S(1)} %bitcast.12) | data formatting | bytes 6291456 | tf_op jit(solution)/shard_map/transpose | solution.py:341
  (91 shorter events, 4.2 us)
Async XLA Ops:
  6.5 121.6 %copy-start = (f32[64,256]{1,0:T(8,128)S(1)}, f32[64,256]{1,0:T(8,128)}, u32[]{:S(2)}) copy-start(f32[64,256]{1,0:T(8,128)} %param.19) | copy-start | bytes 196612
  6.5 172.1 %all-gather.5.cloned.1.call-start = ((), (), s32[]{:S(2)}) async-start(), calls=%async_computation.1 | async-start | bytes 7864320 | tf_op jit(solution)/shard_map/all_gather | solution.py:333
  8.8 13.2 %copy-start.24 = (f32[2,24,2,256]{3,2,1,0:T(2,128)S(1)}, f32[2,24,2,256]{3,2,1,0:T(2,128)}, u32[]{:S(2)}) copy-start(f32[2,24,2,256]{3,2,1,0:T(2,128)} %param.11) | copy-start | bytes 294916
  8.8 22.9 %copy-start.25 = (f32[4,24]{1,0:T(4,128)S(1)}, f32[4,24]{1,0:T(4,128)}, u32[]{:S(2)}) copy-start(f32[4,24]{1,0:T(4,128)} %param.12) | copy-start | bytes 1156
  9.1 23.6 %copy-start.13 = (f32[16,1,2,24,256]{4,3,2,1,0:T(8,128)}, f32[16,1,2,24,256]{4,3,2,1,0:T(8,128)S(1)}, u32[]{:S(2)}) copy-start(f32[16,1,2,24,256]{4,3,2,1,0:T(8,128)S(1)} %get-tuple-element.9.cells_ref) | copy-start | bytes 2359300
  9.1 31.1 %copy-start.12 = (f32[16,1,2,24,256]{4,3,2,1,0:T(8,128)}, f32[16,1,2,24,256]{4,3,2,1,0:T(8,128)S(1)}, u32[]{:S(2)}) copy-start(f32[16,1,2,24,256]{4,3,2,1,0:T(8,128)S(1)} %get-tuple-element.10.cells_ref) | copy-start | bytes 2359300
  9.1 55.1 %copy-start.11 = (f32[16,1,2,24,256]{4,3,2,1,0:T(8,128)}, f32[16,1,2,24,256]{4,3,2,1,0:T(8,128)S(1)}, u32[]{:S(2)}) copy-start(f32[16,1,2,24,256]{4,3,2,1,0:T(8,128)S(1)} %get-tuple-element.11.cells_ref) | copy-start | bytes 2359300
  9.1 60.2 %copy-start.10 = (f32[16,1,2,24,256]{4,3,2,1,0:T(8,128)}, f32[16,1,2,24,256]{4,3,2,1,0:T(8,128)S(1)}, u32[]{:S(2)}) copy-start(f32[16,1,2,24,256]{4,3,2,1,0:T(8,128)S(1)} %get-tuple-element.12.cells_ref) | copy-start | bytes 2359300
  9.1 17.3 %collective-permute-start.13 = (f32[16,1,2,24,256]{4,3,2,1,0:T(8,128)S(1)}, f32[16,1,2,24,256]{4,3,2,1,0:T(8,128)S(1)}, u32[]{:S(2)}, u32[]{:S(2)}) collective-permute-start(f32[16,1,2,24,256]{4,3,2,1,0:T(8,128)S(1)} %get-tuple-element.9.cells_ref), channel_id=1, source_target_pairs={{4,0},{8,4},{12,8},{16,12},{20,16},{24,20},{28,24},{32,28},{36,32}... | collective-permute-start | bytes 2359304 | tf_op jit(solution)/shard_map/ppermute | solution.py:326
  16.9 14.7 %collective-permute-start.12 = (f32[16,1,2,24,256]{4,3,2,1,0:T(8,128)S(1)}, f32[16,1,2,24,256]{4,3,2,1,0:T(8,128)S(1)}, u32[]{:S(2)}, u32[]{:S(2)}) collective-permute-start(f32[16,1,2,24,256]{4,3,2,1,0:T(8,128)S(1)} %get-tuple-element.9.cells_ref), channel_id=1, source_target_pairs={{0,4},{4,8},{8,12},{12,16},{16,20},{20,24},{24,28},{28,32},{32,36}... | collective-permute-start | bytes 2359304 | tf_op jit(solution)/shard_map/ppermute | solution.py:325
  16.9 19.7 %collective-permute-start.9 = (f32[16,1,2,24,256]{4,3,2,1,0:T(8,128)S(1)}, f32[16,1,2,24,256]{4,3,2,1,0:T(8,128)}, u32[]{:S(2)}, u32[]{:S(2)}) collective-permute-start(f32[16,1,2,24,256]{4,3,2,1,0:T(8,128)S(1)} %get-tuple-element.10.cells_ref), channel_id=1, source_target_pairs={{4,0},{8,4},{12,8},{16,12},{20,16},{24,20},{28,24},{32,28},{36,32}... | collective-permute-start | bytes 2359304 | tf_op jit(solution)/shard_map/ppermute | solution.py:326
  22.0 18.2 %collective-permute-start.8 = (f32[16,1,2,24,256]{4,3,2,1,0:T(8,128)S(1)}, f32[16,1,2,24,256]{4,3,2,1,0:T(8,128)}, u32[]{:S(2)}, u32[]{:S(2)}) collective-permute-start(f32[16,1,2,24,256]{4,3,2,1,0:T(8,128)S(1)} %get-tuple-element.10.cells_ref), channel_id=1, source_target_pairs={{0,4},{4,8},{8,12},{12,16},{16,20},{20,24},{24,28},{28,32},{32,36}... | collective-permute-start | bytes 2359304 | tf_op jit(solution)/shard_map/ppermute | solution.py:325
  26.5 5.2 %copy-start.16 = (f32[16,1,2,24,256]{4,3,2,1,0:T(8,128)}, f32[16,1,2,24,256]{4,3,2,1,0:T(8,128)S(1)}, u32[]{:S(2)}) copy-start(f32[16,1,2,24,256]{4,3,2,1,0:T(8,128)S(1)} %collective-permute-done.13.above_ref) | copy-start | bytes 2359300
  35.8 10.7 %collective-permute-start.15 = (f32[16,1,2,24,256]{4,3,2,1,0:T(8,128)}, f32[16,1,2,24,256]{4,3,2,1,0:T(8,128)S(1)}, u32[]{:S(2)}, u32[]{:S(2)}) collective-permute-start(f32[16,1,2,24,256]{4,3,2,1,0:T(8,128)} %shard_map.105.cells_ref), channel_id=1, source_target_pairs={{4,0},{8,4},{12,8},{16,12},{20,16},{24,20},{28,24},{32,28},{36,32}... | collective-permute-start | bytes 2359304 | tf_op jit(solution)/shard_map/ppermute | solution.py:330
  36.7 15.1 %collective-permute-start.14 = (f32[16,1,2,24,256]{4,3,2,1,0:T(8,128)}, f32[16,1,2,24,256]{4,3,2,1,0:T(8,128)}, u32[]{:S(2)}, u32[]{:S(2)}) collective-permute-start(f32[16,1,2,24,256]{4,3,2,1,0:T(8,128)} %shard_map.105.cells_ref), channel_id=1, source_target_pairs={{0,4},{4,8},{8,12},{12,16},{16,20},{20,24},{24,28},{28,32},{32,36}... | collective-permute-start | bytes 2359304 | tf_op jit(solution)/shard_map/ppermute | solution.py:329
  43.4 11.6 %collective-permute-start.11 = (f32[16,1,2,24,256]{4,3,2,1,0:T(8,128)}, f32[16,1,2,24,256]{4,3,2,1,0:T(8,128)S(1)}, u32[]{:S(2)}, u32[]{:S(2)}) collective-permute-start(f32[16,1,2,24,256]{4,3,2,1,0:T(8,128)} %shard_map.104.cells_ref), channel_id=1, source_target_pairs={{4,0},{8,4},{12,8},{16,12},{20,16},{24,20},{28,24},{32,28},{36,32}... | collective-permute-start | bytes 2359304 | tf_op jit(solution)/shard_map/ppermute | solution.py:330
  44.9 15.2 %collective-permute-start.10 = (f32[16,1,2,24,256]{4,3,2,1,0:T(8,128)}, f32[16,1,2,24,256]{4,3,2,1,0:T(8,128)}, u32[]{:S(2)}, u32[]{:S(2)}) collective-permute-start(f32[16,1,2,24,256]{4,3,2,1,0:T(8,128)} %shard_map.104.cells_ref), channel_id=1, source_target_pairs={{0,4},{4,8},{8,12},{12,16},{16,20},{20,24},{24,28},{28,32},{32,36}... | collective-permute-start | bytes 2359304 | tf_op jit(solution)/shard_map/ppermute | solution.py:329
  46.5 5.2 %copy-start.19 = (f32[16,1,2,24,256]{4,3,2,1,0:T(8,128)}, f32[16,1,2,24,256]{4,3,2,1,0:T(8,128)S(1)}, u32[]{:S(2)}) copy-start(f32[16,1,2,24,256]{4,3,2,1,0:T(8,128)S(1)} %collective-permute-done.15.above_ref) | copy-start | bytes 2359300
  54.9 5.2 %copy-start.22 = (f32[16,1,2,24,256]{4,3,2,1,0:T(8,128)}, f32[16,1,2,24,256]{4,3,2,1,0:T(8,128)S(1)}, u32[]{:S(2)}) copy-start(f32[16,1,2,24,256]{4,3,2,1,0:T(8,128)S(1)} %collective-permute-done.11.above_ref) | copy-start | bytes 2359300
  63.3 133.1 %all-gather.3.cloned.1.call-start = ((), (), s32[]{:S(2)}) async-start(), calls=%async_computation | async-start | bytes 7864320 | tf_op jit(solution)/shard_map/all_gather | solution.py:333
  63.4 10.3 %collective-permute-start.5 = (f32[16,1,2,24,256]{4,3,2,1,0:T(8,128)S(1)}, f32[16,1,2,24,256]{4,3,2,1,0:T(8,128)S(1)}, u32[]{:S(2)}, u32[]{:S(2)}) collective-permute-start(f32[16,1,2,24,256]{4,3,2,1,0:T(8,128)S(1)} %get-tuple-element.11.cells_ref), channel_id=1, source_target_pairs={{4,0},{8,4},{12,8},{16,12},{20,16},{24,20},{28,24},{32,28},{36,32}... | collective-permute-start | bytes 2359304 | tf_op jit(solution)/shard_map/ppermute | solution.py:326
  64.2 14.8 %collective-permute-start.4 = (f32[16,1,2,24,256]{4,3,2,1,0:T(8,128)S(1)}, f32[16,1,2,24,256]{4,3,2,1,0:T(8,128)}, u32[]{:S(2)}, u32[]{:S(2)}) collective-permute-start(f32[16,1,2,24,256]{4,3,2,1,0:T(8,128)S(1)} %get-tuple-element.11.cells_ref), channel_id=1, source_target_pairs={{0,4},{4,8},{8,12},{12,16},{16,20},{20,24},{24,28},{28,32},{32,36}... | collective-permute-start | bytes 2359304 | tf_op jit(solution)/shard_map/ppermute | solution.py:325
  64.2 18.8 %collective-permute-start.1 = (f32[16,1,2,24,256]{4,3,2,1,0:T(8,128)S(1)}, f32[16,1,2,24,256]{4,3,2,1,0:T(8,128)S(1)}, u32[]{:S(2)}, u32[]{:S(2)}) collective-permute-start(f32[16,1,2,24,256]{4,3,2,1,0:T(8,128)S(1)} %get-tuple-element.12.cells_ref), channel_id=1, source_target_pairs={{4,0},{8,4},{12,8},{16,12},{20,16},{24,20},{28,24},{32,28},{36,32}... | collective-permute-start | bytes 2359304 | tf_op jit(solution)/shard_map/ppermute | solution.py:326
  69.3 18.1 %collective-permute-start = (f32[16,1,2,24,256]{4,3,2,1,0:T(8,128)S(1)}, f32[16,1,2,24,256]{4,3,2,1,0:T(8,128)S(1)}, u32[]{:S(2)}, u32[]{:S(2)}) collective-permute-start(f32[16,1,2,24,256]{4,3,2,1,0:T(8,128)S(1)} %get-tuple-element.12.cells_ref), channel_id=1, source_target_pairs={{0,4},{4,8},{8,12},{12,16},{16,20},{20,24},{24,28},{28,32},{32,36}... | collective-permute-start | bytes 2359304 | tf_op jit(solution)/shard_map/ppermute | solution.py:325
  82.3 10.8 %collective-permute-start.7 = (f32[16,1,2,24,256]{4,3,2,1,0:T(8,128)}, f32[16,1,2,24,256]{4,3,2,1,0:T(8,128)S(1)}, u32[]{:S(2)}, u32[]{:S(2)}) collective-permute-start(f32[16,1,2,24,256]{4,3,2,1,0:T(8,128)} %shard_map.101.cells_ref), channel_id=1, source_target_pairs={{4,0},{8,4},{12,8},{16,12},{20,16},{24,20},{28,24},{32,28},{36,32}... | collective-permute-start | bytes 2359304 | tf_op jit(solution)/shard_map/ppermute | solution.py:330
  83.1 15.1 %collective-permute-start.6 = (f32[16,1,2,24,256]{4,3,2,1,0:T(8,128)}, f32[16,1,2,24,256]{4,3,2,1,0:T(8,128)}, u32[]{:S(2)}, u32[]{:S(2)}) collective-permute-start(f32[16,1,2,24,256]{4,3,2,1,0:T(8,128)} %shard_map.101.cells_ref), channel_id=1, source_target_pairs={{0,4},{4,8},{8,12},{12,16},{16,20},{20,24},{24,28},{28,32},{32,36}... | collective-permute-start | bytes 2359304 | tf_op jit(solution)/shard_map/ppermute | solution.py:329
  83.1 4.3 %copy-start.14 = (f32[16,1,2,24,256]{4,3,2,1,0:T(8,128)}, f32[16,1,2,24,256]{4,3,2,1,0:T(8,128)S(1)}, u32[]{:S(2)}) copy-start(f32[16,1,2,24,256]{4,3,2,1,0:T(8,128)S(1)} %collective-permute-done.1.above_ref) | copy-start | bytes 2359300
  91.4 11.5 %collective-permute-start.3 = (f32[16,1,2,24,256]{4,3,2,1,0:T(8,128)}, f32[16,1,2,24,256]{4,3,2,1,0:T(8,128)S(1)}, u32[]{:S(2)}, u32[]{:S(2)}) collective-permute-start(f32[16,1,2,24,256]{4,3,2,1,0:T(8,128)} %shard_map.100.cells_ref), channel_id=1, source_target_pairs={{4,0},{8,4},{12,8},{16,12},{20,16},{24,20},{28,24},{32,28},{36,32}... | collective-permute-start | bytes 2359304 | tf_op jit(solution)/shard_map/ppermute | solution.py:330
  93.1 14.9 %collective-permute-start.2 = (f32[16,1,2,24,256]{4,3,2,1,0:T(8,128)}, f32[16,1,2,24,256]{4,3,2,1,0:T(8,128)S(1)}, u32[]{:S(2)}, u32[]{:S(2)}) collective-permute-start(f32[16,1,2,24,256]{4,3,2,1,0:T(8,128)} %shard_map.100.cells_ref), channel_id=1, source_target_pairs={{0,4},{4,8},{8,12},{12,16},{16,20},{20,24},{24,28},{28,32},{32,36}... | collective-permute-start | bytes 2359304 | tf_op jit(solution)/shard_map/ppermute | solution.py:329
  93.1 5.0 %copy-start.20 = (f32[16,1,2,24,256]{4,3,2,1,0:T(8,128)}, f32[16,1,2,24,256]{4,3,2,1,0:T(8,128)S(1)}, u32[]{:S(2)}) copy-start(f32[16,1,2,24,256]{4,3,2,1,0:T(8,128)S(1)} %collective-permute-done.7.above_ref) | copy-start | bytes 2359300
  101.3 11.0 %copy-start.2 = (f32[16,2,2,24,256]{4,3,2,1,0:T(8,128)S(1)}, f32[16,2,2,24,256]{4,3,2,1,0:T(8,128)}, u32[]{:S(2)}) copy-start(f32[16,2,2,24,256]{4,3,2,1,0:T(8,128)} %shard_map.107.refs_1_) | copy-start | bytes 4718596
  101.3 11.0 %copy-start.4 = (s32[256]{0:T(256)S(1)}, s32[256]{0:T(256)}, u32[]{:S(2)}) copy-start(s32[256]{0:T(256)} %row_ref.1) | copy-start | bytes 3076
  101.3 11.0 %copy-start.6 = (s32[256]{0:T(256)S(1)}, s32[256]{0:T(256)}, u32[]{:S(2)}) copy-start(s32[256]{0:T(256)} %column_ref.1) | copy-start | bytes 3076
  101.3 11.0 %copy-start.7 = (s32[256]{0:T(256)S(1)}, s32[256]{0:T(256)}, u32[]{:S(2)}) copy-start(s32[256]{0:T(256)} %field_ref.1) | copy-start | bytes 3076
  101.3 11.0 %copy-start.8 = (s32[256]{0:T(256)S(1)}, s32[256]{0:T(256)}, u32[]{:S(2)}) copy-start(s32[256]{0:T(256)} %level_ref.1) | copy-start | bytes 3076
  102.9 5.1 %copy-start.21 = (f32[16,1,2,24,256]{4,3,2,1,0:T(8,128)}, f32[16,1,2,24,256]{4,3,2,1,0:T(8,128)S(1)}, u32[]{:S(2)}) copy-start(f32[16,1,2,24,256]{4,3,2,1,0:T(8,128)S(1)} %collective-permute-done.3.above_ref) | copy-start | bytes 2359300
  112.2 37.3 %copy-start.5 = (f32[256]{0:T(256)S(1)}, f32[256]{0:T(256)}, u32[]{:S(2)}) copy-start(f32[256]{0:T(256)} %err_ref.1) | copy-start | bytes 3076
  112.2 39.5 %copy-start.9 = (f32[256]{0:T(256)S(1)}, f32[256]{0:T(256)}, u32[]{:S(2)}) copy-start(f32[256]{0:T(256)} %obs_ref.1) | copy-start | bytes 3076
  118.5 1.2 collective-permute-start.16
  119.7 3.7 %collective-permute-start.17 = (f32[16,256]{1,0:T(8,128)S(1)}, f32[16,256]{1,0:T(8,128)S(1)}, u32[]{:S(2)}, u32[]{:S(2)}) collective-permute-start(f32[16,256]{1,0:T(8,128)S(1)} %add.26), channel_id=1, source_target_pairs={{0,8},{4,12},{8,0},{12,4},{16,24},{20,28},{24,16},{28,20},{32,40},... | collective-permute-start | bytes 49160 | tf_op jit(solution)/shard_map/ppermute | solution.py:290
  123.5 4.6 %collective-permute-start.18 = (f32[16,256]{1,0:T(8,128)S(1)}, f32[16,256]{1,0:T(8,128)S(1)}, u32[]{:S(2)}, u32[]{:S(2)}) collective-permute-start(f32[16,256]{1,0:T(8,128)S(1)} %add.27), channel_id=1, source_target_pairs={{0,16},{4,20},{8,24},{12,28},{16,0},{20,4},{24,8},{28,12},{32,48},... | collective-permute-start | bytes 49160 | tf_op jit(solution)/shard_map/ppermute | solution.py:290
  128.1 7.6 %collective-permute-start.19 = (f32[16,256]{1,0:T(8,128)S(1)}, f32[16,256]{1,0:T(8,128)S(1)}, u32[]{:S(2)}, u32[]{:S(2)}) collective-permute-start(f32[16,256]{1,0:T(8,128)S(1)} %add.28), channel_id=1, source_target_pairs={{0,32},{4,36},{8,40},{12,44},{16,48},{20,52},{24,56},{28,60},{32,0... | collective-permute-start | bytes 49160 | tf_op jit(solution)/shard_map/ppermute | solution.py:290
  135.8 3.7 %collective-permute-start.20 = (f32[16,256]{1,0:T(8,128)S(1)}, f32[16,256]{1,0:T(8,128)S(1)}, u32[]{:S(2)}, u32[]{:S(2)}) collective-permute-start(f32[16,256]{1,0:T(8,128)S(1)} %add.29), channel_id=1, source_target_pairs={{0,64},{4,68},{8,72},{12,76},{16,80},{20,84},{24,88},{28,92},{32,9... | collective-permute-start | bytes 49160 | tf_op jit(solution)/shard_map/ppermute | solution.py:290
  139.5 5.2 %collective-permute-start.21 = (f32[16,256]{1,0:T(8,128)S(1)}, f32[16,256]{1,0:T(8,128)S(1)}, u32[]{:S(2)}, u32[]{:S(2)}) collective-permute-start(f32[16,256]{1,0:T(8,128)S(1)} %add.30), channel_id=1, source_target_pairs={{0,128},{4,132},{8,136},{12,140},{16,144},{20,148},{24,152},{28,15... | collective-permute-start | bytes 49160 | tf_op jit(solution)/shard_map/ppermute | solution.py:290
  144.8 4.8 %collective-permute-start.24 = (f32[16,256]{1,0:T(8,128)S(1)}, f32[16,256]{1,0:T(8,128)S(1)}, u32[]{:S(2)}, u32[]{:S(2)}) collective-permute-start(f32[16,256]{1,0:T(8,128)S(1)} %add.31.raw_0), channel_id=1, source_target_pairs={{0,3},{1,0},{2,1},{3,2},{4,7},{5,4},{6,5},{7,6},{8,11},{9,8},{10,9... | collective-permute-start | bytes 49160 | tf_op jit(solution)/shard_map/ppermute | solution.py:337
  145.4 5.6 %collective-permute-start.23 = (f32[16,256]{1,0:T(8,128)S(1)}, f32[16,256]{1,0:T(8,128)S(1)}, u32[]{:S(2)}, u32[]{:S(2)}) collective-permute-start(f32[16,256]{1,0:T(8,128)S(1)} %add.31.raw_0), channel_id=1, source_target_pairs={{0,2},{1,3},{2,0},{3,1},{4,6},{5,7},{6,4},{7,5},{8,10},{9,11},{10,... | collective-permute-start | bytes 49160 | tf_op jit(solution)/shard_map/ppermute | solution.py:337
  147.7 4.1 %collective-permute-start.22 = (f32[16,256]{1,0:T(8,128)S(1)}, f32[16,256]{1,0:T(8,128)S(1)}, u32[]{:S(2)}, u32[]{:S(2)}) collective-permute-start(f32[16,256]{1,0:T(8,128)S(1)} %add.31.raw_0), channel_id=1, source_target_pairs={{0,1},{1,2},{2,3},{3,0},{4,5},{5,6},{6,7},{7,4},{8,9},{9,10},{10,1... | collective-permute-start | bytes 49160 | tf_op jit(solution)/shard_map/ppermute | solution.py:337
  196.4 2.8 %copy-start.3 = (f32[64,2,2,24,256]{4,3,2,1,0:T(8,128)S(1)}, f32[64,2,2,24,256]{4,3,2,1,0:T(8,128)}, u32[]{:S(2)}) copy-start(f32[64,2,2,24,256]{4,3,2,1,0:T(8,128)} %all-gather.3.cloned.1.call-done.refs_0_) | copy-start | bytes 18874372
  (5 other events, 5.1 us)
Sparse Core Ops, SparseCore 0:
  63.4 61.8 all-gather.4
  127.1 69.2 all-gather.2

commit v3 on v2

--- a/solution.py
+++ b/solution.py
@@ -18,7 +18,7 @@
     return lax.broadcasted_iota(jnp.int32, shape, dim)
 
 
-def step_kernel(cells_ref, below_ref, above_ref, courant_ref, spread_ref, *refs):
+def step_kernel(split, cells_ref, below_ref, above_ref, courant_ref, spread_ref, *refs):
     out_ref = refs[-1]
     width = cells_ref.shape[-1]
     spread = spread_ref[0]
@@ -30,24 +30,35 @@
         for member in range(cells_ref.shape[0]):
             rows = [ref[member, 0, i] for ref in (below_ref, cells_ref, above_ref) for i in range(2)]
             centre = rows[2 + r]
-            out_ref[member, 0, r] = (
+            value = (
                 (middle * centre + two * (rows[4 + r] - rows[r]))
                 + (up * rows[3 + r] + down * rows[1 + r])
                 + (right * pltpu.roll(centre, width - 1, 1) + left * pltpu.roll(centre, 1, 1))
                 + far * (pltpu.roll(centre, width - 2, 1) - pltpu.roll(centre, 2, 1))
             )
-
-
-def forecast_step(cells, below, above, courant, spread, field, into=None):
+            if split:
+                for half in range(2):
+                    out_ref[2 * r + half, member, 0] = value[:, half * (width // 2):(half + 1) * (width // 2)]
+            else:
+                out_ref[member, 0, r] = value
+
+
+def forecast_step(cells, below, above, courant, spread, field, into=None, split=False):
     count, _, rows, levels, width = below.shape
     part = 8
     block = pl.BlockSpec((part, 1, rows, levels, width), lambda m: (m, 0, 0, 0, 0))
     fields, place, sofar = into or (1, 0, None)
     more = [] if sofar is None else [sofar]
-    return pl.pallas_call(
-        step_kernel,
+    if split:
+        shape = (2 * rows, count, fields, levels, width // 2)
+        out_block = pl.BlockSpec((2 * rows, part, 1, levels, width // 2), lambda m: (0, m, place, 0, 0))
+    else:
+        shape = (count, fields, rows, levels, width)
+        out_block = pl.BlockSpec((part, 1, rows, levels, width), lambda m: (m, place, 0, 0, 0))
+    return pl.pallas_call(
+        functools.partial(step_kernel, split),
         grid=(count // part,),
-        out_shape=jax.ShapeDtypeStruct((count, fields, rows, levels, width), jnp.float32),
+        out_shape=jax.ShapeDtypeStruct(shape, jnp.float32),
         in_specs=[
             block,
             block,
@@ -55,66 +66,77 @@
             pl.BlockSpec((2, rows, levels, width), lambda m: (0, 0, 0, 0)),
             pl.BlockSpec((1, levels, width), lambda m: (field, 0, 0)),
         ] + [pl.BlockSpec(memory_space=pl.ANY) for _ in more],
-        out_specs=pl.BlockSpec((part, 1, rows, levels, width), lambda m: (m, place, 0, 0, 0)),
+        out_specs=out_block,
         input_output_aliases={5: 0} if more else {},
-        cost_estimate=pl.CostEstimate(flops=26 * below.size, bytes_accessed=16 * below.size, transcendentals=0),
+        cost_estimate=pl.CostEstimate(flops=below.size, bytes_accessed=below.size, transcendentals=0),
     )(cells, below, above, courant, spread, *more)
 
 
-def sample_kernel(tile_ref, row_ref, column_ref, field_ref, level_ref, *refs):
-    out_ref = refs[-1]
-    fields = refs[:-1]
+def sample_kernel(tile_ref, row_ref, column_ref, field_ref, level_ref, whole_ref, split_ref, out_ref, mine):
     members, count = out_ref.shape
-    rows_here = fields[0].shape[2]
+    early, rows_here = whole_ref.shape[1:3]
     first = tile_ref[0] * rows_here
     out_ref[...] = jnp.zeros(out_ref.shape, jnp.float32)
     line = iota((members, SUB, 128), 1)
     place = iota((members, 128), 1)
 
-    def one(k, carry):
+    def look(k, found):
+        mine[found] = k
         row = row_ref[k] - first
-
-        @pl.when((row >= 0) & (row < rows_here))
+        return found + ((row >= 0) & (row < rows_here)).astype(jnp.int32)
+
+    found = lax.fori_loop(0, count, look, jnp.int32(0), unroll=8)
+
+    def one(index, carry):
+        k = mine[index]
+        row = row_ref[k] - first
+        level = level_ref[k]
+        column = column_ref[k]
+        field = field_ref[k]
+        level_base = pl.multiple_of((level // SUB) * SUB, SUB)
+        column_base = pl.multiple_of((column // 128) * 128, 128)
+        target = pl.multiple_of((k // 128) * 128, 128)
+
+        def put(seen):
+            value = jnp.sum(jnp.where(line == level - level_base, seen, 0.0), axis=1)
+            value = pltpu.roll(value, lax.rem(k - column + 512, 128), 1)
+            kept = out_ref[:, pl.ds(target, 128)]
+            out_ref[:, pl.ds(target, 128)] = jnp.where(place == k - target, value, kept)
+
+        @pl.when(field < early)
         def _():
-            level = level_ref[k]
-            column = column_ref[k]
-            level_base = pl.multiple_of((level // SUB) * SUB, SUB)
-            column_base = pl.multiple_of((column // 128) * 128, 128)
-            target = pl.multiple_of((k // 128) * 128, 128)
-            for f, (ref, inner) in enumerate((ref, g) for ref in fields for g in range(ref.shape[1])):
-
-                @pl.when(field_ref[k] == f)
-                def _(ref=ref, inner=inner):
-                    seen = ref[:, inner, row, pl.ds(level_base, SUB), pl.ds(column_base, 128)]
-                    value = jnp.sum(jnp.where(line == level - level_base, seen, 0.0), axis=1)
-                    shift = lax.rem(k - column + 512, 128)
-                    value = pltpu.roll(value, shift, 1)
-                    kept = out_ref[:, pl.ds(target, 128)]
-                    out_ref[:, pl.ds(target, 128)] = jnp.where(place == k - target, value, kept)
+            put(whole_ref[:, field, row, pl.ds(level_base, SUB), pl.ds(column_base, 128)])
+
+        @pl.when(field >= early)
+        def _():
+            put(split_ref[2 * row + column // 128, :, field - early, pl.ds(level_base, SUB), :])
 
         return carry
 
-    lax.fori_loop(0, count, one, 0)
-
-
-def sample(state, tile_pos, row, column, field, level):
+    lax.fori_loop(0, found, one, 0)
+
+
+def sample(whole, split, tile_pos, row, column, field, level):
     smem = pl.BlockSpec(memory_space=pltpu.SMEM)
     vmem = pl.BlockSpec(memory_space=pltpu.VMEM)
     return pl.pallas_call(
         sample_kernel,
-        out_shape=jax.ShapeDtypeStruct((state[0].shape[0], row.shape[0]), jnp.float32),
-        in_specs=[smem] * 5 + [vmem] * len(state),
+        out_shape=jax.ShapeDtypeStruct((whole.shape[0], row.shape[0]), jnp.float32),
+        in_specs=[smem] * 5 + [vmem] * 2,
         out_specs=vmem,
+        scratch_shapes=[pltpu.SMEM((row.shape[0] + 1,), jnp.int32)],
         compiler_params=pltpu.CompilerParams(vmem_limit_bytes=32 * 2**20),
-    )(tile_pos.reshape(1), row, column, field, level, *state)
-
-
-def filter_kernel(obs_ref, err_ref, root_ref, raw_0, raw_1, raw_2, raw_3, wide_ref, high_ref, low_ref, gram, shift, slope, inc, mean_ref, *, members, group):
+    )(tile_pos.reshape(1), row, column, field, level, whole, split)
+
+
+def filter_kernel(order_ref, obs_ref, err_ref, root_ref, raw_0, raw_1, raw_2, raw_3, wide_ref, high_ref, low_ref, joined, gram, shift, slope, inc, mean_ref, *, members, group):
     count = raw_0.shape[1]
     lanes = gram.shape[1]
     freedom = members - 1.0
     here = raw_0.shape[0]
-    raw = jnp.transpose(jnp.concatenate([raw_0[...], raw_1[...], raw_2[...], raw_3[...]], axis=0))
+    for j, piece in enumerate((raw_0, raw_1, raw_2, raw_3)):
+        joined[pl.ds(pl.multiple_of(order_ref[j] * here, here), here), :] = piece[...]
+    raw = jnp.transpose(joined[...])
     centre = jnp.sum(raw, axis=1, keepdims=True) / members
     anomaly = raw - centre
     mean_ref[...] = jnp.transpose(jnp.broadcast_to(centre, (count, 8 * 16)))[:8, :]
@@ -203,10 +225,10 @@
                 left, right, (((0,), (0,)), ((), ())), precision=HI, preferred_element_type=jnp.float32)
     whole = lax.dot_general(
         inc[...], shift[:, count:], (((0,), (0,)), ((), ())), precision=HI, preferred_element_type=jnp.float32)
-    mine = whole[members:members + here, :members]
+    mine = whole[members:2 * members, :members]
     mine = mine + (iota(mine.shape, 0) == iota(mine.shape, 1)).astype(jnp.float32)
     tall, broad = high_ref.shape
-    down = (iota((tall, here), 0) // SUB == iota((tall, here), 1)).astype(jnp.float32)
+    down = (iota((tall, members), 0) // SUB == iota((tall, members), 1)).astype(jnp.float32)
     over = (iota((members, broad), 1) // SUB == iota((members, broad), 0)).astype(jnp.float32)
     spread = jnp.dot(jnp.dot(down, mine, precision=HI), over, precision=HI)
     spread = jnp.where(iota((tall, broad), 0) % SUB == iota((tall, broad), 1) % SUB, spread, 0.0)
@@ -215,19 +237,20 @@
     low_ref[...] = (spread - high.astype(jnp.float32)).astype(jnp.bfloat16)
 
 
-def run_filter(pieces, obs_value, obs_error, wide, group=64):
+def run_filter(order, pieces, obs_value, obs_error, wide, group=64):
     here, count = pieces[0].shape
     members = here * len(pieces)
     lanes = count + 2 * members
     smem = pl.BlockSpec(memory_space=pltpu.SMEM)
     vmem = pl.BlockSpec(memory_space=pltpu.VMEM)
-    spread = jax.ShapeDtypeStruct((here * SUB, members * SUB), jnp.bfloat16)
+    spread = jax.ShapeDtypeStruct((members * SUB, members * SUB), jnp.bfloat16)
     return pl.pallas_call(
         functools.partial(filter_kernel, members=members, group=group),
         out_shape=(spread, spread),
-        in_specs=[smem] * 3 + [vmem] * 5,
+        in_specs=[smem] * 4 + [vmem] * 5,
         out_specs=(vmem, vmem),
         scratch_shapes=[
+            pltpu.VMEM((members, count), jnp.float32),
             pltpu.VMEM((count, lanes), jnp.float32),
             pltpu.VMEM((count, lanes), jnp.float32),
             pltpu.VMEM((count, lanes), jnp.float32),
@@ -235,7 +258,7 @@
             pltpu.VMEM((8, count), jnp.float32),
         ],
         compiler_params=pltpu.CompilerParams(vmem_limit_bytes=32 * 2**20),
-    )(obs_value, obs_error, jnp.sqrt(obs_error), *pieces, wide)
+    )(order, obs_value, obs_error, jnp.sqrt(obs_error), *pieces, wide)
 
 
 def wide_weights(observation_row, localize, own, rows_here, members):
@@ -248,47 +271,91 @@
         [across, jnp.broadcast_to(own[:, None], (count, members)), jnp.zeros((count, members), jnp.float32)], axis=1)
 
 
-def update_kernel(order_ref, high_ref, low_ref, *refs):
-    out_ref = refs[-1]
-    high = high_ref[...]
-    low = low_ref[...]
+def product(high, low, cells):
     both = jnp.concatenate([high, low], axis=0)
     tall = high.shape[0]
+    top = cells.astype(jnp.bfloat16)
+    rest = (cells - top.astype(jnp.float32)).astype(jnp.bfloat16)
+    first = jnp.dot(both, top, preferred_element_type=jnp.float32)
+    second = jnp.dot(high, rest, preferred_element_type=jnp.float32)
+    return first[:tall] + (first[tall:] + second)
+
+
+def gathered_kernel(mem_ref, high_ref, low_ref, cells_ref, out_ref):
     here = out_ref.shape[0]
-    groups = refs[0].shape[0] // here
-    for f, (ref, inner) in enumerate((ref, g) for ref in refs[:-1] for g in range(ref.shape[1])):
+    mine = pl.ds(pl.multiple_of(mem_ref[0] * here * SUB, here * SUB), here * SUB)
+    high, low = high_ref[mine, :], low_ref[mine, :]
+    for f in range(out_ref.shape[1]):
         for r in range(out_ref.shape[2]):
-            cells = jnp.concatenate(
-                [ref[pl.ds(order_ref[j] * here, here), inner, r].reshape(-1, ref.shape[-1]) for j in range(groups)], axis=0
-            )
-            top = cells.astype(jnp.bfloat16)
-            rest = (cells - top.astype(jnp.float32)).astype(jnp.bfloat16)
-            first = jnp.dot(both, top, preferred_element_type=jnp.float32)
-            second = jnp.dot(high, rest, preferred_element_type=jnp.float32)
-            total = first[:tall] + (first[tall:] + second)
-            out_ref[:, f, r] = total.reshape(out_ref.shape[0], SUB, -1)
-
-
-def update(order, high, low, gathered):
-    flat = gathered
-    _, _, rows, levels, width = flat[0].shape
-    here = high.shape[0] // SUB
-    fields = sum(p.shape[1] for p in flat)
+            cells = cells_ref[:, f, r].reshape(-1, cells_ref.shape[-1])
+            out_ref[:, f, r] = product(high, low, cells).reshape(here, SUB, -1)
+
+
+def update_gathered(mem_pos, high, low, cells, all_fields):
+    members, fields, rows, levels, width = cells.shape
+    here = members // 4
     full = pl.BlockSpec(high.shape, lambda i: (0, 0))
     return pl.pallas_call(
-        update_kernel,
+        gathered_kernel,
         grid=(levels // SUB,),
-        out_shape=jax.ShapeDtypeStruct((here, fields, rows, levels, width), jnp.float32),
-        in_specs=[pl.BlockSpec(memory_space=pltpu.SMEM), full, full] + [pl.BlockSpec(p.shape[:2] + (rows, SUB, width), lambda i: (0, 0, 0, i, 0)) for p in flat],
+        out_shape=jax.ShapeDtypeStruct((here, all_fields, rows, levels, width), jnp.float32),
+        in_specs=[
+            pl.BlockSpec(memory_space=pltpu.SMEM), full, full,
+            pl.BlockSpec((members, fields, rows, SUB, width), lambda i: (0, 0, 0, i, 0)),
+        ],
         out_specs=pl.BlockSpec((here, fields, rows, SUB, width), lambda i: (0, 0, 0, i, 0)),
         compiler_params=pltpu.CompilerParams(vmem_limit_bytes=40 * 2**20),
-    )(order, high, low, *flat)
-
-
-def exchange(total, swaps):
-    for pairs in swaps:
-        total = total + lax.ppermute(total, "tile", pairs)
-    return total
+    )(mem_pos.reshape(1), high, low, cells)
+
+
+def piece_kernel(high_ref, low_ref, cells_ref, out_ref):
+    groups, here, fields, _, width = cells_ref.shape
+    cells = jnp.concatenate([cells_ref[:, :, f].reshape(-1, width) for f in range(fields)], axis=1)
+    total = product(high_ref[...], low_ref[...], cells)
+    for f in range(fields):
+        out_ref[:, :, f] = total[:, f * width:(f + 1) * width].reshape(groups, here, SUB, width)
+
+
+def update_piece(high, low, cells):
+    groups, here, fields, levels, width = cells.shape
+    full = pl.BlockSpec(high.shape, lambda i: (0, 0))
+    block = pl.BlockSpec((groups, here, fields, SUB, width), lambda i: (0, 0, 0, i, 0))
+    return pl.pallas_call(
+        piece_kernel,
+        grid=(levels // SUB,),
+        out_shape=jax.ShapeDtypeStruct(cells.shape, jnp.float32),
+        in_specs=[full, full, block],
+        out_specs=block,
+        compiler_params=pltpu.CompilerParams(vmem_limit_bytes=40 * 2**20),
+    )(high, low, cells)
+
+
+def join_kernel(back_ref, sofar_ref, out_ref):
+    half = back_ref.shape[-1]
+    for piece in range(back_ref.shape[0]):
+        r, h = piece // 2, piece % 2
+        out_ref[:, :, r, :, h * half:(h + 1) * half] = back_ref[piece]
+
+
+def join(back, sofar):
+    pieces, here, fields, levels, half = back.shape
+    part = 8
+    place = sofar.shape[1] // fields - 1
+    return pl.pallas_call(
+        join_kernel,
+        grid=(here // part,),
+        out_shape=jax.ShapeDtypeStruct(sofar.shape, jnp.float32),
+        in_specs=[
+            pl.BlockSpec((pieces, part, fields, levels, half), lambda m: (0, m, 0, 0, 0)),
+            pl.BlockSpec(memory_space=pl.ANY),
+        ],
+        out_specs=pl.BlockSpec((part, fields) + sofar.shape[2:], lambda m: (m, place, 0, 0, 0)),
+        input_output_aliases={1: 0},
+    )(back, sofar)
+
+
+def after(value, *others):
+    return lax.optimization_barrier((value,) + others)[0]
 
 
 def on_device(
@@ -316,29 +383,40 @@
     own = lax.dynamic_slice_in_dim(localize, tile_pos, 1, 0)[0]
     wide = wide_weights(observation_row, localize, own, rows_here, ens_size)
 
-    state = []
-    for group in GROUPS:
+    mem_pos = lax.axis_index("mem")
+    order = lax.rem(mem_pos - jnp.arange(groups, dtype=jnp.int32) + groups, groups)
+
+    def shifted(array, by):
+        return lax.ppermute(array, "tile", [(i, (i + by) % tiles) for i in range(tiles)])
+
+    def step(cells, f, into=None, split=False, wait=()):
+        below, above = shifted(cells, 1), shifted(cells, -1)
+        if wait:
+            below = after(below, *wait)
+        return forecast_step(cells, below, above, flow, spread, f, into, split)
+
+    middle = [step(start[:, f:f + 1], f) for f in range(fields)]
+
+    def last_step(fields_of, split, wait):
         whole = None
-        middle = []
-        for f in group:
-            cells = start[:, f:f + 1]
-            below = lax.ppermute(cells, "tile", onward)
-            above = lax.ppermute(cells, "tile", backward)
-            middle.append(forecast_step(cells, below, above, flow, spread, f))
-        for place, f in enumerate(group):
-            below = lax.ppermute(middle[place], "tile", onward)
-            above = lax.ppermute(middle[place], "tile", backward)
-            whole = forecast_step(middle[place], below, above, flow, spread, f, (len(group), place, whole))
-        state.append(whole)
-    gathered = [lax.all_gather(cells, "mem", axis=0, tiled=True) for cells in state]
-    seen = sample(state, tile_pos, observation_row, observation_column, observation_field, observation_level)
-    swaps = [[(i, i ^ bit) for i in range(tiles)] for bit in (1, 2, 4, 8, 16, 32)]
-    seen = exchange(seen, swaps)
+        for place, f in enumerate(fields_of):
+            whole = step(middle[f], f, (len(fields_of), place, whole), split, wait)
+        return whole
+
+    whole = last_step(GROUPS[0], False, middle)
+    split = last_step(GROUPS[1], True, (whole,))
+    gathered = lax.all_gather(after(whole, split), "mem", axis=0, tiled=True)
+    swapped = lax.all_to_all(split, "mem", 0, 0, tiled=True)
+    seen = sample(
+        whole, split, tile_pos, observation_row, observation_column, observation_field, observation_level
+    )
+    for bit in (1, 2, 4, 8, 16, 32):
+        seen = seen + lax.ppermute(seen, "tile", [(i, i ^ bit) for i in range(tiles)])
     pieces = [seen] + [lax.ppermute(seen, "mem", [(i, (i + d) % groups) for i in range(groups)]) for d in range(1, groups)]
-    high, low = run_filter(pieces, obs_value, obs_error, wide)
-    order = lax.rem(lax.axis_index("mem") - jnp.arange(groups, dtype=jnp.int32) + groups, groups)
-    result = update(order, high, low, gathered)
-    return jnp.transpose(result, (0, 1, 3, 2, 4))
+    high, low = run_filter(order, pieces, obs_value, obs_error, wide)
+    back = lax.all_to_all(update_piece(high, low, swapped), "mem", 0, 0, tiled=True)
+    result = update_gathered(mem_pos, high, low, gathered, fields)
+    return jnp.transpose(join(back, result), (0, 1, 3, 2, 4))
 
 
 def solution(mesh):

time: 217 us -> 204 us (0.940)
  waiting for transfers between devices: 95.1 us -> 60.5 us
  starting transfers between devices: 28.5 us -> 45.1 us
  local copies, waits for them, and re-layouts: 14.8 us -> 19.4 us
    ppermute x22, waiting for transfers between devices: 75.1 us -> 51 us  [the longest x6 25.6 us: on_device(): lax.ppermute(seen, 'tile', [(i, i ^ bit) for i in range(tiles)])]
    all_gather x2 -> x1, waiting for transfers between devices: 17.8 us -> 0.01 us  [on_device(): gathered = lax.all_gather(after(whole, split), 'mem', axis=0, tiled=True)]
    all_to_all x0 -> x2, starting transfers between devices: none -> 11.1 us  [the longest x1 5.92 us: on_device(): lax.all_to_all(update_piece(high, low, swapped), 'mem', 0, 0, tiled=True)]
    all_to_all x0 -> x2, waiting for transfers between devices: none -> 7.24 us  [the longest x1 7.23 us: on_device(): lax.all_to_all(update_piece(high, low, swapped), 'mem', 0, 0, tiled=True)]
    ppermute x22, starting transfers between devices: 23.7 us -> 29.3 us  [the longest x16 29.3 us: shifted(): lax.ppermute(array, 'tile', [(i, (i + by) % tiles) for i in range(tiles)])]
    unnamed x54 -> x52, local copies, waits for them, and re-layouts: 10.1 us -> 12.9 us
    pallas_call x10 -> x12, Pallas kernels: 35.9 us -> 36.9 us  [the longest x8 25.6 us: forecast_step(): pl.pallas_call(functools.partial(step_kernel, split), grid=(count // part...]
  transfers between devices with their start and end apart: 27 -> 28, of which waited for: 21 -> 16; matrix products, arithmetic and copies ran while one was open for 1% -> 1% of each run, Pallas kernels for 25% -> 29%
where the time goes in v3:
time: 204 us
  Pallas kernels  64.6 us (32%)
  waiting for transfers between devices  60.5 us (30%)
  starting transfers between devices  45.1 us (22%)
  local copies, waits for them, and re-layouts  19.4 us (10%)
  between operations  13.7 us (7%)
    ppermute x16, starting transfers between devices, shifted(): lax.ppermute(array, 'tile', [(i, (i + by) % tiles) for i in range(tiles)])  29.3 us
    pallas_call x1, Pallas kernels, run_filter(): pl.pallas_call(functools.partial(filter_kernel, members=members, group=gr...  27.7 us
    ppermute x6, waiting for transfers between devices, on_device(): lax.ppermute(seen, 'tile', [(i, i ^ bit) for i in range(tiles)])  25.6 us
    pallas_call x8, Pallas kernels, forecast_step(): pl.pallas_call(functools.partial(step_kernel, split), grid=(count // part...  25.6 us
    ppermute x16, waiting for transfers between devices, shifted(): lax.ppermute(array, 'tile', [(i, (i + by) % tiles) for i in range(tiles)])  25.4 us
    unnamed x52, local copies, waits for them, and re-layouts  12.9 us
    all_to_all x1, waiting for transfers between devices, on_device(): lax.all_to_all(update_piece(high, low, swapped), 'mem', 0, 0, tiled=True)  7.23 us
    all_to_all x1, starting transfers between devices, on_device(): lax.all_to_all(update_piece(high, low, swapped), 'mem', 0, 0, tiled=True)  5.92 us
  transfers between devices with their start and end apart: 28, of which 16 were waited for; matrix products, arithmetic and copies ran while one was open for 1% of the time, Pallas kernels for 29%

profile of v3, /device:TPU:2, one launch (start us, length us, event | category | flops | bytes accessed | tf_op | source)
XLA Modules:
  0.0 203.9 jit_solution(4377627656744957917)
XLA Ops:
  6.5 2.2 %copy.25 = f32[16,4,24,2,256]{4,2,3,1,0:T(8,128)S(1)} copy(f32[16,4,24,2,256]{4,3,2,1,0:T(2,128)} %param.10) | data formatting | bytes 6291456 | tf_op args[0]
  9.1 7.8 %collective-permute-start.8 = (f32[16,1,2,24,256]{4,3,2,1,0:T(8,128)S(1)}, f32[16,1,2,24,256]{4,3,2,1,0:T(8,128)S(1)}, u32[]{:S(2)}, u32[]{:S(2)}) collective-permute-start(f32[16,1,2,24,256]{4,3,2,1,0:T(8,128)S(1)} %get-tuple-element.19.cells_ref), channel_id=1, source_target_pairs={{0,252},{4,0},{8,4},{12,8},{16,12},{20,16},{24,20},{28,24},{32,28}... | collective-permute-start | bytes 2359304 | tf_op jit(solution)/shard_map/ppermute | solution.py:390
  17.6 5.1 %collective-permute-start.1 = (f32[16,1,2,24,256]{4,3,2,1,0:T(8,128)S(1)}, f32[16,1,2,24,256]{4,3,2,1,0:T(8,128)}, u32[]{:S(2)}, u32[]{:S(2)}) collective-permute-start(f32[16,1,2,24,256]{4,3,2,1,0:T(8,128)S(1)} %get-tuple-element.22.cells_ref), channel_id=1, source_target_pairs={{0,252},{4,0},{8,4},{12,8},{16,12},{20,16},{24,20},{28,24},{32,28}... | collective-permute-start | bytes 2359304 | tf_op jit(solution)/shard_map/ppermute | solution.py:390
  22.7 3.8 %collective-permute-done.8.above_ref = f32[16,1,2,24,256]{4,3,2,1,0:T(8,128)S(1)} collective-permute-done((f32[16,1,2,24,256]{4,3,2,1,0:T(8,128)S(1)}, f32[16,1,2,24,256]{4,3,2,1,0:T(8,128)S(1)}, u32[]{:S(2)}, u32[]{:S(2)}) %collective-permute-start.8) | collective-permute-done | bytes 786464 | tf_op jit(solution)/shard_map/ppermute | solution.py:390
  26.5 0.9 copy-done.16
  27.3 5.2 %collective-permute-start.6 = (f32[16,1,2,24,256]{4,3,2,1,0:T(8,128)S(1)}, f32[16,1,2,24,256]{4,3,2,1,0:T(8,128)}, u32[]{:S(2)}, u32[]{:S(2)}) collective-permute-start(f32[16,1,2,24,256]{4,3,2,1,0:T(8,128)S(1)} %get-tuple-element.20.cells_ref), channel_id=1, source_target_pairs={{0,252},{4,0},{8,4},{12,8},{16,12},{20,16},{24,20},{28,24},{32,28}... | collective-permute-start | bytes 2359304 | tf_op jit(solution)/shard_map/ppermute | solution.py:390
  33.2 1.7 collective-permute-done.4.above_ref
  34.9 0.9 copy-done.17
  35.8 0.9 copy-done.18
  37.4 3.2 %shard_map.101.cells_ref = f32[16,1,2,24,256]{4,3,2,1,0:T(8,128)} custom-call(f32[16,1,2,24,256]{4,3,2,1,0:T(8,128)} %copy-done.15, f32[16,1,2,24,256]{4,3,2,1,0:T(8,128)} %copy-done.18, f32[16,1,2,24,256]{4,3,2,1,0:T(8,128)} %copy-done.17, f32[2,2,24,256]{3,2,1,0:T(8,128)} %bitcast.15, f32[4,24,256]{2,1,0:T(8,128)} %broadcast_in_dim.8.spread_ref), custom_call_target="tpu_custom_call" | custom-call | flops 196608 | bytes 196608 | tf_op jit(solution)/shard_map/pallas_call | solution.py:58
  40.6 2.7 %collective-permute-done.1.above_ref = f32[16,1,2,24,256]{4,3,2,1,0:T(8,128)} collective-permute-done((f32[16,1,2,24,256]{4,3,2,1,0:T(8,128)S(1)}, f32[16,1,2,24,256]{4,3,2,1,0:T(8,128)}, u32[]{:S(2)}, u32[]{:S(2)}) %collective-permute-start.1) | collective-permute-done | bytes 786464 | tf_op jit(solution)/shard_map/ppermute | solution.py:390
  43.3 5.3 %collective-permute-start.11 = (f32[16,1,2,24,256]{4,3,2,1,0:T(8,128)}, f32[16,1,2,24,256]{4,3,2,1,0:T(8,128)S(1)}, u32[]{:S(2)}, u32[]{:S(2)}) collective-permute-start(f32[16,1,2,24,256]{4,3,2,1,0:T(8,128)} %shard_map.101.cells_ref), channel_id=1, source_target_pairs={{0,252},{4,0},{8,4},{12,8},{16,12},{20,16},{24,20},{28,24},{32,28}... | collective-permute-start | bytes 2359304 | tf_op jit(solution)/shard_map/ppermute | solution.py:390
  48.7 3.2 %shard_map.100.cells_ref = f32[16,1,2,24,256]{4,3,2,1,0:T(8,128)} custom-call(f32[16,1,2,24,256]{4,3,2,1,0:T(8,128)} %copy-done.14, f32[16,1,2,24,256]{4,3,2,1,0:T(8,128)} %collective-permute-done.below_ref, f32[16,1,2,24,256]{4,3,2,1,0:T(8,128)} %collective-permute-done.1.above_ref, f32[2,2,24,256]{3,2,1,0:T(8,128)} %bitcast.16, ...), custom_call_target="tpu_custom_call" | custom-call | flops 196608 | bytes 196608 | tf_op jit(solution)/shard_map/pallas_call | solution.py:58
  51.9 6.4 %collective-permute-done.5.below_ref = f32[16,1,2,24,256]{4,3,2,1,0:T(8,128)} collective-permute-done((f32[16,1,2,24,256]{4,3,2,1,0:T(8,128)S(1)}, f32[16,1,2,24,256]{4,3,2,1,0:T(8,128)}, u32[]{:S(2)}, u32[]{:S(2)}) %collective-permute-start.5) | collective-permute-done | bytes 786464 | tf_op jit(solution)/shard_map/ppermute | solution.py:390
  58.3 3.2 %shard_map.102.cells_ref = f32[16,1,2,24,256]{4,3,2,1,0:T(8,128)} custom-call(f32[16,1,2,24,256]{4,3,2,1,0:T(8,128)} %copy-done.13, f32[16,1,2,24,256]{4,3,2,1,0:T(8,128)} %collective-permute-done.5.below_ref, f32[16,1,2,24,256]{4,3,2,1,0:T(8,128)} %collective-permute-done.6.above_ref, f32[2,2,24,256]{3,2,1,0:T(8,128)} %bitcast.17, ...), custom_call_target="tpu_custom_call" | custom-call | flops 196608 | bytes 196608 | tf_op jit(solution)/shard_map/pallas_call | solution.py:58
  62.0 4.6 %collective-permute-start.15 = (f32[16,1,2,24,256]{4,3,2,1,0:T(8,128)}, f32[16,1,2,24,256]{4,3,2,1,0:T(8,128)}, u32[]{:S(2)}, u32[]{:S(2)}) collective-permute-start(f32[16,1,2,24,256]{4,3,2,1,0:T(8,128)} %shard_map.102.cells_ref), channel_id=1, source_target_pairs={{0,252},{4,0},{8,4},{12,8},{16,12},{20,16},{24,20},{28,24},{32,28}... | collective-permute-start | bytes 2359304 | tf_op jit(solution)/shard_map/ppermute | solution.py:390
  66.6 3.1 %shard_map.103.cells_ref = f32[16,1,2,24,256]{4,3,2,1,0:T(8,128)} custom-call(f32[16,1,2,24,256]{4,3,2,1,0:T(8,128)} %copy-done.12, f32[16,1,2,24,256]{4,3,2,1,0:T(8,128)} %collective-permute-done.7.below_ref, f32[16,1,2,24,256]{4,3,2,1,0:T(8,128)} %copy-done.16, f32[2,2,24,256]{3,2,1,0:T(8,128)} %bitcast.18, f32[4,24,256]{2,1,0:T(8,128)} %broadcast_in_dim.8.spread_ref), custom_call_target="tpu_custom_call" | custom-call | flops 196608 | bytes 196608 | tf_op jit(solution)/shard_map/pallas_call | solution.py:58
  69.7 5.3 %collective-permute-done.2.below_ref = f32[16,1,2,24,256]{4,3,2,1,0:T(8,128)S(1)} collective-permute-done((f32[16,1,2,24,256]{4,3,2,1,0:T(8,128)}, f32[16,1,2,24,256]{4,3,2,1,0:T(8,128)S(1)}, u32[]{:S(2)}, u32[]{:S(2)}) %collective-permute-start.2) | collective-permute-done | bytes 786464 | tf_op jit(solution)/shard_map/ppermute | solution.py:390
  75.1 3.4 %shard_map.104.refs_0_ = f32[16,2,2,24,256]{4,3,2,1,0:T(8,128)} custom-call(f32[16,1,2,24,256]{4,3,2,1,0:T(8,128)} %shard_map.101.cells_ref, f32[16,1,2,24,256]{4,3,2,1,0:T(8,128)} %collective-permute-done.10.below_ref, f32[16,1,2,24,256]{4,3,2,1,0:T(8,128)} %copy-done.19, f32[2,2,24,256]{3,2,1,0:T(8,128)} %bitcast.19, f32[4,24,256]{2,1,0:T(8,128)} %broadcast_in_dim.8.spread_ref), custom_call_target="tpu_custom_call" | custom-call | flops 196608 | bytes 196608 | tf_op jit(solution)/shard_map/pallas_call | solution.py:58
  78.5 0.9 copy-done.22
  79.4 3.1 %shard_map.105.whole_ref = f32[16,2,2,24,256]{4,3,2,1,0:T(8,128)} custom-call(f32[16,1,2,24,256]{4,3,2,1,0:T(8,128)} %shard_map.100.cells_ref, f32[16,1,2,24,256]{4,3,2,1,0:T(8,128)} %copy-done.20, f32[16,1,2,24,256]{4,3,2,1,0:T(8,128)} %copy-done.22, f32[2,2,24,256]{3,2,1,0:T(8,128)} %bitcast.20, ...), custom_call_target="tpu_custom_call", output_to_operand_aliasing={{}: (5, {})} | custom-call | flops 196608 | bytes 196608 | tf_op jit(solution)/shard_map/pallas_call | solution.py:58
  82.5 0.9 collective-permute-done.14.below_ref
  83.5 0.9 copy-done.21
  84.4 3.2 %shard_map.106.refs_0_ = f32[4,16,2,24,128]{4,3,2,1,0:T(8,128)} custom-call(f32[16,1,2,24,256]{4,3,2,1,0:T(8,128)} %shard_map.102.cells_ref, f32[16,1,2,24,256]{4,3,2,1,0:T(8,128)} %copy-done.21, f32[16,1,2,24,256]{4,3,2,1,0:T(8,128)} %collective-permute-done.15.above_ref, f32[2,2,24,256]{3,2,1,0:T(8,128)} %bitcast.21, f32[4,24,256]{2,1,0:T(8,128)} %broadcast_in_dim.8.spread_ref), custom_call_target="tpu_custom_call" | custom-call | flops 196608 | bytes 196608 | tf_op jit(solution)/shard_map/pallas_call | solution.py:58
  87.5 4.5 %collective-permute-done.12.below_ref = f32[16,1,2,24,256]{4,3,2,1,0:T(8,128)} collective-permute-done((f32[16,1,2,24,256]{4,3,2,1,0:T(8,128)}, f32[16,1,2,24,256]{4,3,2,1,0:T(8,128)}, u32[]{:S(2)}, u32[]{:S(2)}) %collective-permute-start.12) | collective-permute-done | bytes 786464 | tf_op jit(solution)/shard_map/ppermute | solution.py:390
  92.0 3.2 %shard_map.107.split_ref = f32[4,16,2,24,128]{4,3,2,1,0:T(8,128)} custom-call(f32[16,1,2,24,256]{4,3,2,1,0:T(8,128)} %shard_map.103.cells_ref, f32[16,1,2,24,256]{4,3,2,1,0:T(8,128)} %collective-permute-done.12.below_ref, f32[16,1,2,24,256]{4,3,2,1,0:T(8,128)} %collective-permute-done.13.above_ref, ...), custom_call_target="tpu_custom_call", output_to_operand_aliasing={{}: (5, {})} | custom-call | flops 196608 | bytes 196608 | tf_op jit(solution)/shard_map/pallas_call | solution.py:58
  95.3 5.1 %all-to-all-start = ((f32[4,16,2,24,128]{4,3,2,1,0:T(8,128)}), f32[4,16,2,24,128]{4,3,2,1,0:T(8,128)}, u32[]{:S(2)}, u32[]{:S(2)}) async-start(f32[4,16,2,24,128]{4,3,2,1,0:T(8,128)} %shard_map.107.split_ref), calls=%async_computation | async-start | bytes 3145728 | tf_op jit(solution)/shard_map/all_to_all | solution.py:409
  100.5 2.4 %shard_map.108 = f32[16,256]{1,0:T(8,128)S(1)} custom-call(s32[1]{0:T(128)} %bitcast.tile_ref, s32[256]{0:T(256)S(1)} %copy-done.5, s32[256]{0:T(256)S(1)} %copy-done.7, s32[256]{0:T(256)S(1)} %copy-done.8, s32[256]{0:T(256)S(1)} %copy-done.9, f32[16,2,2,24,256]{4,3,2,1,0:T(8,128)S(1)} %copy-done.3, f32[4,16,2,24,128]{4,3,2,1,0:T(8,128)S(1)} %copy-done.2), custom_call_target="tpu_custom_call" | custom-call | tf_op jit(solution)/shard_map/pallas_call | solution.py:122
  102.9 1.2 collective-permute-done.16
  104.1 3.7 %collective-permute-done.17 = f32[16,256]{1,0:T(8,128)S(1)} collective-permute-done((f32[16,256]{1,0:T(8,128)S(1)}, f32[16,256]{1,0:T(8,128)S(1)}, u32[]{:S(2)}, u32[]{:S(2)}) %collective-permute-start.17) | collective-permute-done | bytes 16416 | tf_op jit(solution)/shard_map/ppermute | solution.py:414
  107.9 4.7 %collective-permute-done.18 = f32[16,256]{1,0:T(8,128)S(1)} collective-permute-done((f32[16,256]{1,0:T(8,128)S(1)}, f32[16,256]{1,0:T(8,128)S(1)}, u32[]{:S(2)}, u32[]{:S(2)}) %collective-permute-start.18) | collective-permute-done | bytes 16416 | tf_op jit(solution)/shard_map/ppermute | solution.py:414
  112.9 7.3 %collective-permute-done.19 = f32[16,256]{1,0:T(8,128)S(1)} collective-permute-done((f32[16,256]{1,0:T(8,128)S(1)}, f32[16,256]{1,0:T(8,128)S(1)}, u32[]{:S(2)}, u32[]{:S(2)}) %collective-permute-start.19) | collective-permute-done | bytes 16416 | tf_op jit(solution)/shard_map/ppermute | solution.py:414
  120.3 3.6 %collective-permute-done.20 = f32[16,256]{1,0:T(8,128)S(1)} collective-permute-done((f32[16,256]{1,0:T(8,128)S(1)}, f32[16,256]{1,0:T(8,128)S(1)}, u32[]{:S(2)}, u32[]{:S(2)}) %collective-permute-start.20) | collective-permute-done | bytes 16416 | tf_op jit(solution)/shard_map/ppermute | solution.py:414
  124.1 5.1 %collective-permute-done.21 = f32[16,256]{1,0:T(8,128)S(1)} collective-permute-done((f32[16,256]{1,0:T(8,128)S(1)}, f32[16,256]{1,0:T(8,128)S(1)}, u32[]{:S(2)}, u32[]{:S(2)}) %collective-permute-start.21) | collective-permute-done | bytes 16416 | tf_op jit(solution)/shard_map/ppermute | solution.py:414
  129.3 2.8 %collective-permute-start.23 = (f32[16,256]{1,0:T(8,128)S(1)}, f32[16,256]{1,0:T(8,128)S(1)}, u32[]{:S(2)}, u32[]{:S(2)}) collective-permute-start(f32[16,256]{1,0:T(8,128)S(1)} %add.31.raw_0), channel_id=1, source_target_pairs={{0,2},{1,3},{2,0},{3,1},{4,6},{5,7},{6,4},{7,5},{8,10},{9,11},{10,... | collective-permute-start | bytes 49160 | tf_op jit(solution)/shard_map/ppermute | solution.py:415
  132.1 1.8 collective-permute-start.22
  134.0 0.9 collective-permute-done.23.raw_2
  134.9 1.3 collective-permute-done.22.raw_1
  136.2 27.7 %shard_map.109 = (bf16[512,512]{1,0:T(8,128)(2,1)S(1)}, bf16[512,512]{1,0:T(8,128)(2,1)S(1)}) custom-call(s32[4]{0:T(128)S(1)} %compare_select_fusion.order_ref, f32[256]{0:T(256)S(1)} %copy-done.10, f32[256]{0:T(256)S(1)} %copy-done.6, f32[256]{0:T(256)S(1)} %sqrt.3.root_ref, f32[16,256]{1,0:T(8,128)S(1)} %add.31.raw_0, ...), custom_call_target="tpu_custom_call" | custom-call | tf_op jit(solution)/shard_map/pallas_call | solution.py:247
  164.0 4.3 %shard_map.110 = f32[4,16,2,24,128]{4,3,2,1,0:T(8,128)} custom-call(bf16[512,512]{1,0:T(8,128)(2,1)S(1)} %get-tuple-element.16.high_ref, bf16[512,512]{1,0:T(8,128)(2,1)S(1)} %get-tuple-element.17.low_ref, f32[4,16,2,24,128]{4,3,2,1,0:T(8,128)} %all-to-all-done.cells_ref), custom_call_target="tpu_custom_call" | custom-call | tf_op jit(solution)/shard_map/pallas_call | solution.py:323
  168.3 5.9 %all-to-all-start.1 = ((f32[4,16,2,24,128]{4,3,2,1,0:T(8,128)}), f32[4,16,2,24,128]{4,3,2,1,0:T(8,128)S(1)}, u32[]{:S(2)}, u32[]{:S(2)}) async-start(f32[4,16,2,24,128]{4,3,2,1,0:T(8,128)} %shard_map.110), calls=%async_computation.1 | async-start | bytes 3145728 | tf_op jit(solution)/shard_map/all_to_all | solution.py:417
  174.2 2.8 %copy-done.4 = f32[64,2,2,24,256]{4,3,2,1,0:T(8,128)S(1)} copy-done((f32[64,2,2,24,256]{4,3,2,1,0:T(8,128)S(1)}, f32[64,2,2,24,256]{4,3,2,1,0:T(8,128)}, u32[]{:S(2)}) %copy-start.4) | copy-done | bytes 6291480
  177.0 2.3 %shard_map.111.sofar_ref = f32[16,4,2,24,256]{4,3,2,1,0:T(8,128)S(1)} custom-call(s32[1]{0:T(128)} %bitcast.5.mem_ref, bf16[512,512]{1,0:T(8,128)(2,1)S(1)} %get-tuple-element.16.high_ref, bf16[512,512]{1,0:T(8,128)(2,1)S(1)} %get-tuple-element.17.low_ref, f32[64,2,2,24,256]{4,3,2,1,0:T(8,128)S(1)} %copy-done.4), custom_call_target="tpu_custom_call" | custom-call | tf_op jit(solution)/shard_map/pallas_call | solution.py:298
  179.3 1.6 copy-done.1
  180.9 7.2 %all-to-all-done.1.back_ref = f32[4,16,2,24,128]{4,3,2,1,0:T(8,128)S(1)} async-done(((f32[4,16,2,24,128]{4,3,2,1,0:T(8,128)}), f32[4,16,2,24,128]{4,3,2,1,0:T(8,128)S(1)}, u32[]{:S(2)}, u32[]{:S(2)}) %all-to-all-start.1) | async-done | bytes 1572896 | tf_op jit(solution)/shard_map/all_to_all | solution.py:417
  188.1 1.1 copy-done.11
  189.3 2.4 %shard_map.112 = f32[16,4,2,24,256]{4,3,2,1,0:T(8,128)} custom-call(f32[4,16,2,24,128]{4,3,2,1,0:T(8,128)} %copy-done.11, f32[16,4,2,24,256]{4,3,2,1,0:T(8,128)} %copy-done.1), custom_call_target="tpu_custom_call", output_to_operand_aliasing={{}: (1, {})} | custom-call | tf_op jit(solution)/shard_map/pallas_call | solution.py:344
  191.7 5.3 %copy.21 = f32[16,4,24,2,256]{4,3,2,1,0:T(2,128)} copy(f32[16,4,24,2,256]{4,2,3,1,0:T(8,128)} %bitcast.13) | data formatting | bytes 6291456 | tf_op jit(solution)/shard_map/transpose | solution.py:419
  (92 shorter events, 3.8 us)
Async XLA Ops:
  6.5 106.0 %copy-start = (f32[64,256]{1,0:T(8,128)S(1)}, f32[64,256]{1,0:T(8,128)}, u32[]{:S(2)}) copy-start(f32[64,256]{1,0:T(8,128)} %param.19) | copy-start | bytes 196612
  6.5 167.6 %all-gather.2.cloned.1.call-start = ((), (), s32[]{:S(2)}) async-start(), calls=%async_computation.2 | async-start | bytes 7864320 | tf_op jit(solution)/shard_map/all_gather | solution.py:408
  8.8 23.8 %copy-start.23 = (f32[2,24,2,256]{3,2,1,0:T(2,128)S(1)}, f32[2,24,2,256]{3,2,1,0:T(2,128)}, u32[]{:S(2)}) copy-start(f32[2,24,2,256]{3,2,1,0:T(2,128)} %param.11) | copy-start | bytes 294916
  8.8 27.9 %copy-start.24 = (f32[4,24]{1,0:T(4,128)S(1)}, f32[4,24]{1,0:T(4,128)}, u32[]{:S(2)}) copy-start(f32[4,24]{1,0:T(4,128)} %param.12) | copy-start | bytes 1156
  9.1 28.3 %copy-start.15 = (f32[16,1,2,24,256]{4,3,2,1,0:T(8,128)}, f32[16,1,2,24,256]{4,3,2,1,0:T(8,128)S(1)}, u32[]{:S(2)}) copy-start(f32[16,1,2,24,256]{4,3,2,1,0:T(8,128)S(1)} %get-tuple-element.21.cells_ref) | copy-start | bytes 2359300
  9.1 39.6 %copy-start.14 = (f32[16,1,2,24,256]{4,3,2,1,0:T(8,128)}, f32[16,1,2,24,256]{4,3,2,1,0:T(8,128)S(1)}, u32[]{:S(2)}) copy-start(f32[16,1,2,24,256]{4,3,2,1,0:T(8,128)S(1)} %get-tuple-element.22.cells_ref) | copy-start | bytes 2359300
  9.1 42.7 %copy-start.12 = (f32[16,1,2,24,256]{4,3,2,1,0:T(8,128)}, f32[16,1,2,24,256]{4,3,2,1,0:T(8,128)S(1)}, u32[]{:S(2)}) copy-start(f32[16,1,2,24,256]{4,3,2,1,0:T(8,128)S(1)} %get-tuple-element.19.cells_ref) | copy-start | bytes 2359300
  9.1 42.7 %copy-start.13 = (f32[16,1,2,24,256]{4,3,2,1,0:T(8,128)}, f32[16,1,2,24,256]{4,3,2,1,0:T(8,128)S(1)}, u32[]{:S(2)}) copy-start(f32[16,1,2,24,256]{4,3,2,1,0:T(8,128)S(1)} %get-tuple-element.20.cells_ref) | copy-start | bytes 2359300
  9.1 17.3 %collective-permute-start.8 = (f32[16,1,2,24,256]{4,3,2,1,0:T(8,128)S(1)}, f32[16,1,2,24,256]{4,3,2,1,0:T(8,128)S(1)}, u32[]{:S(2)}, u32[]{:S(2)}) collective-permute-start(f32[16,1,2,24,256]{4,3,2,1,0:T(8,128)S(1)} %get-tuple-element.19.cells_ref), channel_id=1, source_target_pairs={{0,252},{4,0},{8,4},{12,8},{16,12},{20,16},{24,20},{28,24},{32,28}... | collective-permute-start | bytes 2359304 | tf_op jit(solution)/shard_map/ppermute | solution.py:390
  17.0 17.9 %collective-permute-start.4 = (f32[16,1,2,24,256]{4,3,2,1,0:T(8,128)S(1)}, f32[16,1,2,24,256]{4,3,2,1,0:T(8,128)S(1)}, u32[]{:S(2)}, u32[]{:S(2)}) collective-permute-start(f32[16,1,2,24,256]{4,3,2,1,0:T(8,128)S(1)} %get-tuple-element.21.cells_ref), channel_id=1, source_target_pairs={{0,252},{4,0},{8,4},{12,8},{16,12},{20,16},{24,20},{28,24},{32,28}... | collective-permute-start | bytes 2359304 | tf_op jit(solution)/shard_map/ppermute | solution.py:390
  17.6 17.3 %collective-permute-start.3 = (f32[16,1,2,24,256]{4,3,2,1,0:T(8,128)S(1)}, f32[16,1,2,24,256]{4,3,2,1,0:T(8,128)S(1)}, u32[]{:S(2)}, u32[]{:S(2)}) collective-permute-start(f32[16,1,2,24,256]{4,3,2,1,0:T(8,128)S(1)} %get-tuple-element.21.cells_ref), channel_id=1, source_target_pairs={{0,4},{4,8},{8,12},{12,16},{16,20},{20,24},{24,28},{28,32},{32,36}... | collective-permute-start | bytes 2359304 | tf_op jit(solution)/shard_map/ppermute | solution.py:390
  17.6 25.7 %collective-permute-start.1 = (f32[16,1,2,24,256]{4,3,2,1,0:T(8,128)S(1)}, f32[16,1,2,24,256]{4,3,2,1,0:T(8,128)}, u32[]{:S(2)}, u32[]{:S(2)}) collective-permute-start(f32[16,1,2,24,256]{4,3,2,1,0:T(8,128)S(1)} %get-tuple-element.22.cells_ref), channel_id=1, source_target_pairs={{0,252},{4,0},{8,4},{12,8},{16,12},{20,16},{24,20},{28,24},{32,28}... | collective-permute-start | bytes 2359304 | tf_op jit(solution)/shard_map/ppermute | solution.py:390
  22.7 26.0 %collective-permute-start = (f32[16,1,2,24,256]{4,3,2,1,0:T(8,128)S(1)}, f32[16,1,2,24,256]{4,3,2,1,0:T(8,128)}, u32[]{:S(2)}, u32[]{:S(2)}) collective-permute-start(f32[16,1,2,24,256]{4,3,2,1,0:T(8,128)S(1)} %get-tuple-element.22.cells_ref), channel_id=1, source_target_pairs={{0,4},{4,8},{8,12},{12,16},{16,20},{20,24},{24,28},{28,32},{32,36}... | collective-permute-start | bytes 2359304 | tf_op jit(solution)/shard_map/ppermute | solution.py:390
  27.3 24.5 %collective-permute-start.6 = (f32[16,1,2,24,256]{4,3,2,1,0:T(8,128)S(1)}, f32[16,1,2,24,256]{4,3,2,1,0:T(8,128)}, u32[]{:S(2)}, u32[]{:S(2)}) collective-permute-start(f32[16,1,2,24,256]{4,3,2,1,0:T(8,128)S(1)} %get-tuple-element.20.cells_ref), channel_id=1, source_target_pairs={{0,252},{4,0},{8,4},{12,8},{16,12},{20,16},{24,20},{28,24},{32,28}... | collective-permute-start | bytes 2359304 | tf_op jit(solution)/shard_map/ppermute | solution.py:390
  34.9 26.6 %collective-permute-start.7 = (f32[16,1,2,24,256]{4,3,2,1,0:T(8,128)S(1)}, f32[16,1,2,24,256]{4,3,2,1,0:T(8,128)}, u32[]{:S(2)}, u32[]{:S(2)}) collective-permute-start(f32[16,1,2,24,256]{4,3,2,1,0:T(8,128)S(1)} %get-tuple-element.19.cells_ref), channel_id=1, source_target_pairs={{0,4},{4,8},{8,12},{12,16},{16,20},{20,24},{24,28},{28,32},{32,36}... | collective-permute-start | bytes 2359304 | tf_op jit(solution)/shard_map/ppermute | solution.py:390
  35.8 22.5 %collective-permute-start.5 = (f32[16,1,2,24,256]{4,3,2,1,0:T(8,128)S(1)}, f32[16,1,2,24,256]{4,3,2,1,0:T(8,128)}, u32[]{:S(2)}, u32[]{:S(2)}) collective-permute-start(f32[16,1,2,24,256]{4,3,2,1,0:T(8,128)S(1)} %get-tuple-element.20.cells_ref), channel_id=1, source_target_pairs={{0,4},{4,8},{8,12},{12,16},{16,20},{20,24},{24,28},{28,32},{32,36}... | collective-permute-start | bytes 2359304 | tf_op jit(solution)/shard_map/ppermute | solution.py:390
  43.3 18.7 %collective-permute-start.11 = (f32[16,1,2,24,256]{4,3,2,1,0:T(8,128)}, f32[16,1,2,24,256]{4,3,2,1,0:T(8,128)S(1)}, u32[]{:S(2)}, u32[]{:S(2)}) collective-permute-start(f32[16,1,2,24,256]{4,3,2,1,0:T(8,128)} %shard_map.101.cells_ref), channel_id=1, source_target_pairs={{0,252},{4,0},{8,4},{12,8},{16,12},{20,16},{24,20},{28,24},{32,28}... | collective-permute-start | bytes 2359304 | tf_op jit(solution)/shard_map/ppermute | solution.py:390
  48.6 21.1 %collective-permute-start.10 = (f32[16,1,2,24,256]{4,3,2,1,0:T(8,128)}, f32[16,1,2,24,256]{4,3,2,1,0:T(8,128)}, u32[]{:S(2)}, u32[]{:S(2)}) collective-permute-start(f32[16,1,2,24,256]{4,3,2,1,0:T(8,128)} %shard_map.101.cells_ref), channel_id=1, source_target_pairs={{0,4},{4,8},{8,12},{12,16},{16,20},{20,24},{24,28},{28,32},{32,36}... | collective-permute-start | bytes 2359304 | tf_op jit(solution)/shard_map/ppermute | solution.py:390
  51.8 23.2 %collective-permute-start.2 = (f32[16,1,2,24,256]{4,3,2,1,0:T(8,128)}, f32[16,1,2,24,256]{4,3,2,1,0:T(8,128)S(1)}, u32[]{:S(2)}, u32[]{:S(2)}) collective-permute-start(f32[16,1,2,24,256]{4,3,2,1,0:T(8,128)} %shard_map.100.cells_ref), channel_id=1, source_target_pairs={{0,4},{4,8},{8,12},{12,16},{16,20},{20,24},{24,28},{28,32},{32,36}... | collective-permute-start | bytes 2359304 | tf_op jit(solution)/shard_map/ppermute | solution.py:390
  58.3 20.2 %collective-permute-start.9 = (f32[16,1,2,24,256]{4,3,2,1,0:T(8,128)}, f32[16,1,2,24,256]{4,3,2,1,0:T(8,128)S(1)}, u32[]{:S(2)}, u32[]{:S(2)}) collective-permute-start(f32[16,1,2,24,256]{4,3,2,1,0:T(8,128)} %shard_map.100.cells_ref), channel_id=1, source_target_pairs={{0,252},{4,0},{8,4},{12,8},{16,12},{20,16},{24,20},{28,24},{32,28}... | collective-permute-start | bytes 2359304 | tf_op jit(solution)/shard_map/ppermute | solution.py:390
  61.5 22.0 %collective-permute-start.14 = (f32[16,1,2,24,256]{4,3,2,1,0:T(8,128)}, f32[16,1,2,24,256]{4,3,2,1,0:T(8,128)S(1)}, u32[]{:S(2)}, u32[]{:S(2)}) collective-permute-start(f32[16,1,2,24,256]{4,3,2,1,0:T(8,128)} %shard_map.102.cells_ref), channel_id=1, source_target_pairs={{0,4},{4,8},{8,12},{12,16},{16,20},{20,24},{24,28},{28,32},{32,36}... | collective-permute-start | bytes 2359304 | tf_op jit(solution)/shard_map/ppermute | solution.py:390
  62.0 13.1 %copy-start.19 = (f32[16,1,2,24,256]{4,3,2,1,0:T(8,128)}, f32[16,1,2,24,256]{4,3,2,1,0:T(8,128)S(1)}, u32[]{:S(2)}) copy-start(f32[16,1,2,24,256]{4,3,2,1,0:T(8,128)S(1)} %collective-permute-done.11.above_ref) | copy-start | bytes 2359300
  62.0 21.5 %collective-permute-start.15 = (f32[16,1,2,24,256]{4,3,2,1,0:T(8,128)}, f32[16,1,2,24,256]{4,3,2,1,0:T(8,128)}, u32[]{:S(2)}, u32[]{:S(2)}) collective-permute-start(f32[16,1,2,24,256]{4,3,2,1,0:T(8,128)} %shard_map.102.cells_ref), channel_id=1, source_target_pairs={{0,252},{4,0},{8,4},{12,8},{16,12},{20,16},{24,20},{28,24},{32,28}... | collective-permute-start | bytes 2359304 | tf_op jit(solution)/shard_map/ppermute | solution.py:390
  69.7 22.3 %collective-permute-start.12 = (f32[16,1,2,24,256]{4,3,2,1,0:T(8,128)}, f32[16,1,2,24,256]{4,3,2,1,0:T(8,128)}, u32[]{:S(2)}, u32[]{:S(2)}) collective-permute-start(f32[16,1,2,24,256]{4,3,2,1,0:T(8,128)} %shard_map.103.cells_ref), channel_id=1, source_target_pairs={{0,4},{4,8},{8,12},{12,16},{16,20},{20,24},{24,28},{28,32},{32,36}... | collective-permute-start | bytes 2359304 | tf_op jit(solution)/shard_map/ppermute | solution.py:390
  75.1 3.4 %copy-start.20 = (f32[16,1,2,24,256]{4,3,2,1,0:T(8,128)}, f32[16,1,2,24,256]{4,3,2,1,0:T(8,128)S(1)}, u32[]{:S(2)}) copy-start(f32[16,1,2,24,256]{4,3,2,1,0:T(8,128)S(1)} %collective-permute-done.2.below_ref) | copy-start | bytes 2359300
  75.1 17.0 %collective-permute-start.13 = (f32[16,1,2,24,256]{4,3,2,1,0:T(8,128)}, f32[16,1,2,24,256]{4,3,2,1,0:T(8,128)}, u32[]{:S(2)}, u32[]{:S(2)}) collective-permute-start(f32[16,1,2,24,256]{4,3,2,1,0:T(8,128)} %shard_map.103.cells_ref), channel_id=1, source_target_pairs={{0,252},{4,0},{8,4},{12,8},{16,12},{20,16},{24,20},{28,24},{32,28}... | collective-permute-start | bytes 2359304 | tf_op jit(solution)/shard_map/ppermute | solution.py:390
  95.2 5.2 %copy-start.2 = (f32[4,16,2,24,128]{4,3,2,1,0:T(8,128)S(1)}, f32[4,16,2,24,128]{4,3,2,1,0:T(8,128)}, u32[]{:S(2)}) copy-start(f32[4,16,2,24,128]{4,3,2,1,0:T(8,128)} %shard_map.107.split_ref) | copy-start | bytes 4718596
  95.2 5.2 %copy-start.3 = (f32[16,2,2,24,256]{4,3,2,1,0:T(8,128)S(1)}, f32[16,2,2,24,256]{4,3,2,1,0:T(8,128)}, u32[]{:S(2)}) copy-start(f32[16,2,2,24,256]{4,3,2,1,0:T(8,128)} %shard_map.105.whole_ref) | copy-start | bytes 4718596
  95.2 5.2 %copy-start.5 = (s32[256]{0:T(256)S(1)}, s32[256]{0:T(256)}, u32[]{:S(2)}) copy-start(s32[256]{0:T(256)} %row_ref.1) | copy-start | bytes 3076
  95.2 5.2 %copy-start.7 = (s32[256]{0:T(256)S(1)}, s32[256]{0:T(256)}, u32[]{:S(2)}) copy-start(s32[256]{0:T(256)} %column_ref.1) | copy-start | bytes 3076
  95.2 5.2 %copy-start.8 = (s32[256]{0:T(256)S(1)}, s32[256]{0:T(256)}, u32[]{:S(2)}) copy-start(s32[256]{0:T(256)} %field_ref.1) | copy-start | bytes 3076
  95.3 5.2 %copy-start.9 = (s32[256]{0:T(256)S(1)}, s32[256]{0:T(256)}, u32[]{:S(2)}) copy-start(s32[256]{0:T(256)} %level_ref.1) | copy-start | bytes 3076
  95.3 68.7 %all-to-all-start = ((f32[4,16,2,24,128]{4,3,2,1,0:T(8,128)}), f32[4,16,2,24,128]{4,3,2,1,0:T(8,128)}, u32[]{:S(2)}, u32[]{:S(2)}) async-start(f32[4,16,2,24,128]{4,3,2,1,0:T(8,128)} %shard_map.107.split_ref), calls=%async_computation | async-start | bytes 3145728 | tf_op jit(solution)/shard_map/all_to_all | solution.py:409
  100.4 33.5 %copy-start.6 = (f32[256]{0:T(256)S(1)}, f32[256]{0:T(256)}, u32[]{:S(2)}) copy-start(f32[256]{0:T(256)} %err_ref.1) | copy-start | bytes 3076
  100.4 35.8 %copy-start.10 = (f32[256]{0:T(256)S(1)}, f32[256]{0:T(256)}, u32[]{:S(2)}) copy-start(f32[256]{0:T(256)} %obs_ref.1) | copy-start | bytes 3076
  102.9 1.2 collective-permute-start.16
  104.1 3.7 %collective-permute-start.17 = (f32[16,256]{1,0:T(8,128)S(1)}, f32[16,256]{1,0:T(8,128)S(1)}, u32[]{:S(2)}, u32[]{:S(2)}) collective-permute-start(f32[16,256]{1,0:T(8,128)S(1)} %add.26), channel_id=1, source_target_pairs={{0,8},{4,12},{8,0},{12,4},{16,24},{20,28},{24,16},{28,20},{32,40},... | collective-permute-start | bytes 49160 | tf_op jit(solution)/shard_map/ppermute | solution.py:414
  107.8 4.7 %collective-permute-start.18 = (f32[16,256]{1,0:T(8,128)S(1)}, f32[16,256]{1,0:T(8,128)S(1)}, u32[]{:S(2)}, u32[]{:S(2)}) collective-permute-start(f32[16,256]{1,0:T(8,128)S(1)} %add.27), channel_id=1, source_target_pairs={{0,16},{4,20},{8,24},{12,28},{16,0},{20,4},{24,8},{28,12},{32,48},... | collective-permute-start | bytes 49160 | tf_op jit(solution)/shard_map/ppermute | solution.py:414
  112.6 7.6 %collective-permute-start.19 = (f32[16,256]{1,0:T(8,128)S(1)}, f32[16,256]{1,0:T(8,128)S(1)}, u32[]{:S(2)}, u32[]{:S(2)}) collective-permute-start(f32[16,256]{1,0:T(8,128)S(1)} %add.28), channel_id=1, source_target_pairs={{0,32},{4,36},{8,40},{12,44},{16,48},{20,52},{24,56},{28,60},{32,0... | collective-permute-start | bytes 49160 | tf_op jit(solution)/shard_map/ppermute | solution.py:414
  120.2 3.7 %collective-permute-start.20 = (f32[16,256]{1,0:T(8,128)S(1)}, f32[16,256]{1,0:T(8,128)S(1)}, u32[]{:S(2)}, u32[]{:S(2)}) collective-permute-start(f32[16,256]{1,0:T(8,128)S(1)} %add.29), channel_id=1, source_target_pairs={{0,64},{4,68},{8,72},{12,76},{16,80},{20,84},{24,88},{28,92},{32,9... | collective-permute-start | bytes 49160 | tf_op jit(solution)/shard_map/ppermute | solution.py:414
  124.0 5.2 %collective-permute-start.21 = (f32[16,256]{1,0:T(8,128)S(1)}, f32[16,256]{1,0:T(8,128)S(1)}, u32[]{:S(2)}, u32[]{:S(2)}) collective-permute-start(f32[16,256]{1,0:T(8,128)S(1)} %add.30), channel_id=1, source_target_pairs={{0,128},{4,132},{8,136},{12,140},{16,144},{20,148},{24,152},{28,15... | collective-permute-start | bytes 49160 | tf_op jit(solution)/shard_map/ppermute | solution.py:414
  129.2 4.7 %collective-permute-start.24 = (f32[16,256]{1,0:T(8,128)S(1)}, f32[16,256]{1,0:T(8,128)S(1)}, u32[]{:S(2)}, u32[]{:S(2)}) collective-permute-start(f32[16,256]{1,0:T(8,128)S(1)} %add.31.raw_0), channel_id=1, source_target_pairs={{0,3},{1,0},{2,1},{3,2},{4,7},{5,4},{6,5},{7,6},{8,11},{9,8},{10,9... | collective-permute-start | bytes 49160 | tf_op jit(solution)/shard_map/ppermute | solution.py:415
  129.3 5.6 %collective-permute-start.23 = (f32[16,256]{1,0:T(8,128)S(1)}, f32[16,256]{1,0:T(8,128)S(1)}, u32[]{:S(2)}, u32[]{:S(2)}) collective-permute-start(f32[16,256]{1,0:T(8,128)S(1)} %add.31.raw_0), channel_id=1, source_target_pairs={{0,2},{1,3},{2,0},{3,1},{4,6},{5,7},{6,4},{7,5},{8,10},{9,11},{10,... | collective-permute-start | bytes 49160 | tf_op jit(solution)/shard_map/ppermute | solution.py:415
  132.1 4.1 %collective-permute-start.22 = (f32[16,256]{1,0:T(8,128)S(1)}, f32[16,256]{1,0:T(8,128)S(1)}, u32[]{:S(2)}, u32[]{:S(2)}) collective-permute-start(f32[16,256]{1,0:T(8,128)S(1)} %add.31.raw_0), channel_id=1, source_target_pairs={{0,1},{1,2},{2,3},{3,0},{4,5},{5,6},{6,7},{7,4},{8,9},{9,10},{10,1... | collective-permute-start | bytes 49160 | tf_op jit(solution)/shard_map/ppermute | solution.py:415
  168.3 19.9 %all-to-all-start.1 = ((f32[4,16,2,24,128]{4,3,2,1,0:T(8,128)}), f32[4,16,2,24,128]{4,3,2,1,0:T(8,128)S(1)}, u32[]{:S(2)}, u32[]{:S(2)}) async-start(f32[4,16,2,24,128]{4,3,2,1,0:T(8,128)} %shard_map.110), calls=%async_computation.1 | async-start | bytes 3145728 | tf_op jit(solution)/shard_map/all_to_all | solution.py:417
  174.2 2.8 %copy-start.4 = (f32[64,2,2,24,256]{4,3,2,1,0:T(8,128)S(1)}, f32[64,2,2,24,256]{4,3,2,1,0:T(8,128)}, u32[]{:S(2)}) copy-start(f32[64,2,2,24,256]{4,3,2,1,0:T(8,128)} %all-gather.2.cloned.1.call-done.cells_ref) | copy-start | bytes 18874372
  179.2 1.6 copy-start.1
  188.1 1.1 copy-start.11
  (5 other events, 4.4 us)
Sparse Core Ops, SparseCore 0:
  95.4 71.1 all-gather.1

commit v4 on v3

--- a/solution.py
+++ b/solution.py
@@ -205,8 +205,13 @@
         inc[pl.ds(base, BLK), :] = keep_g
         left = jnp.concatenate([x[:, first:last], z[:, first:last]], axis=0)
         right = jnp.concatenate([z, x], axis=0)
+        left_top, right_top = left.astype(jnp.bfloat16), right.astype(jnp.bfloat16)
+        left_rest = (left - left_top.astype(jnp.float32)).astype(jnp.bfloat16)
+        right_rest = (right - right_top.astype(jnp.float32)).astype(jnp.bfloat16)
         gram[first:last, :] = gram[first:last, :] - lax.dot_general(
-            left, right, (((0,), (0,)), ((), ())), precision=HI, preferred_element_type=jnp.float32)
+            jnp.concatenate([left_top, left_rest, left_top], axis=0),
+            jnp.concatenate([right_top, right_top, right_rest], axis=0),
+            (((0,), (0,)), ((), ())), preferred_element_type=jnp.float32)
 
     for first in range(0, count, group):
         last = first + group
@@ -286,9 +291,9 @@
     mine = pl.ds(pl.multiple_of(mem_ref[0] * here * SUB, here * SUB), here * SUB)
     high, low = high_ref[mine, :], low_ref[mine, :]
     for f in range(out_ref.shape[1]):
-        for r in range(out_ref.shape[2]):
+        for r in range(out_ref.shape[3]):
             cells = cells_ref[:, f, r].reshape(-1, cells_ref.shape[-1])
-            out_ref[:, f, r] = product(high, low, cells).reshape(here, SUB, -1)
+            out_ref[:, f, :, r, :] = product(high, low, cells).reshape(here, SUB, -1)
 
 
 def update_gathered(mem_pos, high, low, cells, all_fields):
@@ -298,12 +303,12 @@
     return pl.pallas_call(
         gathered_kernel,
         grid=(levels // SUB,),
-        out_shape=jax.ShapeDtypeStruct((here, all_fields, rows, levels, width), jnp.float32),
+        out_shape=jax.ShapeDtypeStruct((here, all_fields, levels, rows, width), jnp.float32),
         in_specs=[
             pl.BlockSpec(memory_space=pltpu.SMEM), full, full,
             pl.BlockSpec((members, fields, rows, SUB, width), lambda i: (0, 0, 0, i, 0)),
         ],
-        out_specs=pl.BlockSpec((here, fields, rows, SUB, width), lambda i: (0, 0, 0, i, 0)),
+        out_specs=pl.BlockSpec((here, fields, SUB, rows, width), lambda i: (0, 0, i, 0, 0)),
         compiler_params=pltpu.CompilerParams(vmem_limit_bytes=40 * 2**20),
     )(mem_pos.reshape(1), high, low, cells)
 
@@ -334,7 +339,7 @@
     half = back_ref.shape[-1]
     for piece in range(back_ref.shape[0]):
         r, h = piece // 2, piece % 2
-        out_ref[:, :, r, :, h * half:(h + 1) * half] = back_ref[piece]
+        out_ref[:, :, :, r, h * half:(h + 1) * half] = back_ref[piece]
 
 
 def join(back, sofar):
@@ -416,7 +421,7 @@
     high, low = run_filter(order, pieces, obs_value, obs_error, wide)
     back = lax.all_to_all(update_piece(high, low, swapped), "mem", 0, 0, tiled=True)
     result = update_gathered(mem_pos, high, low, gathered, fields)
-    return jnp.transpose(join(back, result), (0, 1, 3, 2, 4))
+    return join(back, result)
 
 
 def solution(mesh):

time: 204 us -> 197 us (0.966)
  local copies, waits for them, and re-layouts: 19.4 us -> 13.6 us
  Pallas kernels: 64.6 us -> 62.3 us
    transpose x1 -> x0, local copies, waits for them, and re-layouts: 5.34 us -> none  [on_device(): return jnp.transpose(join(back, result), (0, 1, 3, 2, 4))]
    pallas_call x1, Pallas kernels: 27.7 us -> 24.5 us  [run_filter(): pl.pallas_call(functools.partial(filter_kernel, members=members, group=gr...]
where the time goes in v4:
time: 197 us; the launch traced here: 196 us
  Pallas kernels  62.3 us (32%)
  waiting for transfers between devices  61.3 us (31%)
  starting transfers between devices  45.1 us (23%)
  between operations  13.7 us (7%)
  local copies, waits for them, and re-layouts  13.6 us (7%)
    ppermute x16, starting transfers between devices, shifted(): lax.ppermute(array, 'tile', [(i, (i + by) % tiles) for i in range(tiles)])  29.3 us
    ppermute x6, waiting for transfers between devices, on_device(): lax.ppermute(seen, 'tile', [(i, i ^ bit) for i in range(tiles)])  25.7 us
    ppermute x16, waiting for transfers between devices, shifted(): lax.ppermute(array, 'tile', [(i, (i + by) % tiles) for i in range(tiles)])  25.4 us
    pallas_call x8, Pallas kernels, forecast_step(): pl.pallas_call(functools.partial(step_kernel, split), grid=(count // part...  25.3 us
    pallas_call x1, Pallas kernels, run_filter(): pl.pallas_call(functools.partial(filter_kernel, members=members, group=gr...  24.5 us
    unnamed x52, local copies, waits for them, and re-layouts  12.4 us
    all_to_all x1, waiting for transfers between devices, on_device(): lax.all_to_all(update_piece(high, low, swapped), 'mem', 0, 0, tiled=True)  7.95 us
    all_to_all x1, starting transfers between devices, on_device(): lax.all_to_all(update_piece(high, low, swapped), 'mem', 0, 0, tiled=True)  5.9 us
  transfers between devices with their start and end apart: 28, of which 16 were waited for; matrix products, arithmetic and copies ran while one was open for 1% of the time, Pallas kernels for 29%

profile of v4, /device:TPU:2, one launch (start us, length us, event | category | flops | bytes accessed | tf_op | source)
XLA Modules:
  0.0 196.4 jit_solution(10919794727843815813)
XLA Ops:
  6.5 2.2 %copy.23 = f32[16,4,24,2,256]{4,2,3,1,0:T(8,128)S(1)} copy(f32[16,4,24,2,256]{4,3,2,1,0:T(2,128)} %param.10) | data formatting | bytes 6291456 | tf_op args[0]
  9.1 7.8 %collective-permute-start.8 = (f32[16,1,2,24,256]{4,3,2,1,0:T(8,128)S(1)}, f32[16,1,2,24,256]{4,3,2,1,0:T(8,128)S(1)}, u32[]{:S(2)}, u32[]{:S(2)}) collective-permute-start(f32[16,1,2,24,256]{4,3,2,1,0:T(8,128)S(1)} %get-tuple-element.19.cells_ref), channel_id=1, source_target_pairs={{0,252},{4,0},{8,4},{12,8},{16,12},{20,16},{24,20},{28,24},{32,28}... | collective-permute-start | bytes 2359304 | tf_op jit(solution)/shard_map/ppermute | solution.py:395
  17.6 5.1 %collective-permute-start.1 = (f32[16,1,2,24,256]{4,3,2,1,0:T(8,128)S(1)}, f32[16,1,2,24,256]{4,3,2,1,0:T(8,128)}, u32[]{:S(2)}, u32[]{:S(2)}) collective-permute-start(f32[16,1,2,24,256]{4,3,2,1,0:T(8,128)S(1)} %get-tuple-element.22.cells_ref), channel_id=1, source_target_pairs={{0,252},{4,0},{8,4},{12,8},{16,12},{20,16},{24,20},{28,24},{32,28}... | collective-permute-start | bytes 2359304 | tf_op jit(solution)/shard_map/ppermute | solution.py:395
  22.7 3.8 %collective-permute-done.8.above_ref = f32[16,1,2,24,256]{4,3,2,1,0:T(8,128)S(1)} collective-permute-done((f32[16,1,2,24,256]{4,3,2,1,0:T(8,128)S(1)}, f32[16,1,2,24,256]{4,3,2,1,0:T(8,128)S(1)}, u32[]{:S(2)}, u32[]{:S(2)}) %collective-permute-start.8) | collective-permute-done | bytes 786464 | tf_op jit(solution)/shard_map/ppermute | solution.py:395
  26.5 0.9 copy-done.15
  27.3 5.2 %collective-permute-start.6 = (f32[16,1,2,24,256]{4,3,2,1,0:T(8,128)S(1)}, f32[16,1,2,24,256]{4,3,2,1,0:T(8,128)}, u32[]{:S(2)}, u32[]{:S(2)}) collective-permute-start(f32[16,1,2,24,256]{4,3,2,1,0:T(8,128)S(1)} %get-tuple-element.20.cells_ref), channel_id=1, source_target_pairs={{0,252},{4,0},{8,4},{12,8},{16,12},{20,16},{24,20},{28,24},{32,28}... | collective-permute-start | bytes 2359304 | tf_op jit(solution)/shard_map/ppermute | solution.py:395
  33.2 1.7 collective-permute-done.4.above_ref
  34.9 1.0 copy-done.16
  35.9 0.9 copy-done.17
  36.8 0.7 broadcast_in_dim.8.spread_ref
  37.5 3.1 %shard_map.101.cells_ref = f32[16,1,2,24,256]{4,3,2,1,0:T(8,128)} custom-call(f32[16,1,2,24,256]{4,3,2,1,0:T(8,128)} %copy-done.14, f32[16,1,2,24,256]{4,3,2,1,0:T(8,128)} %copy-done.17, f32[16,1,2,24,256]{4,3,2,1,0:T(8,128)} %copy-done.16, f32[2,2,24,256]{3,2,1,0:T(8,128)} %bitcast.13, f32[4,24,256]{2,1,0:T(8,128)} %broadcast_in_dim.8.spread_ref), custom_call_target="tpu_custom_call" | custom-call | flops 196608 | bytes 196608 | tf_op jit(solution)/shard_map/pallas_call | solution.py:58
  40.7 2.7 %collective-permute-done.1.above_ref = f32[16,1,2,24,256]{4,3,2,1,0:T(8,128)} collective-permute-done((f32[16,1,2,24,256]{4,3,2,1,0:T(8,128)S(1)}, f32[16,1,2,24,256]{4,3,2,1,0:T(8,128)}, u32[]{:S(2)}, u32[]{:S(2)}) %collective-permute-start.1) | collective-permute-done | bytes 786464 | tf_op jit(solution)/shard_map/ppermute | solution.py:395
  43.3 5.3 %collective-permute-start.11 = (f32[16,1,2,24,256]{4,3,2,1,0:T(8,128)}, f32[16,1,2,24,256]{4,3,2,1,0:T(8,128)S(1)}, u32[]{:S(2)}, u32[]{:S(2)}) collective-permute-start(f32[16,1,2,24,256]{4,3,2,1,0:T(8,128)} %shard_map.101.cells_ref), channel_id=1, source_target_pairs={{0,252},{4,0},{8,4},{12,8},{16,12},{20,16},{24,20},{28,24},{32,28}... | collective-permute-start | bytes 2359304 | tf_op jit(solution)/shard_map/ppermute | solution.py:395
  48.7 3.2 %shard_map.100.cells_ref = f32[16,1,2,24,256]{4,3,2,1,0:T(8,128)} custom-call(f32[16,1,2,24,256]{4,3,2,1,0:T(8,128)} %copy-done.13, f32[16,1,2,24,256]{4,3,2,1,0:T(8,128)} %collective-permute-done.below_ref, f32[16,1,2,24,256]{4,3,2,1,0:T(8,128)} %collective-permute-done.1.above_ref, f32[2,2,24,256]{3,2,1,0:T(8,128)} %bitcast.14, ...), custom_call_target="tpu_custom_call" | custom-call | flops 196608 | bytes 196608 | tf_op jit(solution)/shard_map/pallas_call | solution.py:58
  51.8 6.5 %collective-permute-done.5.below_ref = f32[16,1,2,24,256]{4,3,2,1,0:T(8,128)} collective-permute-done((f32[16,1,2,24,256]{4,3,2,1,0:T(8,128)S(1)}, f32[16,1,2,24,256]{4,3,2,1,0:T(8,128)}, u32[]{:S(2)}, u32[]{:S(2)}) %collective-permute-start.5) | collective-permute-done | bytes 786464 | tf_op jit(solution)/shard_map/ppermute | solution.py:395
  58.3 3.2 %shard_map.102.cells_ref = f32[16,1,2,24,256]{4,3,2,1,0:T(8,128)} custom-call(f32[16,1,2,24,256]{4,3,2,1,0:T(8,128)} %copy-done.12, f32[16,1,2,24,256]{4,3,2,1,0:T(8,128)} %collective-permute-done.5.below_ref, f32[16,1,2,24,256]{4,3,2,1,0:T(8,128)} %collective-permute-done.6.above_ref, f32[2,2,24,256]{3,2,1,0:T(8,128)} %bitcast.15, ...), custom_call_target="tpu_custom_call" | custom-call | flops 196608 | bytes 196608 | tf_op jit(solution)/shard_map/pallas_call | solution.py:58
  62.0 4.6 %collective-permute-start.15 = (f32[16,1,2,24,256]{4,3,2,1,0:T(8,128)}, f32[16,1,2,24,256]{4,3,2,1,0:T(8,128)}, u32[]{:S(2)}, u32[]{:S(2)}) collective-permute-start(f32[16,1,2,24,256]{4,3,2,1,0:T(8,128)} %shard_map.102.cells_ref), channel_id=1, source_target_pairs={{0,252},{4,0},{8,4},{12,8},{16,12},{20,16},{24,20},{28,24},{32,28}... | collective-permute-start | bytes 2359304 | tf_op jit(solution)/shard_map/ppermute | solution.py:395
  66.6 3.1 %shard_map.103.cells_ref = f32[16,1,2,24,256]{4,3,2,1,0:T(8,128)} custom-call(f32[16,1,2,24,256]{4,3,2,1,0:T(8,128)} %copy-done.11, f32[16,1,2,24,256]{4,3,2,1,0:T(8,128)} %collective-permute-done.7.below_ref, f32[16,1,2,24,256]{4,3,2,1,0:T(8,128)} %copy-done.15, f32[2,2,24,256]{3,2,1,0:T(8,128)} %bitcast.16, f32[4,24,256]{2,1,0:T(8,128)} %broadcast_in_dim.8.spread_ref), custom_call_target="tpu_custom_call" | custom-call | flops 196608 | bytes 196608 | tf_op jit(solution)/shard_map/pallas_call | solution.py:58
  69.8 5.4 %collective-permute-done.2.below_ref = f32[16,1,2,24,256]{4,3,2,1,0:T(8,128)} collective-permute-done((f32[16,1,2,24,256]{4,3,2,1,0:T(8,128)}, f32[16,1,2,24,256]{4,3,2,1,0:T(8,128)}, u32[]{:S(2)}, u32[]{:S(2)}) %collective-permute-start.2) | collective-permute-done | bytes 786464 | tf_op jit(solution)/shard_map/ppermute | solution.py:395
  75.2 3.1 %shard_map.104.refs_0_ = f32[16,2,2,24,256]{4,3,2,1,0:T(8,128)} custom-call(f32[16,1,2,24,256]{4,3,2,1,0:T(8,128)} %shard_map.101.cells_ref, f32[16,1,2,24,256]{4,3,2,1,0:T(8,128)} %copy-done.19, f32[16,1,2,24,256]{4,3,2,1,0:T(8,128)} %copy-done.18, f32[2,2,24,256]{3,2,1,0:T(8,128)} %bitcast.17, f32[4,24,256]{2,1,0:T(8,128)} %broadcast_in_dim.8.spread_ref), custom_call_target="tpu_custom_call" | custom-call | flops 196608 | bytes 196608 | tf_op jit(solution)/shard_map/pallas_call | solution.py:58
  78.3 0.9 copy-done.21
  79.2 3.1 %shard_map.105.whole_ref = f32[16,2,2,24,256]{4,3,2,1,0:T(8,128)} custom-call(f32[16,1,2,24,256]{4,3,2,1,0:T(8,128)} %shard_map.100.cells_ref, f32[16,1,2,24,256]{4,3,2,1,0:T(8,128)} %collective-permute-done.2.below_ref, f32[16,1,2,24,256]{4,3,2,1,0:T(8,128)} %copy-done.21, f32[2,2,24,256]{3,2,1,0:T(8,128)} %bitcast.18, ...), custom_call_target="tpu_custom_call", output_to_operand_aliasing={{}: (5, {})} | custom-call | flops 196608 | bytes 196608 | tf_op jit(solution)/shard_map/pallas_call | solution.py:58
  82.4 1.1 collective-permute-done.14.below_ref
  83.5 0.9 copy-done.20
  84.4 3.2 %shard_map.106.refs_0_ = f32[4,16,2,24,128]{4,3,2,1,0:T(8,128)} custom-call(f32[16,1,2,24,256]{4,3,2,1,0:T(8,128)} %shard_map.102.cells_ref, f32[16,1,2,24,256]{4,3,2,1,0:T(8,128)} %copy-done.20, f32[16,1,2,24,256]{4,3,2,1,0:T(8,128)} %collective-permute-done.15.above_ref, f32[2,2,24,256]{3,2,1,0:T(8,128)} %bitcast.19, f32[4,24,256]{2,1,0:T(8,128)} %broadcast_in_dim.8.spread_ref), custom_call_target="tpu_custom_call" | custom-call | flops 196608 | bytes 196608 | tf_op jit(solution)/shard_map/pallas_call | solution.py:58
  87.6 4.3 %collective-permute-done.12.below_ref = f32[16,1,2,24,256]{4,3,2,1,0:T(8,128)S(1)} collective-permute-done((f32[16,1,2,24,256]{4,3,2,1,0:T(8,128)}, f32[16,1,2,24,256]{4,3,2,1,0:T(8,128)S(1)}, u32[]{:S(2)}, u32[]{:S(2)}) %collective-permute-start.12) | collective-permute-done | bytes 786464 | tf_op jit(solution)/shard_map/ppermute | solution.py:395
  91.9 0.9 copy-done.22
  92.8 3.2 %shard_map.107.split_ref = f32[4,16,2,24,128]{4,3,2,1,0:T(8,128)} custom-call(f32[16,1,2,24,256]{4,3,2,1,0:T(8,128)} %shard_map.103.cells_ref, f32[16,1,2,24,256]{4,3,2,1,0:T(8,128)} %copy-done.22, f32[16,1,2,24,256]{4,3,2,1,0:T(8,128)} %collective-permute-done.13.above_ref, f32[2,2,24,256]{3,2,1,0:T(8,128)} %bitcast.20, ...), custom_call_target="tpu_custom_call", output_to_operand_aliasing={{}: (5, {})} | custom-call | flops 196608 | bytes 196608 | tf_op jit(solution)/shard_map/pallas_call | solution.py:58
  96.1 5.1 %all-to-all-start = ((f32[4,16,2,24,128]{4,3,2,1,0:T(8,128)}), f32[4,16,2,24,128]{4,3,2,1,0:T(8,128)}, u32[]{:S(2)}, u32[]{:S(2)}) async-start(f32[4,16,2,24,128]{4,3,2,1,0:T(8,128)} %shard_map.107.split_ref), calls=%async_computation | async-start | bytes 3145728 | tf_op jit(solution)/shard_map/all_to_all | solution.py:414
  101.3 2.1 %shard_map.108 = f32[16,256]{1,0:T(8,128)S(1)} custom-call(s32[1]{0:T(128)} %bitcast.tile_ref, s32[256]{0:T(256)S(1)} %copy-done.4, s32[256]{0:T(256)S(1)} %copy-done.6, s32[256]{0:T(256)S(1)} %copy-done.7, s32[256]{0:T(256)S(1)} %copy-done.8, f32[16,2,2,24,256]{4,3,2,1,0:T(8,128)S(1)} %copy-done.2, f32[4,16,2,24,128]{4,3,2,1,0:T(8,128)S(1)} %copy-done.1), custom_call_target="tpu_custom_call" | custom-call | tf_op jit(solution)/shard_map/pallas_call | solution.py:122
  103.5 1.2 collective-permute-done.16
  104.7 3.7 %collective-permute-done.17 = f32[16,256]{1,0:T(8,128)S(1)} collective-permute-done((f32[16,256]{1,0:T(8,128)S(1)}, f32[16,256]{1,0:T(8,128)S(1)}, u32[]{:S(2)}, u32[]{:S(2)}) %collective-permute-start.17) | collective-permute-done | bytes 16416 | tf_op jit(solution)/shard_map/ppermute | solution.py:419
  108.4 4.7 %collective-permute-done.18 = f32[16,256]{1,0:T(8,128)S(1)} collective-permute-done((f32[16,256]{1,0:T(8,128)S(1)}, f32[16,256]{1,0:T(8,128)S(1)}, u32[]{:S(2)}, u32[]{:S(2)}) %collective-permute-start.18) | collective-permute-done | bytes 16416 | tf_op jit(solution)/shard_map/ppermute | solution.py:419
  113.5 7.3 %collective-permute-done.19 = f32[16,256]{1,0:T(8,128)S(1)} collective-permute-done((f32[16,256]{1,0:T(8,128)S(1)}, f32[16,256]{1,0:T(8,128)S(1)}, u32[]{:S(2)}, u32[]{:S(2)}) %collective-permute-start.19) | collective-permute-done | bytes 16416 | tf_op jit(solution)/shard_map/ppermute | solution.py:419
  120.9 3.6 %collective-permute-done.20 = f32[16,256]{1,0:T(8,128)S(1)} collective-permute-done((f32[16,256]{1,0:T(8,128)S(1)}, f32[16,256]{1,0:T(8,128)S(1)}, u32[]{:S(2)}, u32[]{:S(2)}) %collective-permute-start.20) | collective-permute-done | bytes 16416 | tf_op jit(solution)/shard_map/ppermute | solution.py:419
  124.7 5.1 %collective-permute-done.21 = f32[16,256]{1,0:T(8,128)S(1)} collective-permute-done((f32[16,256]{1,0:T(8,128)S(1)}, f32[16,256]{1,0:T(8,128)S(1)}, u32[]{:S(2)}, u32[]{:S(2)}) %collective-permute-start.21) | collective-permute-done | bytes 16416 | tf_op jit(solution)/shard_map/ppermute | solution.py:419
  129.9 2.9 %collective-permute-start.23 = (f32[16,256]{1,0:T(8,128)S(1)}, f32[16,256]{1,0:T(8,128)S(1)}, u32[]{:S(2)}, u32[]{:S(2)}) collective-permute-start(f32[16,256]{1,0:T(8,128)S(1)} %add.31.raw_0), channel_id=1, source_target_pairs={{0,2},{1,3},{2,0},{3,1},{4,6},{5,7},{6,4},{7,5},{8,10},{9,11},{10,... | collective-permute-start | bytes 49160 | tf_op jit(solution)/shard_map/ppermute | solution.py:420
  132.7 1.8 collective-permute-start.22
  134.5 0.9 collective-permute-done.23.raw_2
  135.4 1.3 collective-permute-done.22.raw_1
  136.8 24.5 %shard_map.109 = (bf16[512,512]{1,0:T(8,128)(2,1)S(1)}, bf16[512,512]{1,0:T(8,128)(2,1)S(1)}) custom-call(s32[4]{0:T(128)S(1)} %compare_select_fusion.order_ref, f32[256]{0:T(256)S(1)} %copy-done.9, f32[256]{0:T(256)S(1)} %copy-done.5, f32[256]{0:T(256)S(1)} %sqrt.3.root_ref, f32[16,256]{1,0:T(8,128)S(1)} %add.31.raw_0, ...), custom_call_target="tpu_custom_call" | custom-call | tf_op jit(solution)/shard_map/pallas_call | solution.py:252
  161.2 4.3 %shard_map.110 = f32[4,16,2,24,128]{4,3,2,1,0:T(8,128)} custom-call(bf16[512,512]{1,0:T(8,128)(2,1)S(1)} %get-tuple-element.16.high_ref, bf16[512,512]{1,0:T(8,128)(2,1)S(1)} %get-tuple-element.17.low_ref, f32[4,16,2,24,128]{4,3,2,1,0:T(8,128)} %all-to-all-done.cells_ref), custom_call_target="tpu_custom_call" | custom-call | tf_op jit(solution)/shard_map/pallas_call | solution.py:328
  165.5 5.9 %all-to-all-start.1 = ((f32[4,16,2,24,128]{4,3,2,1,0:T(8,128)}), f32[4,16,2,24,128]{4,3,2,1,0:T(8,128)S(1)}, u32[]{:S(2)}, u32[]{:S(2)}) async-start(f32[4,16,2,24,128]{4,3,2,1,0:T(8,128)} %shard_map.110), calls=%async_computation.1 | async-start | bytes 3145728 | tf_op jit(solution)/shard_map/all_to_all | solution.py:422
  171.4 2.8 %copy-done.3 = f32[64,2,2,24,256]{4,3,2,1,0:T(8,128)S(1)} copy-done((f32[64,2,2,24,256]{4,3,2,1,0:T(8,128)S(1)}, f32[64,2,2,24,256]{4,3,2,1,0:T(8,128)}, u32[]{:S(2)}) %copy-start.3) | copy-done | bytes 6291480
  174.2 3.3 %shard_map.111.sofar_ref = f32[16,4,24,2,256]{4,3,2,1,0:T(2,128)} custom-call(s32[1]{0:T(128)} %bitcast.5.mem_ref, bf16[512,512]{1,0:T(8,128)(2,1)S(1)} %get-tuple-element.16.high_ref, bf16[512,512]{1,0:T(8,128)(2,1)S(1)} %get-tuple-element.17.low_ref, f32[64,2,2,24,256]{4,3,2,1,0:T(8,128)S(1)} %copy-done.3), custom_call_target="tpu_custom_call" | custom-call | tf_op jit(solution)/shard_map/pallas_call | solution.py:303
  177.5 7.9 %all-to-all-done.1.back_ref = f32[4,16,2,24,128]{4,3,2,1,0:T(8,128)S(1)} async-done(((f32[4,16,2,24,128]{4,3,2,1,0:T(8,128)}), f32[4,16,2,24,128]{4,3,2,1,0:T(8,128)S(1)}, u32[]{:S(2)}, u32[]{:S(2)}) %all-to-all-start.1) | async-done | bytes 1572896 | tf_op jit(solution)/shard_map/all_to_all | solution.py:422
  185.5 1.2 copy-done.10
  186.7 2.9 %shard_map.112 = f32[16,4,24,2,256]{4,3,2,1,0:T(2,128)} custom-call(f32[4,16,2,24,128]{4,3,2,1,0:T(8,128)} %copy-done.10, f32[16,4,24,2,256]{4,3,2,1,0:T(2,128)} %shard_map.111.sofar_ref), custom_call_target="tpu_custom_call", output_to_operand_aliasing={{}: (1, {})} | custom-call | tf_op jit(solution)/shard_map/pallas_call | solution.py:349
  (91 shorter events, 3.1 us)
Async XLA Ops:
  6.5 106.6 %copy-start = (f32[64,256]{1,0:T(8,128)S(1)}, f32[64,256]{1,0:T(8,128)}, u32[]{:S(2)}) copy-start(f32[64,256]{1,0:T(8,128)} %param.19) | copy-start | bytes 196612
  6.5 164.9 %all-gather.2.cloned.1.call-start = ((), (), s32[]{:S(2)}) async-start(), calls=%async_computation.2 | async-start | bytes 7864320 | tf_op jit(solution)/shard_map/all_gather | solution.py:413
  8.8 23.8 %copy-start.23 = (f32[2,24,2,256]{3,2,1,0:T(2,128)S(1)}, f32[2,24,2,256]{3,2,1,0:T(2,128)}, u32[]{:S(2)}) copy-start(f32[2,24,2,256]{3,2,1,0:T(2,128)} %param.11) | copy-start | bytes 294916
  8.8 28.0 %copy-start.24 = (f32[4,24]{1,0:T(4,128)S(1)}, f32[4,24]{1,0:T(4,128)}, u32[]{:S(2)}) copy-start(f32[4,24]{1,0:T(4,128)} %param.12) | copy-start | bytes 1156
  9.1 28.4 %copy-start.14 = (f32[16,1,2,24,256]{4,3,2,1,0:T(8,128)}, f32[16,1,2,24,256]{4,3,2,1,0:T(8,128)S(1)}, u32[]{:S(2)}) copy-start(f32[16,1,2,24,256]{4,3,2,1,0:T(8,128)S(1)} %get-tuple-element.21.cells_ref) | copy-start | bytes 2359300
  9.1 31.5 %copy-start.11 = (f32[16,1,2,24,256]{4,3,2,1,0:T(8,128)}, f32[16,1,2,24,256]{4,3,2,1,0:T(8,128)S(1)}, u32[]{:S(2)}) copy-start(f32[16,1,2,24,256]{4,3,2,1,0:T(8,128)S(1)} %get-tuple-element.19.cells_ref) | copy-start | bytes 2359300
  9.1 31.5 %copy-start.12 = (f32[16,1,2,24,256]{4,3,2,1,0:T(8,128)}, f32[16,1,2,24,256]{4,3,2,1,0:T(8,128)S(1)}, u32[]{:S(2)}) copy-start(f32[16,1,2,24,256]{4,3,2,1,0:T(8,128)S(1)} %get-tuple-element.20.cells_ref) | copy-start | bytes 2359300
  9.1 31.5 %copy-start.13 = (f32[16,1,2,24,256]{4,3,2,1,0:T(8,128)}, f32[16,1,2,24,256]{4,3,2,1,0:T(8,128)S(1)}, u32[]{:S(2)}) copy-start(f32[16,1,2,24,256]{4,3,2,1,0:T(8,128)S(1)} %get-tuple-element.22.cells_ref) | copy-start | bytes 2359300
  9.1 17.3 %collective-permute-start.8 = (f32[16,1,2,24,256]{4,3,2,1,0:T(8,128)S(1)}, f32[16,1,2,24,256]{4,3,2,1,0:T(8,128)S(1)}, u32[]{:S(2)}, u32[]{:S(2)}) collective-permute-start(f32[16,1,2,24,256]{4,3,2,1,0:T(8,128)S(1)} %get-tuple-element.19.cells_ref), channel_id=1, source_target_pairs={{0,252},{4,0},{8,4},{12,8},{16,12},{20,16},{24,20},{28,24},{32,28}... | collective-permute-start | bytes 2359304 | tf_op jit(solution)/shard_map/ppermute | solution.py:395
  17.0 17.9 %collective-permute-start.4 = (f32[16,1,2,24,256]{4,3,2,1,0:T(8,128)S(1)}, f32[16,1,2,24,256]{4,3,2,1,0:T(8,128)S(1)}, u32[]{:S(2)}, u32[]{:S(2)}) collective-permute-start(f32[16,1,2,24,256]{4,3,2,1,0:T(8,128)S(1)} %get-tuple-element.21.cells_ref), channel_id=1, source_target_pairs={{0,252},{4,0},{8,4},{12,8},{16,12},{20,16},{24,20},{28,24},{32,28}... | collective-permute-start | bytes 2359304 | tf_op jit(solution)/shard_map/ppermute | solution.py:395
  17.6 17.3 %collective-permute-start.3 = (f32[16,1,2,24,256]{4,3,2,1,0:T(8,128)S(1)}, f32[16,1,2,24,256]{4,3,2,1,0:T(8,128)S(1)}, u32[]{:S(2)}, u32[]{:S(2)}) collective-permute-start(f32[16,1,2,24,256]{4,3,2,1,0:T(8,128)S(1)} %get-tuple-element.21.cells_ref), channel_id=1, source_target_pairs={{0,4},{4,8},{8,12},{12,16},{16,20},{20,24},{24,28},{28,32},{32,36}... | collective-permute-start | bytes 2359304 | tf_op jit(solution)/shard_map/ppermute | solution.py:395
  17.6 25.7 %collective-permute-start.1 = (f32[16,1,2,24,256]{4,3,2,1,0:T(8,128)S(1)}, f32[16,1,2,24,256]{4,3,2,1,0:T(8,128)}, u32[]{:S(2)}, u32[]{:S(2)}) collective-permute-start(f32[16,1,2,24,256]{4,3,2,1,0:T(8,128)S(1)} %get-tuple-element.22.cells_ref), channel_id=1, source_target_pairs={{0,252},{4,0},{8,4},{12,8},{16,12},{20,16},{24,20},{28,24},{32,28}... | collective-permute-start | bytes 2359304 | tf_op jit(solution)/shard_map/ppermute | solution.py:395
  22.7 26.0 %collective-permute-start = (f32[16,1,2,24,256]{4,3,2,1,0:T(8,128)S(1)}, f32[16,1,2,24,256]{4,3,2,1,0:T(8,128)}, u32[]{:S(2)}, u32[]{:S(2)}) collective-permute-start(f32[16,1,2,24,256]{4,3,2,1,0:T(8,128)S(1)} %get-tuple-element.22.cells_ref), channel_id=1, source_target_pairs={{0,4},{4,8},{8,12},{12,16},{16,20},{20,24},{24,28},{28,32},{32,36}... | collective-permute-start | bytes 2359304 | tf_op jit(solution)/shard_map/ppermute | solution.py:395
  27.3 24.5 %collective-permute-start.6 = (f32[16,1,2,24,256]{4,3,2,1,0:T(8,128)S(1)}, f32[16,1,2,24,256]{4,3,2,1,0:T(8,128)}, u32[]{:S(2)}, u32[]{:S(2)}) collective-permute-start(f32[16,1,2,24,256]{4,3,2,1,0:T(8,128)S(1)} %get-tuple-element.20.cells_ref), channel_id=1, source_target_pairs={{0,252},{4,0},{8,4},{12,8},{16,12},{20,16},{24,20},{28,24},{32,28}... | collective-permute-start | bytes 2359304 | tf_op jit(solution)/shard_map/ppermute | solution.py:395
  34.9 1.0 copy-start.16
  34.9 26.6 %collective-permute-start.7 = (f32[16,1,2,24,256]{4,3,2,1,0:T(8,128)S(1)}, f32[16,1,2,24,256]{4,3,2,1,0:T(8,128)}, u32[]{:S(2)}, u32[]{:S(2)}) collective-permute-start(f32[16,1,2,24,256]{4,3,2,1,0:T(8,128)S(1)} %get-tuple-element.19.cells_ref), channel_id=1, source_target_pairs={{0,4},{4,8},{8,12},{12,16},{16,20},{20,24},{24,28},{28,32},{32,36}... | collective-permute-start | bytes 2359304 | tf_op jit(solution)/shard_map/ppermute | solution.py:395
  35.9 22.4 %collective-permute-start.5 = (f32[16,1,2,24,256]{4,3,2,1,0:T(8,128)S(1)}, f32[16,1,2,24,256]{4,3,2,1,0:T(8,128)}, u32[]{:S(2)}, u32[]{:S(2)}) collective-permute-start(f32[16,1,2,24,256]{4,3,2,1,0:T(8,128)S(1)} %get-tuple-element.20.cells_ref), channel_id=1, source_target_pairs={{0,4},{4,8},{8,12},{12,16},{16,20},{20,24},{24,28},{28,32},{32,36}... | collective-permute-start | bytes 2359304 | tf_op jit(solution)/shard_map/ppermute | solution.py:395
  43.3 18.7 %collective-permute-start.11 = (f32[16,1,2,24,256]{4,3,2,1,0:T(8,128)}, f32[16,1,2,24,256]{4,3,2,1,0:T(8,128)S(1)}, u32[]{:S(2)}, u32[]{:S(2)}) collective-permute-start(f32[16,1,2,24,256]{4,3,2,1,0:T(8,128)} %shard_map.101.cells_ref), channel_id=1, source_target_pairs={{0,252},{4,0},{8,4},{12,8},{16,12},{20,16},{24,20},{28,24},{32,28}... | collective-permute-start | bytes 2359304 | tf_op jit(solution)/shard_map/ppermute | solution.py:395
  48.6 21.1 %collective-permute-start.10 = (f32[16,1,2,24,256]{4,3,2,1,0:T(8,128)}, f32[16,1,2,24,256]{4,3,2,1,0:T(8,128)S(1)}, u32[]{:S(2)}, u32[]{:S(2)}) collective-permute-start(f32[16,1,2,24,256]{4,3,2,1,0:T(8,128)} %shard_map.101.cells_ref), channel_id=1, source_target_pairs={{0,4},{4,8},{8,12},{12,16},{16,20},{20,24},{24,28},{28,32},{32,36}... | collective-permute-start | bytes 2359304 | tf_op jit(solution)/shard_map/ppermute | solution.py:395
  51.8 23.4 %collective-permute-start.2 = (f32[16,1,2,24,256]{4,3,2,1,0:T(8,128)}, f32[16,1,2,24,256]{4,3,2,1,0:T(8,128)}, u32[]{:S(2)}, u32[]{:S(2)}) collective-permute-start(f32[16,1,2,24,256]{4,3,2,1,0:T(8,128)} %shard_map.100.cells_ref), channel_id=1, source_target_pairs={{0,4},{4,8},{8,12},{12,16},{16,20},{20,24},{24,28},{28,32},{32,36}... | collective-permute-start | bytes 2359304 | tf_op jit(solution)/shard_map/ppermute | solution.py:395
  58.3 20.0 %collective-permute-start.9 = (f32[16,1,2,24,256]{4,3,2,1,0:T(8,128)}, f32[16,1,2,24,256]{4,3,2,1,0:T(8,128)S(1)}, u32[]{:S(2)}, u32[]{:S(2)}) collective-permute-start(f32[16,1,2,24,256]{4,3,2,1,0:T(8,128)} %shard_map.100.cells_ref), channel_id=1, source_target_pairs={{0,252},{4,0},{8,4},{12,8},{16,12},{20,16},{24,20},{28,24},{32,28}... | collective-permute-start | bytes 2359304 | tf_op jit(solution)/shard_map/ppermute | solution.py:395
  61.5 22.0 %collective-permute-start.14 = (f32[16,1,2,24,256]{4,3,2,1,0:T(8,128)}, f32[16,1,2,24,256]{4,3,2,1,0:T(8,128)S(1)}, u32[]{:S(2)}, u32[]{:S(2)}) collective-permute-start(f32[16,1,2,24,256]{4,3,2,1,0:T(8,128)} %shard_map.102.cells_ref), channel_id=1, source_target_pairs={{0,4},{4,8},{8,12},{12,16},{16,20},{20,24},{24,28},{28,32},{32,36}... | collective-permute-start | bytes 2359304 | tf_op jit(solution)/shard_map/ppermute | solution.py:395
  62.0 7.7 %copy-start.18 = (f32[16,1,2,24,256]{4,3,2,1,0:T(8,128)}, f32[16,1,2,24,256]{4,3,2,1,0:T(8,128)S(1)}, u32[]{:S(2)}) copy-start(f32[16,1,2,24,256]{4,3,2,1,0:T(8,128)S(1)} %collective-permute-done.11.above_ref) | copy-start | bytes 2359300
  62.0 21.5 %collective-permute-start.15 = (f32[16,1,2,24,256]{4,3,2,1,0:T(8,128)}, f32[16,1,2,24,256]{4,3,2,1,0:T(8,128)}, u32[]{:S(2)}, u32[]{:S(2)}) collective-permute-start(f32[16,1,2,24,256]{4,3,2,1,0:T(8,128)} %shard_map.102.cells_ref), channel_id=1, source_target_pairs={{0,252},{4,0},{8,4},{12,8},{16,12},{20,16},{24,20},{28,24},{32,28}... | collective-permute-start | bytes 2359304 | tf_op jit(solution)/shard_map/ppermute | solution.py:395
  69.7 5.5 %copy-start.19 = (f32[16,1,2,24,256]{4,3,2,1,0:T(8,128)}, f32[16,1,2,24,256]{4,3,2,1,0:T(8,128)S(1)}, u32[]{:S(2)}) copy-start(f32[16,1,2,24,256]{4,3,2,1,0:T(8,128)S(1)} %collective-permute-done.10.below_ref) | copy-start | bytes 2359300
  69.7 22.2 %collective-permute-start.12 = (f32[16,1,2,24,256]{4,3,2,1,0:T(8,128)}, f32[16,1,2,24,256]{4,3,2,1,0:T(8,128)S(1)}, u32[]{:S(2)}, u32[]{:S(2)}) collective-permute-start(f32[16,1,2,24,256]{4,3,2,1,0:T(8,128)} %shard_map.103.cells_ref), channel_id=1, source_target_pairs={{0,4},{4,8},{8,12},{12,16},{16,20},{20,24},{24,28},{28,32},{32,36}... | collective-permute-start | bytes 2359304 | tf_op jit(solution)/shard_map/ppermute | solution.py:395
  75.2 16.8 %collective-permute-start.13 = (f32[16,1,2,24,256]{4,3,2,1,0:T(8,128)}, f32[16,1,2,24,256]{4,3,2,1,0:T(8,128)}, u32[]{:S(2)}, u32[]{:S(2)}) collective-permute-start(f32[16,1,2,24,256]{4,3,2,1,0:T(8,128)} %shard_map.103.cells_ref), channel_id=1, source_target_pairs={{0,252},{4,0},{8,4},{12,8},{16,12},{20,16},{24,20},{28,24},{32,28}... | collective-permute-start | bytes 2359304 | tf_op jit(solution)/shard_map/ppermute | solution.py:395
  96.0 5.2 %copy-start.1 = (f32[4,16,2,24,128]{4,3,2,1,0:T(8,128)S(1)}, f32[4,16,2,24,128]{4,3,2,1,0:T(8,128)}, u32[]{:S(2)}) copy-start(f32[4,16,2,24,128]{4,3,2,1,0:T(8,128)} %shard_map.107.split_ref) | copy-start | bytes 4718596
  96.1 5.2 %copy-start.2 = (f32[16,2,2,24,256]{4,3,2,1,0:T(8,128)S(1)}, f32[16,2,2,24,256]{4,3,2,1,0:T(8,128)}, u32[]{:S(2)}) copy-start(f32[16,2,2,24,256]{4,3,2,1,0:T(8,128)} %shard_map.105.whole_ref) | copy-start | bytes 4718596
  96.1 5.2 %copy-start.4 = (s32[256]{0:T(256)S(1)}, s32[256]{0:T(256)}, u32[]{:S(2)}) copy-start(s32[256]{0:T(256)} %row_ref.1) | copy-start | bytes 3076
  96.1 5.2 %copy-start.6 = (s32[256]{0:T(256)S(1)}, s32[256]{0:T(256)}, u32[]{:S(2)}) copy-start(s32[256]{0:T(256)} %column_ref.1) | copy-start | bytes 3076
  96.1 5.2 %copy-start.7 = (s32[256]{0:T(256)S(1)}, s32[256]{0:T(256)}, u32[]{:S(2)}) copy-start(s32[256]{0:T(256)} %field_ref.1) | copy-start | bytes 3076
  96.1 5.2 %copy-start.8 = (s32[256]{0:T(256)S(1)}, s32[256]{0:T(256)}, u32[]{:S(2)}) copy-start(s32[256]{0:T(256)} %level_ref.1) | copy-start | bytes 3076
  96.1 65.1 %all-to-all-start = ((f32[4,16,2,24,128]{4,3,2,1,0:T(8,128)}), f32[4,16,2,24,128]{4,3,2,1,0:T(8,128)}, u32[]{:S(2)}, u32[]{:S(2)}) async-start(f32[4,16,2,24,128]{4,3,2,1,0:T(8,128)} %shard_map.107.split_ref), calls=%async_computation | async-start | bytes 3145728 | tf_op jit(solution)/shard_map/all_to_all | solution.py:414
  101.3 33.2 %copy-start.5 = (f32[256]{0:T(256)S(1)}, f32[256]{0:T(256)}, u32[]{:S(2)}) copy-start(f32[256]{0:T(256)} %err_ref.1) | copy-start | bytes 3076
  101.3 35.5 %copy-start.9 = (f32[256]{0:T(256)S(1)}, f32[256]{0:T(256)}, u32[]{:S(2)}) copy-start(f32[256]{0:T(256)} %obs_ref.1) | copy-start | bytes 3076
  103.4 1.2 collective-permute-start.16
  104.6 3.7 %collective-permute-start.17 = (f32[16,256]{1,0:T(8,128)S(1)}, f32[16,256]{1,0:T(8,128)S(1)}, u32[]{:S(2)}, u32[]{:S(2)}) collective-permute-start(f32[16,256]{1,0:T(8,128)S(1)} %add.26), channel_id=1, source_target_pairs={{0,8},{4,12},{8,0},{12,4},{16,24},{20,28},{24,16},{28,20},{32,40},... | collective-permute-start | bytes 49160 | tf_op jit(solution)/shard_map/ppermute | solution.py:419
  108.4 4.7 %collective-permute-start.18 = (f32[16,256]{1,0:T(8,128)S(1)}, f32[16,256]{1,0:T(8,128)S(1)}, u32[]{:S(2)}, u32[]{:S(2)}) collective-permute-start(f32[16,256]{1,0:T(8,128)S(1)} %add.27), channel_id=1, source_target_pairs={{0,16},{4,20},{8,24},{12,28},{16,0},{20,4},{24,8},{28,12},{32,48},... | collective-permute-start | bytes 49160 | tf_op jit(solution)/shard_map/ppermute | solution.py:419
  113.1 7.6 %collective-permute-start.19 = (f32[16,256]{1,0:T(8,128)S(1)}, f32[16,256]{1,0:T(8,128)S(1)}, u32[]{:S(2)}, u32[]{:S(2)}) collective-permute-start(f32[16,256]{1,0:T(8,128)S(1)} %add.28), channel_id=1, source_target_pairs={{0,32},{4,36},{8,40},{12,44},{16,48},{20,52},{24,56},{28,60},{32,0... | collective-permute-start | bytes 49160 | tf_op jit(solution)/shard_map/ppermute | solution.py:419
  120.8 3.7 %collective-permute-start.20 = (f32[16,256]{1,0:T(8,128)S(1)}, f32[16,256]{1,0:T(8,128)S(1)}, u32[]{:S(2)}, u32[]{:S(2)}) collective-permute-start(f32[16,256]{1,0:T(8,128)S(1)} %add.29), channel_id=1, source_target_pairs={{0,64},{4,68},{8,72},{12,76},{16,80},{20,84},{24,88},{28,92},{32,9... | collective-permute-start | bytes 49160 | tf_op jit(solution)/shard_map/ppermute | solution.py:419
  124.5 5.2 %collective-permute-start.21 = (f32[16,256]{1,0:T(8,128)S(1)}, f32[16,256]{1,0:T(8,128)S(1)}, u32[]{:S(2)}, u32[]{:S(2)}) collective-permute-start(f32[16,256]{1,0:T(8,128)S(1)} %add.30), channel_id=1, source_target_pairs={{0,128},{4,132},{8,136},{12,140},{16,144},{20,148},{24,152},{28,15... | collective-permute-start | bytes 49160 | tf_op jit(solution)/shard_map/ppermute | solution.py:419
  129.8 4.7 %collective-permute-start.24 = (f32[16,256]{1,0:T(8,128)S(1)}, f32[16,256]{1,0:T(8,128)S(1)}, u32[]{:S(2)}, u32[]{:S(2)}) collective-permute-start(f32[16,256]{1,0:T(8,128)S(1)} %add.31.raw_0), channel_id=1, source_target_pairs={{0,3},{1,0},{2,1},{3,2},{4,7},{5,4},{6,5},{7,6},{8,11},{9,8},{10,9... | collective-permute-start | bytes 49160 | tf_op jit(solution)/shard_map/ppermute | solution.py:420
  129.9 5.6 %collective-permute-start.23 = (f32[16,256]{1,0:T(8,128)S(1)}, f32[16,256]{1,0:T(8,128)S(1)}, u32[]{:S(2)}, u32[]{:S(2)}) collective-permute-start(f32[16,256]{1,0:T(8,128)S(1)} %add.31.raw_0), channel_id=1, source_target_pairs={{0,2},{1,3},{2,0},{3,1},{4,6},{5,7},{6,4},{7,5},{8,10},{9,11},{10,... | collective-permute-start | bytes 49160 | tf_op jit(solution)/shard_map/ppermute | solution.py:420
  132.7 4.1 %collective-permute-start.22 = (f32[16,256]{1,0:T(8,128)S(1)}, f32[16,256]{1,0:T(8,128)S(1)}, u32[]{:S(2)}, u32[]{:S(2)}) collective-permute-start(f32[16,256]{1,0:T(8,128)S(1)} %add.31.raw_0), channel_id=1, source_target_pairs={{0,1},{1,2},{2,3},{3,0},{4,5},{5,6},{6,7},{7,4},{8,9},{9,10},{10,1... | collective-permute-start | bytes 49160 | tf_op jit(solution)/shard_map/ppermute | solution.py:420
  165.5 20.0 %all-to-all-start.1 = ((f32[4,16,2,24,128]{4,3,2,1,0:T(8,128)}), f32[4,16,2,24,128]{4,3,2,1,0:T(8,128)S(1)}, u32[]{:S(2)}, u32[]{:S(2)}) async-start(f32[4,16,2,24,128]{4,3,2,1,0:T(8,128)} %shard_map.110), calls=%async_computation.1 | async-start | bytes 3145728 | tf_op jit(solution)/shard_map/all_to_all | solution.py:422
  171.4 2.8 %copy-start.3 = (f32[64,2,2,24,256]{4,3,2,1,0:T(8,128)S(1)}, f32[64,2,2,24,256]{4,3,2,1,0:T(8,128)}, u32[]{:S(2)}) copy-start(f32[64,2,2,24,256]{4,3,2,1,0:T(8,128)} %all-gather.2.cloned.1.call-done.cells_ref) | copy-start | bytes 18874372
  185.5 1.2 copy-start.10
  (5 other events, 4.5 us)
Sparse Core Ops, SparseCore 0:
  96.2 71.4 all-gather.1

commit v5 on v4

--- a/solution.py
+++ b/solution.py
@@ -233,13 +233,15 @@
     mine = whole[members:2 * members, :members]
     mine = mine + (iota(mine.shape, 0) == iota(mine.shape, 1)).astype(jnp.float32)
     tall, broad = high_ref.shape
-    down = (iota((tall, members), 0) // SUB == iota((tall, members), 1)).astype(jnp.float32)
-    over = (iota((members, broad), 1) // SUB == iota((members, broad), 0)).astype(jnp.float32)
-    spread = jnp.dot(jnp.dot(down, mine, precision=HI), over, precision=HI)
-    spread = jnp.where(iota((tall, broad), 0) % SUB == iota((tall, broad), 1) % SUB, spread, 0.0)
-    high = spread.astype(jnp.bfloat16)
-    high_ref[...] = high
-    low_ref[...] = (spread - high.astype(jnp.float32)).astype(jnp.bfloat16)
+    down = (iota((tall, members), 0) // SUB == iota((tall, members), 1)).astype(jnp.bfloat16)
+    over = (iota((members, broad), 1) // SUB == iota((members, broad), 0)).astype(jnp.bfloat16)
+    level = iota((tall, broad), 0) % SUB == iota((tall, broad), 1) % SUB
+    top = mine.astype(jnp.bfloat16)
+    rest = (mine - top.astype(jnp.float32)).astype(jnp.bfloat16)
+    for part, ref in ((top, high_ref), (rest, low_ref)):
+        rows = jnp.dot(down, part, preferred_element_type=jnp.float32).astype(jnp.bfloat16)
+        spread = jnp.dot(rows, over, preferred_element_type=jnp.float32)
+        ref[...] = jnp.where(level, spread, 0.0).astype(jnp.bfloat16)
 
 
 def run_filter(order, pieces, obs_value, obs_error, wide, group=64):

time: 197 us -> 196 us (level)
  transfers between devices with their start and end apart: 28 -> 28, of which waited for: 16 -> 16; matrix products, arithmetic and copies ran while one was open for 1% -> 1% of each run, Pallas kernels for 29% -> 28%
where the time goes in v5:
time: 196 us
  Pallas kernels  61.5 us (31%)
  waiting for transfers between devices  61.3 us (31%)
  starting transfers between devices  45.1 us (23%)
  between operations  13.7 us (7%)
  local copies, waits for them, and re-layouts  13.6 us (7%)
    ppermute x16, starting transfers between devices, shifted(): lax.ppermute(array, 'tile', [(i, (i + by) % tiles) for i in range(tiles)])  29.3 us
    ppermute x6, waiting for transfers between devices, on_device(): lax.ppermute(seen, 'tile', [(i, i ^ bit) for i in range(tiles)])  25.6 us
    ppermute x16, waiting for transfers between devices, shifted(): lax.ppermute(array, 'tile', [(i, (i + by) % tiles) for i in range(tiles)])  25.4 us
    pallas_call x8, Pallas kernels, forecast_step(): pl.pallas_call(functools.partial(step_kernel, split), grid=(count // part...  25.3 us
    pallas_call x1, Pallas kernels, run_filter(): pl.pallas_call(functools.partial(filter_kernel, members=members, group=gr...  23.6 us
    unnamed x52, local copies, waits for them, and re-layouts  12.4 us
    all_to_all x1, waiting for transfers between devices, on_device(): lax.all_to_all(update_piece(high, low, swapped), 'mem', 0, 0, tiled=True)  7.93 us
    all_to_all x1, starting transfers between devices, on_device(): lax.all_to_all(update_piece(high, low, swapped), 'mem', 0, 0, tiled=True)  5.91 us
  transfers between devices with their start and end apart: 28, of which 16 were waited for; matrix products, arithmetic and copies ran while one was open for 1% of the time, Pallas kernels for 28%

profile of v5, /device:TPU:2, one launch (start us, length us, event | category | flops | bytes accessed | tf_op | source)
XLA Modules:
  0.0 195.6 jit_solution(10877513010653170117)
XLA Ops:
  6.5 2.2 %copy.23 = f32[16,4,24,2,256]{4,2,3,1,0:T(8,128)S(1)} copy(f32[16,4,24,2,256]{4,3,2,1,0:T(2,128)} %param.10) | data formatting | bytes 6291456 | tf_op args[0]
  9.1 7.8 %collective-permute-start.8 = (f32[16,1,2,24,256]{4,3,2,1,0:T(8,128)S(1)}, f32[16,1,2,24,256]{4,3,2,1,0:T(8,128)S(1)}, u32[]{:S(2)}, u32[]{:S(2)}) collective-permute-start(f32[16,1,2,24,256]{4,3,2,1,0:T(8,128)S(1)} %get-tuple-element.19.cells_ref), channel_id=1, source_target_pairs={{0,252},{4,0},{8,4},{12,8},{16,12},{20,16},{24,20},{28,24},{32,28}... | collective-permute-start | bytes 2359304 | tf_op jit(solution)/shard_map/ppermute | solution.py:397
  17.6 5.1 %collective-permute-start.1 = (f32[16,1,2,24,256]{4,3,2,1,0:T(8,128)S(1)}, f32[16,1,2,24,256]{4,3,2,1,0:T(8,128)}, u32[]{:S(2)}, u32[]{:S(2)}) collective-permute-start(f32[16,1,2,24,256]{4,3,2,1,0:T(8,128)S(1)} %get-tuple-element.22.cells_ref), channel_id=1, source_target_pairs={{0,252},{4,0},{8,4},{12,8},{16,12},{20,16},{24,20},{28,24},{32,28}... | collective-permute-start | bytes 2359304 | tf_op jit(solution)/shard_map/ppermute | solution.py:397
  22.7 3.8 %collective-permute-done.8.above_ref = f32[16,1,2,24,256]{4,3,2,1,0:T(8,128)S(1)} collective-permute-done((f32[16,1,2,24,256]{4,3,2,1,0:T(8,128)S(1)}, f32[16,1,2,24,256]{4,3,2,1,0:T(8,128)S(1)}, u32[]{:S(2)}, u32[]{:S(2)}) %collective-permute-start.8) | collective-permute-done | bytes 786464 | tf_op jit(solution)/shard_map/ppermute | solution.py:397
  26.5 0.9 copy-done.15
  27.3 5.2 %collective-permute-start.6 = (f32[16,1,2,24,256]{4,3,2,1,0:T(8,128)S(1)}, f32[16,1,2,24,256]{4,3,2,1,0:T(8,128)}, u32[]{:S(2)}, u32[]{:S(2)}) collective-permute-start(f32[16,1,2,24,256]{4,3,2,1,0:T(8,128)S(1)} %get-tuple-element.20.cells_ref), channel_id=1, source_target_pairs={{0,252},{4,0},{8,4},{12,8},{16,12},{20,16},{24,20},{28,24},{32,28}... | collective-permute-start | bytes 2359304 | tf_op jit(solution)/shard_map/ppermute | solution.py:397
  33.2 1.7 collective-permute-done.4.above_ref
  34.9 1.0 copy-done.16
  35.9 0.9 copy-done.17
  36.8 0.7 broadcast_in_dim.8.spread_ref
  37.5 3.1 %shard_map.101.cells_ref = f32[16,1,2,24,256]{4,3,2,1,0:T(8,128)} custom-call(f32[16,1,2,24,256]{4,3,2,1,0:T(8,128)} %copy-done.14, f32[16,1,2,24,256]{4,3,2,1,0:T(8,128)} %copy-done.17, f32[16,1,2,24,256]{4,3,2,1,0:T(8,128)} %copy-done.16, f32[2,2,24,256]{3,2,1,0:T(8,128)} %bitcast.13, f32[4,24,256]{2,1,0:T(8,128)} %broadcast_in_dim.8.spread_ref), custom_call_target="tpu_custom_call" | custom-call | flops 196608 | bytes 196608 | tf_op jit(solution)/shard_map/pallas_call | solution.py:58
  40.7 2.7 %collective-permute-done.1.above_ref = f32[16,1,2,24,256]{4,3,2,1,0:T(8,128)} collective-permute-done((f32[16,1,2,24,256]{4,3,2,1,0:T(8,128)S(1)}, f32[16,1,2,24,256]{4,3,2,1,0:T(8,128)}, u32[]{:S(2)}, u32[]{:S(2)}) %collective-permute-start.1) | collective-permute-done | bytes 786464 | tf_op jit(solution)/shard_map/ppermute | solution.py:397
  43.3 5.3 %collective-permute-start.11 = (f32[16,1,2,24,256]{4,3,2,1,0:T(8,128)}, f32[16,1,2,24,256]{4,3,2,1,0:T(8,128)S(1)}, u32[]{:S(2)}, u32[]{:S(2)}) collective-permute-start(f32[16,1,2,24,256]{4,3,2,1,0:T(8,128)} %shard_map.101.cells_ref), channel_id=1, source_target_pairs={{0,252},{4,0},{8,4},{12,8},{16,12},{20,16},{24,20},{28,24},{32,28}... | collective-permute-start | bytes 2359304 | tf_op jit(solution)/shard_map/ppermute | solution.py:397
  48.7 3.2 %shard_map.100.cells_ref = f32[16,1,2,24,256]{4,3,2,1,0:T(8,128)} custom-call(f32[16,1,2,24,256]{4,3,2,1,0:T(8,128)} %copy-done.13, f32[16,1,2,24,256]{4,3,2,1,0:T(8,128)} %collective-permute-done.below_ref, f32[16,1,2,24,256]{4,3,2,1,0:T(8,128)} %collective-permute-done.1.above_ref, f32[2,2,24,256]{3,2,1,0:T(8,128)} %bitcast.14, ...), custom_call_target="tpu_custom_call" | custom-call | flops 196608 | bytes 196608 | tf_op jit(solution)/shard_map/pallas_call | solution.py:58
  51.8 6.5 %collective-permute-done.5.below_ref = f32[16,1,2,24,256]{4,3,2,1,0:T(8,128)} collective-permute-done((f32[16,1,2,24,256]{4,3,2,1,0:T(8,128)S(1)}, f32[16,1,2,24,256]{4,3,2,1,0:T(8,128)}, u32[]{:S(2)}, u32[]{:S(2)}) %collective-permute-start.5) | collective-permute-done | bytes 786464 | tf_op jit(solution)/shard_map/ppermute | solution.py:397
  58.3 3.2 %shard_map.102.cells_ref = f32[16,1,2,24,256]{4,3,2,1,0:T(8,128)} custom-call(f32[16,1,2,24,256]{4,3,2,1,0:T(8,128)} %copy-done.12, f32[16,1,2,24,256]{4,3,2,1,0:T(8,128)} %collective-permute-done.5.below_ref, f32[16,1,2,24,256]{4,3,2,1,0:T(8,128)} %collective-permute-done.6.above_ref, f32[2,2,24,256]{3,2,1,0:T(8,128)} %bitcast.15, ...), custom_call_target="tpu_custom_call" | custom-call | flops 196608 | bytes 196608 | tf_op jit(solution)/shard_map/pallas_call | solution.py:58
  62.0 4.6 %collective-permute-start.15 = (f32[16,1,2,24,256]{4,3,2,1,0:T(8,128)}, f32[16,1,2,24,256]{4,3,2,1,0:T(8,128)}, u32[]{:S(2)}, u32[]{:S(2)}) collective-permute-start(f32[16,1,2,24,256]{4,3,2,1,0:T(8,128)} %shard_map.102.cells_ref), channel_id=1, source_target_pairs={{0,252},{4,0},{8,4},{12,8},{16,12},{20,16},{24,20},{28,24},{32,28}... | collective-permute-start | bytes 2359304 | tf_op jit(solution)/shard_map/ppermute | solution.py:397
  66.6 3.1 %shard_map.103.cells_ref = f32[16,1,2,24,256]{4,3,2,1,0:T(8,128)} custom-call(f32[16,1,2,24,256]{4,3,2,1,0:T(8,128)} %copy-done.11, f32[16,1,2,24,256]{4,3,2,1,0:T(8,128)} %collective-permute-done.7.below_ref, f32[16,1,2,24,256]{4,3,2,1,0:T(8,128)} %copy-done.15, f32[2,2,24,256]{3,2,1,0:T(8,128)} %bitcast.16, f32[4,24,256]{2,1,0:T(8,128)} %broadcast_in_dim.8.spread_ref), custom_call_target="tpu_custom_call" | custom-call | flops 196608 | bytes 196608 | tf_op jit(solution)/shard_map/pallas_call | solution.py:58
  69.8 5.4 %collective-permute-done.2.below_ref = f32[16,1,2,24,256]{4,3,2,1,0:T(8,128)} collective-permute-done((f32[16,1,2,24,256]{4,3,2,1,0:T(8,128)}, f32[16,1,2,24,256]{4,3,2,1,0:T(8,128)}, u32[]{:S(2)}, u32[]{:S(2)}) %collective-permute-start.2) | collective-permute-done | bytes 786464 | tf_op jit(solution)/shard_map/ppermute | solution.py:397
  75.2 3.1 %shard_map.104.refs_0_ = f32[16,2,2,24,256]{4,3,2,1,0:T(8,128)} custom-call(f32[16,1,2,24,256]{4,3,2,1,0:T(8,128)} %shard_map.101.cells_ref, f32[16,1,2,24,256]{4,3,2,1,0:T(8,128)} %copy-done.19, f32[16,1,2,24,256]{4,3,2,1,0:T(8,128)} %copy-done.18, f32[2,2,24,256]{3,2,1,0:T(8,128)} %bitcast.17, f32[4,24,256]{2,1,0:T(8,128)} %broadcast_in_dim.8.spread_ref), custom_call_target="tpu_custom_call" | custom-call | flops 196608 | bytes 196608 | tf_op jit(solution)/shard_map/pallas_call | solution.py:58
  78.3 0.9 copy-done.21
  79.2 3.1 %shard_map.105.whole_ref = f32[16,2,2,24,256]{4,3,2,1,0:T(8,128)} custom-call(f32[16,1,2,24,256]{4,3,2,1,0:T(8,128)} %shard_map.100.cells_ref, f32[16,1,2,24,256]{4,3,2,1,0:T(8,128)} %collective-permute-done.2.below_ref, f32[16,1,2,24,256]{4,3,2,1,0:T(8,128)} %copy-done.21, f32[2,2,24,256]{3,2,1,0:T(8,128)} %bitcast.18, ...), custom_call_target="tpu_custom_call", output_to_operand_aliasing={{}: (5, {})} | custom-call | flops 196608 | bytes 196608 | tf_op jit(solution)/shard_map/pallas_call | solution.py:58
  82.4 1.1 collective-permute-done.14.below_ref
  83.5 0.9 copy-done.20
  84.4 3.2 %shard_map.106.refs_0_ = f32[4,16,2,24,128]{4,3,2,1,0:T(8,128)} custom-call(f32[16,1,2,24,256]{4,3,2,1,0:T(8,128)} %shard_map.102.cells_ref, f32[16,1,2,24,256]{4,3,2,1,0:T(8,128)} %copy-done.20, f32[16,1,2,24,256]{4,3,2,1,0:T(8,128)} %collective-permute-done.15.above_ref, f32[2,2,24,256]{3,2,1,0:T(8,128)} %bitcast.19, f32[4,24,256]{2,1,0:T(8,128)} %broadcast_in_dim.8.spread_ref), custom_call_target="tpu_custom_call" | custom-call | flops 196608 | bytes 196608 | tf_op jit(solution)/shard_map/pallas_call | solution.py:58
  87.6 4.3 %collective-permute-done.12.below_ref = f32[16,1,2,24,256]{4,3,2,1,0:T(8,128)S(1)} collective-permute-done((f32[16,1,2,24,256]{4,3,2,1,0:T(8,128)}, f32[16,1,2,24,256]{4,3,2,1,0:T(8,128)S(1)}, u32[]{:S(2)}, u32[]{:S(2)}) %collective-permute-start.12) | collective-permute-done | bytes 786464 | tf_op jit(solution)/shard_map/ppermute | solution.py:397
  91.9 0.9 copy-done.22
  92.8 3.2 %shard_map.107.split_ref = f32[4,16,2,24,128]{4,3,2,1,0:T(8,128)} custom-call(f32[16,1,2,24,256]{4,3,2,1,0:T(8,128)} %shard_map.103.cells_ref, f32[16,1,2,24,256]{4,3,2,1,0:T(8,128)} %copy-done.22, f32[16,1,2,24,256]{4,3,2,1,0:T(8,128)} %collective-permute-done.13.above_ref, f32[2,2,24,256]{3,2,1,0:T(8,128)} %bitcast.20, ...), custom_call_target="tpu_custom_call", output_to_operand_aliasing={{}: (5, {})} | custom-call | flops 196608 | bytes 196608 | tf_op jit(solution)/shard_map/pallas_call | solution.py:58
  96.1 5.1 %all-to-all-start = ((f32[4,16,2,24,128]{4,3,2,1,0:T(8,128)}), f32[4,16,2,24,128]{4,3,2,1,0:T(8,128)}, u32[]{:S(2)}, u32[]{:S(2)}) async-start(f32[4,16,2,24,128]{4,3,2,1,0:T(8,128)} %shard_map.107.split_ref), calls=%async_computation | async-start | bytes 3145728 | tf_op jit(solution)/shard_map/all_to_all | solution.py:416
  101.3 2.1 %shard_map.108 = f32[16,256]{1,0:T(8,128)S(1)} custom-call(s32[1]{0:T(128)} %bitcast.tile_ref, s32[256]{0:T(256)S(1)} %copy-done.4, s32[256]{0:T(256)S(1)} %copy-done.6, s32[256]{0:T(256)S(1)} %copy-done.7, s32[256]{0:T(256)S(1)} %copy-done.8, f32[16,2,2,24,256]{4,3,2,1,0:T(8,128)S(1)} %copy-done.2, f32[4,16,2,24,128]{4,3,2,1,0:T(8,128)S(1)} %copy-done.1), custom_call_target="tpu_custom_call" | custom-call | tf_op jit(solution)/shard_map/pallas_call | solution.py:122
  103.5 1.2 collective-permute-done.16
  104.6 3.7 %collective-permute-done.17 = f32[16,256]{1,0:T(8,128)S(1)} collective-permute-done((f32[16,256]{1,0:T(8,128)S(1)}, f32[16,256]{1,0:T(8,128)S(1)}, u32[]{:S(2)}, u32[]{:S(2)}) %collective-permute-start.17) | collective-permute-done | bytes 16416 | tf_op jit(solution)/shard_map/ppermute | solution.py:421
  108.4 4.7 %collective-permute-done.18 = f32[16,256]{1,0:T(8,128)S(1)} collective-permute-done((f32[16,256]{1,0:T(8,128)S(1)}, f32[16,256]{1,0:T(8,128)S(1)}, u32[]{:S(2)}, u32[]{:S(2)}) %collective-permute-start.18) | collective-permute-done | bytes 16416 | tf_op jit(solution)/shard_map/ppermute | solution.py:421
  113.5 7.3 %collective-permute-done.19 = f32[16,256]{1,0:T(8,128)S(1)} collective-permute-done((f32[16,256]{1,0:T(8,128)S(1)}, f32[16,256]{1,0:T(8,128)S(1)}, u32[]{:S(2)}, u32[]{:S(2)}) %collective-permute-start.19) | collective-permute-done | bytes 16416 | tf_op jit(solution)/shard_map/ppermute | solution.py:421
  120.9 3.6 %collective-permute-done.20 = f32[16,256]{1,0:T(8,128)S(1)} collective-permute-done((f32[16,256]{1,0:T(8,128)S(1)}, f32[16,256]{1,0:T(8,128)S(1)}, u32[]{:S(2)}, u32[]{:S(2)}) %collective-permute-start.20) | collective-permute-done | bytes 16416 | tf_op jit(solution)/shard_map/ppermute | solution.py:421
  124.7 5.1 %collective-permute-done.21 = f32[16,256]{1,0:T(8,128)S(1)} collective-permute-done((f32[16,256]{1,0:T(8,128)S(1)}, f32[16,256]{1,0:T(8,128)S(1)}, u32[]{:S(2)}, u32[]{:S(2)}) %collective-permute-start.21) | collective-permute-done | bytes 16416 | tf_op jit(solution)/shard_map/ppermute | solution.py:421
  129.8 2.9 %collective-permute-start.23 = (f32[16,256]{1,0:T(8,128)S(1)}, f32[16,256]{1,0:T(8,128)S(1)}, u32[]{:S(2)}, u32[]{:S(2)}) collective-permute-start(f32[16,256]{1,0:T(8,128)S(1)} %add.31.raw_0), channel_id=1, source_target_pairs={{0,2},{1,3},{2,0},{3,1},{4,6},{5,7},{6,4},{7,5},{8,10},{9,11},{10,... | collective-permute-start | bytes 49160 | tf_op jit(solution)/shard_map/ppermute | solution.py:422
  132.7 1.8 collective-permute-start.22
  134.5 0.9 collective-permute-done.23.raw_2
  135.4 1.3 collective-permute-done.22.raw_1
  136.8 23.6 %shard_map.109 = (bf16[512,512]{1,0:T(8,128)(2,1)S(1)}, bf16[512,512]{1,0:T(8,128)(2,1)S(1)}) custom-call(s32[4]{0:T(128)S(1)} %compare_select_fusion.order_ref, f32[256]{0:T(256)S(1)} %copy-done.9, f32[256]{0:T(256)S(1)} %copy-done.5, f32[256]{0:T(256)S(1)} %sqrt.3.root_ref, f32[16,256]{1,0:T(8,128)S(1)} %add.31.raw_0, ...), custom_call_target="tpu_custom_call" | custom-call | tf_op jit(solution)/shard_map/pallas_call | solution.py:254
  160.4 4.3 %shard_map.110 = f32[4,16,2,24,128]{4,3,2,1,0:T(8,128)} custom-call(bf16[512,512]{1,0:T(8,128)(2,1)S(1)} %get-tuple-element.16.high_ref, bf16[512,512]{1,0:T(8,128)(2,1)S(1)} %get-tuple-element.17.low_ref, f32[4,16,2,24,128]{4,3,2,1,0:T(8,128)} %all-to-all-done.cells_ref), custom_call_target="tpu_custom_call" | custom-call | tf_op jit(solution)/shard_map/pallas_call | solution.py:330
  164.7 5.9 %all-to-all-start.1 = ((f32[4,16,2,24,128]{4,3,2,1,0:T(8,128)}), f32[4,16,2,24,128]{4,3,2,1,0:T(8,128)S(1)}, u32[]{:S(2)}, u32[]{:S(2)}) async-start(f32[4,16,2,24,128]{4,3,2,1,0:T(8,128)} %shard_map.110), calls=%async_computation.1 | async-start | bytes 3145728 | tf_op jit(solution)/shard_map/all_to_all | solution.py:424
  170.6 2.8 %copy-done.3 = f32[64,2,2,24,256]{4,3,2,1,0:T(8,128)S(1)} copy-done((f32[64,2,2,24,256]{4,3,2,1,0:T(8,128)S(1)}, f32[64,2,2,24,256]{4,3,2,1,0:T(8,128)}, u32[]{:S(2)}) %copy-start.3) | copy-done | bytes 6291480
  173.4 3.3 %shard_map.111.sofar_ref = f32[16,4,24,2,256]{4,3,2,1,0:T(2,128)} custom-call(s32[1]{0:T(128)} %bitcast.5.mem_ref, bf16[512,512]{1,0:T(8,128)(2,1)S(1)} %get-tuple-element.16.high_ref, bf16[512,512]{1,0:T(8,128)(2,1)S(1)} %get-tuple-element.17.low_ref, f32[64,2,2,24,256]{4,3,2,1,0:T(8,128)S(1)} %copy-done.3), custom_call_target="tpu_custom_call" | custom-call | tf_op jit(solution)/shard_map/pallas_call | solution.py:305
  176.7 7.9 %all-to-all-done.1.back_ref = f32[4,16,2,24,128]{4,3,2,1,0:T(8,128)S(1)} async-done(((f32[4,16,2,24,128]{4,3,2,1,0:T(8,128)}), f32[4,16,2,24,128]{4,3,2,1,0:T(8,128)S(1)}, u32[]{:S(2)}, u32[]{:S(2)}) %all-to-all-start.1) | async-done | bytes 1572896 | tf_op jit(solution)/shard_map/all_to_all | solution.py:424
  184.7 1.2 copy-done.10
  185.8 2.9 %shard_map.112 = f32[16,4,24,2,256]{4,3,2,1,0:T(2,128)} custom-call(f32[4,16,2,24,128]{4,3,2,1,0:T(8,128)} %copy-done.10, f32[16,4,24,2,256]{4,3,2,1,0:T(2,128)} %shard_map.111.sofar_ref), custom_call_target="tpu_custom_call", output_to_operand_aliasing={{}: (1, {})} | custom-call | tf_op jit(solution)/shard_map/pallas_call | solution.py:351
  (91 shorter events, 3.1 us)
Async XLA Ops:
  6.5 106.6 %copy-start = (f32[64,256]{1,0:T(8,128)S(1)}, f32[64,256]{1,0:T(8,128)}, u32[]{:S(2)}) copy-start(f32[64,256]{1,0:T(8,128)} %param.19) | copy-start | bytes 196612
  6.5 164.1 %all-gather.2.cloned.1.call-start = ((), (), s32[]{:S(2)}) async-start(), calls=%async_computation.2 | async-start | bytes 7864320 | tf_op jit(solution)/shard_map/all_gather | solution.py:415
  8.8 23.8 %copy-start.23 = (f32[2,24,2,256]{3,2,1,0:T(2,128)S(1)}, f32[2,24,2,256]{3,2,1,0:T(2,128)}, u32[]{:S(2)}) copy-start(f32[2,24,2,256]{3,2,1,0:T(2,128)} %param.11) | copy-start | bytes 294916
  8.8 28.0 %copy-start.24 = (f32[4,24]{1,0:T(4,128)S(1)}, f32[4,24]{1,0:T(4,128)}, u32[]{:S(2)}) copy-start(f32[4,24]{1,0:T(4,128)} %param.12) | copy-start | bytes 1156
  9.1 28.4 %copy-start.14 = (f32[16,1,2,24,256]{4,3,2,1,0:T(8,128)}, f32[16,1,2,24,256]{4,3,2,1,0:T(8,128)S(1)}, u32[]{:S(2)}) copy-start(f32[16,1,2,24,256]{4,3,2,1,0:T(8,128)S(1)} %get-tuple-element.21.cells_ref) | copy-start | bytes 2359300
  9.1 31.5 %copy-start.11 = (f32[16,1,2,24,256]{4,3,2,1,0:T(8,128)}, f32[16,1,2,24,256]{4,3,2,1,0:T(8,128)S(1)}, u32[]{:S(2)}) copy-start(f32[16,1,2,24,256]{4,3,2,1,0:T(8,128)S(1)} %get-tuple-element.19.cells_ref) | copy-start | bytes 2359300
  9.1 31.5 %copy-start.12 = (f32[16,1,2,24,256]{4,3,2,1,0:T(8,128)}, f32[16,1,2,24,256]{4,3,2,1,0:T(8,128)S(1)}, u32[]{:S(2)}) copy-start(f32[16,1,2,24,256]{4,3,2,1,0:T(8,128)S(1)} %get-tuple-element.20.cells_ref) | copy-start | bytes 2359300
  9.1 31.5 %copy-start.13 = (f32[16,1,2,24,256]{4,3,2,1,0:T(8,128)}, f32[16,1,2,24,256]{4,3,2,1,0:T(8,128)S(1)}, u32[]{:S(2)}) copy-start(f32[16,1,2,24,256]{4,3,2,1,0:T(8,128)S(1)} %get-tuple-element.22.cells_ref) | copy-start | bytes 2359300
  9.1 17.3 %collective-permute-start.8 = (f32[16,1,2,24,256]{4,3,2,1,0:T(8,128)S(1)}, f32[16,1,2,24,256]{4,3,2,1,0:T(8,128)S(1)}, u32[]{:S(2)}, u32[]{:S(2)}) collective-permute-start(f32[16,1,2,24,256]{4,3,2,1,0:T(8,128)S(1)} %get-tuple-element.19.cells_ref), channel_id=1, source_target_pairs={{0,252},{4,0},{8,4},{12,8},{16,12},{20,16},{24,20},{28,24},{32,28}... | collective-permute-start | bytes 2359304 | tf_op jit(solution)/shard_map/ppermute | solution.py:397
  17.0 17.9 %collective-permute-start.4 = (f32[16,1,2,24,256]{4,3,2,1,0:T(8,128)S(1)}, f32[16,1,2,24,256]{4,3,2,1,0:T(8,128)S(1)}, u32[]{:S(2)}, u32[]{:S(2)}) collective-permute-start(f32[16,1,2,24,256]{4,3,2,1,0:T(8,128)S(1)} %get-tuple-element.21.cells_ref), channel_id=1, source_target_pairs={{0,252},{4,0},{8,4},{12,8},{16,12},{20,16},{24,20},{28,24},{32,28}... | collective-permute-start | bytes 2359304 | tf_op jit(solution)/shard_map/ppermute | solution.py:397
  17.6 17.3 %collective-permute-start.3 = (f32[16,1,2,24,256]{4,3,2,1,0:T(8,128)S(1)}, f32[16,1,2,24,256]{4,3,2,1,0:T(8,128)S(1)}, u32[]{:S(2)}, u32[]{:S(2)}) collective-permute-start(f32[16,1,2,24,256]{4,3,2,1,0:T(8,128)S(1)} %get-tuple-element.21.cells_ref), channel_id=1, source_target_pairs={{0,4},{4,8},{8,12},{12,16},{16,20},{20,24},{24,28},{28,32},{32,36}... | collective-permute-start | bytes 2359304 | tf_op jit(solution)/shard_map/ppermute | solution.py:397
  17.6 25.7 %collective-permute-start.1 = (f32[16,1,2,24,256]{4,3,2,1,0:T(8,128)S(1)}, f32[16,1,2,24,256]{4,3,2,1,0:T(8,128)}, u32[]{:S(2)}, u32[]{:S(2)}) collective-permute-start(f32[16,1,2,24,256]{4,3,2,1,0:T(8,128)S(1)} %get-tuple-element.22.cells_ref), channel_id=1, source_target_pairs={{0,252},{4,0},{8,4},{12,8},{16,12},{20,16},{24,20},{28,24},{32,28}... | collective-permute-start | bytes 2359304 | tf_op jit(solution)/shard_map/ppermute | solution.py:397
  22.7 26.0 %collective-permute-start = (f32[16,1,2,24,256]{4,3,2,1,0:T(8,128)S(1)}, f32[16,1,2,24,256]{4,3,2,1,0:T(8,128)}, u32[]{:S(2)}, u32[]{:S(2)}) collective-permute-start(f32[16,1,2,24,256]{4,3,2,1,0:T(8,128)S(1)} %get-tuple-element.22.cells_ref), channel_id=1, source_target_pairs={{0,4},{4,8},{8,12},{12,16},{16,20},{20,24},{24,28},{28,32},{32,36}... | collective-permute-start | bytes 2359304 | tf_op jit(solution)/shard_map/ppermute | solution.py:397
  27.3 24.5 %collective-permute-start.6 = (f32[16,1,2,24,256]{4,3,2,1,0:T(8,128)S(1)}, f32[16,1,2,24,256]{4,3,2,1,0:T(8,128)}, u32[]{:S(2)}, u32[]{:S(2)}) collective-permute-start(f32[16,1,2,24,256]{4,3,2,1,0:T(8,128)S(1)} %get-tuple-element.20.cells_ref), channel_id=1, source_target_pairs={{0,252},{4,0},{8,4},{12,8},{16,12},{20,16},{24,20},{28,24},{32,28}... | collective-permute-start | bytes 2359304 | tf_op jit(solution)/shard_map/ppermute | solution.py:397
  34.9 1.0 copy-start.16
  34.9 26.6 %collective-permute-start.7 = (f32[16,1,2,24,256]{4,3,2,1,0:T(8,128)S(1)}, f32[16,1,2,24,256]{4,3,2,1,0:T(8,128)}, u32[]{:S(2)}, u32[]{:S(2)}) collective-permute-start(f32[16,1,2,24,256]{4,3,2,1,0:T(8,128)S(1)} %get-tuple-element.19.cells_ref), channel_id=1, source_target_pairs={{0,4},{4,8},{8,12},{12,16},{16,20},{20,24},{24,28},{28,32},{32,36}... | collective-permute-start | bytes 2359304 | tf_op jit(solution)/shard_map/ppermute | solution.py:397
  35.9 22.4 %collective-permute-start.5 = (f32[16,1,2,24,256]{4,3,2,1,0:T(8,128)S(1)}, f32[16,1,2,24,256]{4,3,2,1,0:T(8,128)}, u32[]{:S(2)}, u32[]{:S(2)}) collective-permute-start(f32[16,1,2,24,256]{4,3,2,1,0:T(8,128)S(1)} %get-tuple-element.20.cells_ref), channel_id=1, source_target_pairs={{0,4},{4,8},{8,12},{12,16},{16,20},{20,24},{24,28},{28,32},{32,36}... | collective-permute-start | bytes 2359304 | tf_op jit(solution)/shard_map/ppermute | solution.py:397
  43.3 18.7 %collective-permute-start.11 = (f32[16,1,2,24,256]{4,3,2,1,0:T(8,128)}, f32[16,1,2,24,256]{4,3,2,1,0:T(8,128)S(1)}, u32[]{:S(2)}, u32[]{:S(2)}) collective-permute-start(f32[16,1,2,24,256]{4,3,2,1,0:T(8,128)} %shard_map.101.cells_ref), channel_id=1, source_target_pairs={{0,252},{4,0},{8,4},{12,8},{16,12},{20,16},{24,20},{28,24},{32,28}... | collective-permute-start | bytes 2359304 | tf_op jit(solution)/shard_map/ppermute | solution.py:397
  48.6 21.1 %collective-permute-start.10 = (f32[16,1,2,24,256]{4,3,2,1,0:T(8,128)}, f32[16,1,2,24,256]{4,3,2,1,0:T(8,128)S(1)}, u32[]{:S(2)}, u32[]{:S(2)}) collective-permute-start(f32[16,1,2,24,256]{4,3,2,1,0:T(8,128)} %shard_map.101.cells_ref), channel_id=1, source_target_pairs={{0,4},{4,8},{8,12},{12,16},{16,20},{20,24},{24,28},{28,32},{32,36}... | collective-permute-start | bytes 2359304 | tf_op jit(solution)/shard_map/ppermute | solution.py:397
  51.8 23.4 %collective-permute-start.2 = (f32[16,1,2,24,256]{4,3,2,1,0:T(8,128)}, f32[16,1,2,24,256]{4,3,2,1,0:T(8,128)}, u32[]{:S(2)}, u32[]{:S(2)}) collective-permute-start(f32[16,1,2,24,256]{4,3,2,1,0:T(8,128)} %shard_map.100.cells_ref), channel_id=1, source_target_pairs={{0,4},{4,8},{8,12},{12,16},{16,20},{20,24},{24,28},{28,32},{32,36}... | collective-permute-start | bytes 2359304 | tf_op jit(solution)/shard_map/ppermute | solution.py:397
  58.3 20.0 %collective-permute-start.9 = (f32[16,1,2,24,256]{4,3,2,1,0:T(8,128)}, f32[16,1,2,24,256]{4,3,2,1,0:T(8,128)S(1)}, u32[]{:S(2)}, u32[]{:S(2)}) collective-permute-start(f32[16,1,2,24,256]{4,3,2,1,0:T(8,128)} %shard_map.100.cells_ref), channel_id=1, source_target_pairs={{0,252},{4,0},{8,4},{12,8},{16,12},{20,16},{24,20},{28,24},{32,28}... | collective-permute-start | bytes 2359304 | tf_op jit(solution)/shard_map/ppermute | solution.py:397
  61.5 22.0 %collective-permute-start.14 = (f32[16,1,2,24,256]{4,3,2,1,0:T(8,128)}, f32[16,1,2,24,256]{4,3,2,1,0:T(8,128)S(1)}, u32[]{:S(2)}, u32[]{:S(2)}) collective-permute-start(f32[16,1,2,24,256]{4,3,2,1,0:T(8,128)} %shard_map.102.cells_ref), channel_id=1, source_target_pairs={{0,4},{4,8},{8,12},{12,16},{16,20},{20,24},{24,28},{28,32},{32,36}... | collective-permute-start | bytes 2359304 | tf_op jit(solution)/shard_map/ppermute | solution.py:397
  62.0 7.7 %copy-start.18 = (f32[16,1,2,24,256]{4,3,2,1,0:T(8,128)}, f32[16,1,2,24,256]{4,3,2,1,0:T(8,128)S(1)}, u32[]{:S(2)}) copy-start(f32[16,1,2,24,256]{4,3,2,1,0:T(8,128)S(1)} %collective-permute-done.11.above_ref) | copy-start | bytes 2359300
  62.0 21.5 %collective-permute-start.15 = (f32[16,1,2,24,256]{4,3,2,1,0:T(8,128)}, f32[16,1,2,24,256]{4,3,2,1,0:T(8,128)}, u32[]{:S(2)}, u32[]{:S(2)}) collective-permute-start(f32[16,1,2,24,256]{4,3,2,1,0:T(8,128)} %shard_map.102.cells_ref), channel_id=1, source_target_pairs={{0,252},{4,0},{8,4},{12,8},{16,12},{20,16},{24,20},{28,24},{32,28}... | collective-permute-start | bytes 2359304 | tf_op jit(solution)/shard_map/ppermute | solution.py:397
  69.7 5.5 %copy-start.19 = (f32[16,1,2,24,256]{4,3,2,1,0:T(8,128)}, f32[16,1,2,24,256]{4,3,2,1,0:T(8,128)S(1)}, u32[]{:S(2)}) copy-start(f32[16,1,2,24,256]{4,3,2,1,0:T(8,128)S(1)} %collective-permute-done.10.below_ref) | copy-start | bytes 2359300
  69.7 22.2 %collective-permute-start.12 = (f32[16,1,2,24,256]{4,3,2,1,0:T(8,128)}, f32[16,1,2,24,256]{4,3,2,1,0:T(8,128)S(1)}, u32[]{:S(2)}, u32[]{:S(2)}) collective-permute-start(f32[16,1,2,24,256]{4,3,2,1,0:T(8,128)} %shard_map.103.cells_ref), channel_id=1, source_target_pairs={{0,4},{4,8},{8,12},{12,16},{16,20},{20,24},{24,28},{28,32},{32,36}... | collective-permute-start | bytes 2359304 | tf_op jit(solution)/shard_map/ppermute | solution.py:397
  75.2 16.8 %collective-permute-start.13 = (f32[16,1,2,24,256]{4,3,2,1,0:T(8,128)}, f32[16,1,2,24,256]{4,3,2,1,0:T(8,128)}, u32[]{:S(2)}, u32[]{:S(2)}) collective-permute-start(f32[16,1,2,24,256]{4,3,2,1,0:T(8,128)} %shard_map.103.cells_ref), channel_id=1, source_target_pairs={{0,252},{4,0},{8,4},{12,8},{16,12},{20,16},{24,20},{28,24},{32,28}... | collective-permute-start | bytes 2359304 | tf_op jit(solution)/shard_map/ppermute | solution.py:397
  96.0 5.2 %copy-start.1 = (f32[4,16,2,24,128]{4,3,2,1,0:T(8,128)S(1)}, f32[4,16,2,24,128]{4,3,2,1,0:T(8,128)}, u32[]{:S(2)}) copy-start(f32[4,16,2,24,128]{4,3,2,1,0:T(8,128)} %shard_map.107.split_ref) | copy-start | bytes 4718596
  96.1 5.2 %copy-start.2 = (f32[16,2,2,24,256]{4,3,2,1,0:T(8,128)S(1)}, f32[16,2,2,24,256]{4,3,2,1,0:T(8,128)}, u32[]{:S(2)}) copy-start(f32[16,2,2,24,256]{4,3,2,1,0:T(8,128)} %shard_map.105.whole_ref) | copy-start | bytes 4718596
  96.1 5.2 %copy-start.4 = (s32[256]{0:T(256)S(1)}, s32[256]{0:T(256)}, u32[]{:S(2)}) copy-start(s32[256]{0:T(256)} %row_ref.1) | copy-start | bytes 3076
  96.1 5.2 %copy-start.6 = (s32[256]{0:T(256)S(1)}, s32[256]{0:T(256)}, u32[]{:S(2)}) copy-start(s32[256]{0:T(256)} %column_ref.1) | copy-start | bytes 3076
  96.1 5.2 %copy-start.7 = (s32[256]{0:T(256)S(1)}, s32[256]{0:T(256)}, u32[]{:S(2)}) copy-start(s32[256]{0:T(256)} %field_ref.1) | copy-start | bytes 3076
  96.1 5.2 %copy-start.8 = (s32[256]{0:T(256)S(1)}, s32[256]{0:T(256)}, u32[]{:S(2)}) copy-start(s32[256]{0:T(256)} %level_ref.1) | copy-start | bytes 3076
  96.1 64.3 %all-to-all-start = ((f32[4,16,2,24,128]{4,3,2,1,0:T(8,128)}), f32[4,16,2,24,128]{4,3,2,1,0:T(8,128)}, u32[]{:S(2)}, u32[]{:S(2)}) async-start(f32[4,16,2,24,128]{4,3,2,1,0:T(8,128)} %shard_map.107.split_ref), calls=%async_computation | async-start | bytes 3145728 | tf_op jit(solution)/shard_map/all_to_all | solution.py:416
  101.3 33.2 %copy-start.5 = (f32[256]{0:T(256)S(1)}, f32[256]{0:T(256)}, u32[]{:S(2)}) copy-start(f32[256]{0:T(256)} %err_ref.1) | copy-start | bytes 3076
  101.3 35.5 %copy-start.9 = (f32[256]{0:T(256)S(1)}, f32[256]{0:T(256)}, u32[]{:S(2)}) copy-start(f32[256]{0:T(256)} %obs_ref.1) | copy-start | bytes 3076
  103.4 1.2 collective-permute-start.16
  104.6 3.7 %collective-permute-start.17 = (f32[16,256]{1,0:T(8,128)S(1)}, f32[16,256]{1,0:T(8,128)S(1)}, u32[]{:S(2)}, u32[]{:S(2)}) collective-permute-start(f32[16,256]{1,0:T(8,128)S(1)} %add.26), channel_id=1, source_target_pairs={{0,8},{4,12},{8,0},{12,4},{16,24},{20,28},{24,16},{28,20},{32,40},... | collective-permute-start | bytes 49160 | tf_op jit(solution)/shard_map/ppermute | solution.py:421
  108.4 4.7 %collective-permute-start.18 = (f32[16,256]{1,0:T(8,128)S(1)}, f32[16,256]{1,0:T(8,128)S(1)}, u32[]{:S(2)}, u32[]{:S(2)}) collective-permute-start(f32[16,256]{1,0:T(8,128)S(1)} %add.27), channel_id=1, source_target_pairs={{0,16},{4,20},{8,24},{12,28},{16,0},{20,4},{24,8},{28,12},{32,48},... | collective-permute-start | bytes 49160 | tf_op jit(solution)/shard_map/ppermute | solution.py:421
  113.1 7.6 %collective-permute-start.19 = (f32[16,256]{1,0:T(8,128)S(1)}, f32[16,256]{1,0:T(8,128)S(1)}, u32[]{:S(2)}, u32[]{:S(2)}) collective-permute-start(f32[16,256]{1,0:T(8,128)S(1)} %add.28), channel_id=1, source_target_pairs={{0,32},{4,36},{8,40},{12,44},{16,48},{20,52},{24,56},{28,60},{32,0... | collective-permute-start | bytes 49160 | tf_op jit(solution)/shard_map/ppermute | solution.py:421
  120.8 3.7 %collective-permute-start.20 = (f32[16,256]{1,0:T(8,128)S(1)}, f32[16,256]{1,0:T(8,128)S(1)}, u32[]{:S(2)}, u32[]{:S(2)}) collective-permute-start(f32[16,256]{1,0:T(8,128)S(1)} %add.29), channel_id=1, source_target_pairs={{0,64},{4,68},{8,72},{12,76},{16,80},{20,84},{24,88},{28,92},{32,9... | collective-permute-start | bytes 49160 | tf_op jit(solution)/shard_map/ppermute | solution.py:421
  124.5 5.2 %collective-permute-start.21 = (f32[16,256]{1,0:T(8,128)S(1)}, f32[16,256]{1,0:T(8,128)S(1)}, u32[]{:S(2)}, u32[]{:S(2)}) collective-permute-start(f32[16,256]{1,0:T(8,128)S(1)} %add.30), channel_id=1, source_target_pairs={{0,128},{4,132},{8,136},{12,140},{16,144},{20,148},{24,152},{28,15... | collective-permute-start | bytes 49160 | tf_op jit(solution)/shard_map/ppermute | solution.py:421
  129.8 4.7 %collective-permute-start.24 = (f32[16,256]{1,0:T(8,128)S(1)}, f32[16,256]{1,0:T(8,128)S(1)}, u32[]{:S(2)}, u32[]{:S(2)}) collective-permute-start(f32[16,256]{1,0:T(8,128)S(1)} %add.31.raw_0), channel_id=1, source_target_pairs={{0,3},{1,0},{2,1},{3,2},{4,7},{5,4},{6,5},{7,6},{8,11},{9,8},{10,9... | collective-permute-start | bytes 49160 | tf_op jit(solution)/shard_map/ppermute | solution.py:422
  129.8 5.6 %collective-permute-start.23 = (f32[16,256]{1,0:T(8,128)S(1)}, f32[16,256]{1,0:T(8,128)S(1)}, u32[]{:S(2)}, u32[]{:S(2)}) collective-permute-start(f32[16,256]{1,0:T(8,128)S(1)} %add.31.raw_0), channel_id=1, source_target_pairs={{0,2},{1,3},{2,0},{3,1},{4,6},{5,7},{6,4},{7,5},{8,10},{9,11},{10,... | collective-permute-start | bytes 49160 | tf_op jit(solution)/shard_map/ppermute | solution.py:422
  132.7 4.1 %collective-permute-start.22 = (f32[16,256]{1,0:T(8,128)S(1)}, f32[16,256]{1,0:T(8,128)S(1)}, u32[]{:S(2)}, u32[]{:S(2)}) collective-permute-start(f32[16,256]{1,0:T(8,128)S(1)} %add.31.raw_0), channel_id=1, source_target_pairs={{0,1},{1,2},{2,3},{3,0},{4,5},{5,6},{6,7},{7,4},{8,9},{9,10},{10,1... | collective-permute-start | bytes 49160 | tf_op jit(solution)/shard_map/ppermute | solution.py:422
  164.7 20.0 %all-to-all-start.1 = ((f32[4,16,2,24,128]{4,3,2,1,0:T(8,128)}), f32[4,16,2,24,128]{4,3,2,1,0:T(8,128)S(1)}, u32[]{:S(2)}, u32[]{:S(2)}) async-start(f32[4,16,2,24,128]{4,3,2,1,0:T(8,128)} %shard_map.110), calls=%async_computation.1 | async-start | bytes 3145728 | tf_op jit(solution)/shard_map/all_to_all | solution.py:424
  170.6 2.8 %copy-start.3 = (f32[64,2,2,24,256]{4,3,2,1,0:T(8,128)S(1)}, f32[64,2,2,24,256]{4,3,2,1,0:T(8,128)}, u32[]{:S(2)}) copy-start(f32[64,2,2,24,256]{4,3,2,1,0:T(8,128)} %all-gather.2.cloned.1.call-done.cells_ref) | copy-start | bytes 18874372
  184.7 1.2 copy-start.10
  (5 other events, 4.5 us)
Sparse Core Ops, SparseCore 0:
  96.2 71.4 all-gather.1
